TPU v7x, 128 devices: a whole 4x4x4 slice. The times are simulated.
128 devices in a mesh: op: 8 (over x, core), sec: 16 (over z, y).
Axes of the slice: x: 4, y: 4, z: 4, core: 2. Of those that a mesh axis runs over, the one named last changes fastest.
Arguments:
- start_vector: float32 [16, 256, 256], P('sec'), may hold values from -6 to 6
- diag_guess: float32 [16, 256, 256], P('sec'), may hold values from -4 to 4
- left_env: bfloat16 [8192, 256, 256], P(('op', 'sec')), may hold values from -0.015625 to 0.015625
- right_env: bfloat16 [8192, 256, 256], P(('op', 'sec')), may hold values from -0.375 to 0.375
- sector_from: int32 [8192], P(('op', 'sec')), may hold values from 0 to 15
- sector_to: int32 [8192], P(('op', 'sec')), may hold values from 0 to 15
- term_count: int32 [128], P(('op', 'sec')), may hold values from 1 to 64, as said below
Outputs:
- ritz_vector: float32 [16, 256, 256], P('sec')
- ritz_residual: float32 [16, 256, 256], P('sec')
Inputs may be any that keep to these rules, and one draw needn't show every extreme that they name: `term_count`: every device holds at least one live term, and some device has all 64 slots live.
All inputs are finite; a program needn't handle non-finite values.
Results may differ from a plain program's by a relative error of at most 0.0044.
The roundings to bfloat16 on the way count: a program that leaves them out, or rounds other values in their place, can miss the bound.
Values may be sent and summed in bfloat16 or wider, within the bound.
No kernel may reach another device: no remote copies, remote signals or barrier semaphores. Data moves between devices by JAX's collectives and lax.ppermute only.
A program may use at most 128 MiB of HBM per device.

v0:
```python
import jax
import jax.numpy as jnp
from jax import lax
from jax.sharding import PartitionSpec as P


def apply_ham(vector, left_env, right_env, sector_from, sector_to, live_terms):
    blocks = lax.all_gather(vector.astype(jnp.bfloat16), "sec", axis=0, tiled=True)

    def add_term(term_index, accum):
        left_block = left_env[term_index]
        right_block = right_env[term_index]
        source = sector_from[term_index]
        target = sector_to[term_index]
        first = jnp.dot(left_block, blocks[source], preferred_element_type=jnp.float32).astype(
            jnp.bfloat16
        )
        forward = lax.dot_general(
            first, right_block, (((1,), (1,)), ((), ())), preferred_element_type=jnp.float32
        )
        second = lax.dot_general(
            left_block, blocks[target], (((0,), (0,)), ((), ())), preferred_element_type=jnp.float32
        ).astype(jnp.bfloat16)
        backward = jnp.dot(second, right_block, preferred_element_type=jnp.float32)
        accum = accum.at[target].add(forward)
        accum = accum.at[source].add(backward)
        return accum

    partial_sum = lax.fori_loop(0, live_terms, add_term, jnp.zeros(blocks.shape, jnp.float32))
    owned = lax.psum_scatter(partial_sum, "sec", scatter_dimension=0, tiled=True)
    return lax.psum(owned, "op")


def per_device(start_vector, diag_guess, left_env, right_env, sector_from, sector_to, term_count):
    entries = start_vector.size * lax.axis_size("sec")
    live_terms = term_count[0]
    start_sq = lax.psum(jnp.sum(start_vector * start_vector), "sec") / entries
    vec_one = start_vector / jnp.sqrt(start_sq + 1e-06)
    sigma_one = apply_ham(vec_one, left_env, right_env, sector_from, sector_to, live_terms)
    theta = lax.psum(jnp.sum(vec_one * sigma_one), "sec") / entries
    resid_one = sigma_one - theta * vec_one
    correction = resid_one / jnp.maximum(jnp.abs(diag_guess - theta), 1.0)
    along = lax.psum(jnp.sum(vec_one * correction), "sec") / entries
    ortho = correction - along * vec_one
    ortho_sq = lax.psum(jnp.sum(ortho * ortho), "sec") / entries
    vec_two = ortho / jnp.sqrt(ortho_sq + 1e-06)
    sigma_two = apply_ham(vec_two, left_env, right_env, sector_from, sector_to, live_terms)
    beta_sum, gamma_sum = lax.psum(
        (jnp.sum(vec_one * sigma_two), jnp.sum(vec_two * sigma_two)), "sec"
    )
    beta = beta_sum / entries
    gamma = gamma_sum / entries
    lowest = 0.5 * (theta + gamma) - jnp.sqrt((0.5 * (theta - gamma)) ** 2 + beta * beta)
    norm_scale = jnp.sqrt(beta * beta + (lowest - theta) ** 2)
    coef_one = beta / norm_scale
    coef_two = (lowest - theta) / norm_scale
    ritz_vector = coef_one * vec_one + coef_two * vec_two
    ritz_residual = coef_one * sigma_one + coef_two * sigma_two - lowest * ritz_vector
    return (ritz_vector, ritz_residual)


def solution(mesh):
    return jax.shard_map(
        per_device,
        mesh=mesh,
        in_specs=(
            P("sec", None, None),
            P("sec", None, None),
            P(("op", "sec"), None, None),
            P(("op", "sec"), None, None),
            P(("op", "sec")),
            P(("op", "sec")),
            P(("op", "sec")),
        ),
        out_specs=(P("sec", None, None), P("sec", None, None)),
        check_vma=False,
    )
```

profile of v0, /device:TPU:1, one launch (start us, length us, event | category | flops | bytes accessed | tf_op | source)
XLA Modules:
  0.0 2139.2 jit_solution(13002008714286456953)
XLA Ops:
  8.9 36.1 %psum.56 = f32[]{:T(128)} all-reduce(f32[]{:T(128)} %multiply_reduce_fusion.5), channel_id=1, replica_groups=mesh['op'=8,'sec'=16] {'sec'}, use_global_device_ids=true, to_apply=%region_1.0 | all-reduce | flops 1 | bytes 8 | tf_op jit(solution)/shard_map/psum | solution.py:37
  47.4 47.9 %all-gather.3.cloned.1.call-done = bf16[16,256,256]{2,1,0:T(8,128)(2,1)} async-done(((bf16[1,256,256]{2,1,0:T(8,128)(2,1)}), bf16[16,256,256]{2,1,0:T(8,128)(2,1)}) %all-gather.3.cloned.1.call-update) | async-done | bytes 2097168 | tf_op jit(solution)/shard_map/all_gather | solution.py:8
  97.6 780.2 %while.24 = (s32[]{:T(128)}, f32[16,256,256]{2,1,0:T(8,128)}, s32[]{:T(128)}, s32[64]{0:T(128)S(1)}, bf16[64,256,256]{2,1,0:T(8,128)(2,1)}, /*index=5*/s32[64]{0...) while((s32[]{:T(128)}, f32[16,256,256]{2,1,0:T(8,128)}, ...), condition=%wide.region_5.0_spmd, body=%wide.region_2.0_spmd.sunk | while | flops 134610992 | bytes 1840421 | solution.py:29
  107.0 2.9 fusion.85
  119.2 2.9 fusion.85
  204.4 2.9 fusion.85
  216.6 2.9 fusion.85
  399.3 2.9 fusion.85
  435.9 2.9 fusion.85
  460.2 2.9 fusion.85
  472.4 2.9 fusion.85
  545.5 2.9 fusion.85
  582.0 2.9 fusion.85
  618.6 2.9 fusion.85
  630.8 2.9 fusion.85
  655.1 2.9 fusion.85
  667.3 2.9 fusion.85
  679.5 2.9 fusion.85
  752.6 2.9 fusion.85
  801.3 2.9 fusion.85
  813.5 2.9 fusion.85
  837.8 2.9 fusion.85
  877.9 76.5 %reduce-scatter.7.cloned.1.call-done = f32[1,256,256]{2,1,0:T(8,128)} async-done(((f32[16,256,256]{2,1,0:T(8,128)}), f32[1,256,256]{2,1,0:T(8,128)}) %reduce-scatter.7.cloned.1.call-update) | async-done | bytes 262160
  954.5 60.9 %all-reduce.6.cloned.1.call-done = f32[1,256,256]{2,1,0:T(8,128)} async-done(((f32[1,256,256]{2,1,0:T(8,128)}), f32[1,256,256]{2,1,0:T(8,128)}) %all-reduce.6.cloned.1.call-update) | async-done | bytes 262160 | tf_op jit(solution)/shard_map/psum | solution.py:31
  1017.0 34.2 %psum.58 = f32[]{:T(128)} all-reduce(f32[]{:T(128)} %multiply_reduce_fusion.4), channel_id=1, replica_groups=mesh['op'=8,'sec'=16] {'sec'}, use_global_device_ids=true, to_apply=%region_9.0 | all-reduce | flops 1 | bytes 8 | tf_op jit(solution)/shard_map/psum | solution.py:40
  1053.5 29.2 %psum.59 = f32[]{:T(128)} all-reduce(f32[]{:T(128)} %get-tuple-element.180), channel_id=1, replica_groups=mesh['op'=8,'sec'=16] {'sec'}, use_global_device_ids=true, to_apply=%region_11.0 | all-reduce | flops 1 | bytes 8 | tf_op jit(solution)/shard_map/psum | solution.py:43
  1084.0 30.8 %psum.60 = f32[]{:T(128)} all-reduce(f32[]{:T(128)} %multiply_reduce_fusion.2), channel_id=1, replica_groups=mesh['op'=8,'sec'=16] {'sec'}, use_global_device_ids=true, to_apply=%region_13.0 | all-reduce | flops 1 | bytes 8 | tf_op jit(solution)/shard_map/psum | solution.py:45
  1116.3 61.3 %all-gather.5.cloned.1.call-done = bf16[16,256,256]{2,1,0:T(8,128)(2,1)} async-done(((bf16[1,256,256]{2,1,0:T(8,128)(2,1)}), bf16[16,256,256]{2,1,0:T(8,128)(2,1)}) %all-gather.5.cloned.1.call-update) | async-done | bytes 2097168 | tf_op jit(solution)/shard_map/all_gather | solution.py:8
  1180.0 774.3 %while.25 = (s32[]{:T(128)}, f32[16,256,256]{2,1,0:T(8,128)}, s32[]{:T(128)}, s32[64]{0:T(128)S(1)}, bf16[64,256,256]{2,1,0:T(8,128)(2,1)}, /*index=5*/s32[64]{0...) while((s32[]{:T(128)}, f32[16,256,256]{2,1,0:T(8,128)}, ...), condition=%wide.region_17.0_spmd, body=%wide.region_14.0_spmd.sunk | while | flops 134610992 | bytes 1840421 | solution.py:29
  1954.4 76.7 %reduce-scatter.9.cloned.1.call-done = f32[1,256,256]{2,1,0:T(8,128)} async-done(((f32[16,256,256]{2,1,0:T(8,128)}), f32[1,256,256]{2,1,0:T(8,128)}) %reduce-scatter.9.cloned.1.call-update) | async-done | bytes 262160
  2031.2 60.8 %all-reduce.8.cloned.1.call-done = f32[1,256,256]{2,1,0:T(8,128)} async-done(((f32[1,256,256]{2,1,0:T(8,128)}), f32[1,256,256]{2,1,0:T(8,128)}) %all-reduce.8.cloned.1.call-update) | async-done | bytes 262160 | tf_op jit(solution)/shard_map/psum | solution.py:31
  2093.6 34.2 %all-reduce.2 = (f32[]{:T(128)}, f32[]{:T(128)}) all-reduce(f32[]{:T(128)} %get-tuple-element.143, f32[]{:T(128)} %get-tuple-element.142), channel_id=1, replica_groups=mesh['op'=8,'sec'=16] {'sec'}, use_global_device_ids=true, to_apply=%region_23.0 | all-reduce | flops 2 | bytes 16 | tf_op jit(solution)/shard_map/psum | solution.py:48
  (655 shorter events, 939.4 us)
Async XLA Ops:
  7.2 90.5 %copy-start.3 = (s32[3]{0:T(128)S(1)}, s32[3]{0:T(128)}, u32[]{:S(2)}) copy-start(s32[3]{0:T(128)} %constant.108.clone.1) | copy-start | bytes 40
  7.2 90.5 %copy-start.4 = (s32[64]{0:T(128)S(1)}, s32[64]{0:T(128)}, u32[]{:S(2)}) copy-start(s32[64]{0:T(128)} %param.24) | copy-start | bytes 772
  7.2 90.5 %copy-start.5 = (s32[64]{0:T(128)S(1)}, s32[64]{0:T(128)}, u32[]{:S(2)}) copy-start(s32[64]{0:T(128)} %param.23) | copy-start | bytes 772
  7.2 88.1 %all-gather.3.cloned.1.call-start = ((), (), s32[]{:S(2)}) async-start(), calls=%async_computation.2 | async-start | bytes 2228224 | tf_op jit(solution)/shard_map/all_gather | solution.py:8
  47.4 907.1 %reduce-scatter.7.cloned.1.call-start = ((), (), s32[]{:S(2)}) async-start(), calls=%async_computation.6 | async-start | bytes 4456448
  877.8 137.6 %copy-start = (f32[1,256,256]{2,1,0:T(8,128)S(1)}, f32[1,256,256]{2,1,0:T(8,128)}, u32[]{:S(2)}) copy-start(f32[1,256,256]{2,1,0:T(8,128)} %param.19) | copy-start | bytes 786436
  877.8 174.0 %copy-start.2 = (f32[1,256,256]{2,1,0:T(8,128)S(1)}, f32[1,256,256]{2,1,0:T(8,128)}, u32[]{:S(2)}) copy-start(f32[1,256,256]{2,1,0:T(8,128)} %param.20) | copy-start | bytes 786436
  877.9 137.5 %all-reduce.6.cloned.1.call-start = ((), (), s32[]{:S(2)}) async-start(), calls=%async_computation.3 | async-start | bytes 524288 | tf_op jit(solution)/shard_map/psum | solution.py:31
  954.5 223.2 %all-gather.5.cloned.1.call-start = ((), (), s32[]{:S(2)}) async-start(), calls=%async_computation.4 | async-start | bytes 2228224 | tf_op jit(solution)/shard_map/all_gather | solution.py:8
  1116.2 914.9 %reduce-scatter.9.cloned.1.call-start = ((), (), s32[]{:S(2)}) async-start(), calls=%async_computation.7 | async-start | bytes 4456448
  1954.3 176.2 %copy-start.1 = (f32[1,256,256]{2,1,0:T(8,128)S(1)}, f32[1,256,256]{2,1,0:T(8,128)}, u32[]{:S(2)}) copy-start(f32[1,256,256]{2,1,0:T(8,128)} %all-reduce.6.cloned.1.call-done) | copy-start | bytes 786436
  1954.4 137.6 %all-reduce.8.cloned.1.call-start = ((), (), s32[]{:S(2)}) async-start(), calls=%async_computation.5 | async-start | bytes 524288 | tf_op jit(solution)/shard_map/psum | solution.py:31
Sparse Core Ops, SparseCore 0:
  47.5 47.7 all-gather.2
  878.0 76.3 reduce-scatter.6
  956.9 58.4 all-reduce.5
  1116.3 61.2 all-gather.4
  1954.5 76.5 reduce-scatter.8
  2033.4 58.4 all-reduce.7
where the time goes:
time: 2160 us; the launch traced here: 2140 us
  matrix products  722 us (33%)
  loops' own time  577 us (27%)
  waiting for transfers between devices  384 us (18%)
  blocking collectives  164 us (8%)
  local copies, waits for them, and re-layouts  161 us (7%)
  other arithmetic  111 us (5%)
    another operation x2, loops' own time, apply_ham(): lax.fori_loop(0, live_terms, add_term, jnp.zeros(blocks.shape, jnp.float32))  577 us
    dot_general x128, matrix products, add_term(): backward = jnp.dot(second, right_block, preferred_element_type=jnp.float32)  364 us
    dot_general x128, matrix products, add_term(): lax.dot_general(first, right_block, (((1,), (1,)), ((), ())), preferred_e...  358 us
    unnamed x8, waiting for transfers between devices  153 us
    psum x2, waiting for transfers between devices, apply_ham(): return lax.psum(owned, 'op')  122 us
    all_gather x2, waiting for transfers between devices, apply_ham(): lax.all_gather(vector.astype(jnp.bfloat16), 'sec', axis=0, tiled=True)  109 us
    another operation x128, other arithmetic  99.2 us
    dynamic_slice x128, local copies, waits for them, and re-layouts, add_term(): source = sector_from[term_index]  81 us
  transfers between devices with their start and end apart: 6, of which 6 were waited for; matrix products, arithmetic and copies ran while one was open for 0% of the time, Pallas kernels for 0%

commit v1 on v0

v1 whole, which is shorter than its diff:
```python
import jax
import jax.numpy as jnp
from jax import lax
from jax.experimental import pallas as pl
from jax.experimental.pallas import tpu as pltpu
from jax.sharding import PartitionSpec as P

F32, BF16 = jnp.float32, jnp.bfloat16
SEC, B, ROWS, LANES = 16, 256, 32, 128
CHIPS_X, N_OP = 4, 8
PIECES = CHIPS_X * SEC
TERMS, STEP = 64, 8
ENTRIES = SEC * B * B
CORE_SWAP = [(i, i ^ 1) for i in range(N_OP)]
GROUPS = [[(2 * x + core) * SEC + s for x in range(CHIPS_X) for s in range(SEC)] for core in range(2)]
VMEM = pltpu.CompilerParams(vmem_limit_bytes=56 << 20)


def dot(a, b, contract):
    return lax.dot_general(a, b, ((contract[:1], contract[1:]), ((), ())), preferred_element_type=F32)


def fold(block):
    return jnp.sum(block.reshape(-1, 8, LANES), axis=0)


def block_rows(x, core):
    return pl.ds(pl.multiple_of((2 * x + core) * ROWS, ROWS), ROWS)


def apply_terms(i, count_ref, from_ref, to_ref, x_ref, left_ref, right_ref, acc_ref):
    live = count_ref[0] - i * STEP

    def halves(j):
        source, target = from_ref[i * STEP + j], to_ref[i * STEP + j]
        first = dot(left_ref[j], x_ref[source], (1, 0)).astype(BF16)
        second = dot(left_ref[j], x_ref[target], (0, 0)).astype(BF16)
        return j, source, target, first, second

    def add(j, source, target, first, second):
        acc_ref[target] += dot(first, right_ref[j], (1, 1))
        acc_ref[source] += dot(second, right_ref[j], (1, 0))

    @pl.when(live >= STEP)
    def _():
        held = halves(0)
        for j in range(1, STEP):
            ahead = halves(j)
            add(*held)
            held = ahead
        add(*held)

    @pl.when((live > 0) & (live < STEP))
    def _():
        @pl.loop(0, live)
        def _(j):
            add(*halves(j))


def split_out(core, acc_ref, keep_ref, send_ref):
    @pl.loop(0, SEC)
    def _(s):
        for x in range(CHIPS_X):
            mine = acc_ref[s, block_rows(x, core), :]
            theirs = acc_ref[s, block_rows(x, 1 - core), :].astype(BF16)
            keep_ref[x * SEC + s, :ROWS, :] = mine[:, :LANES]
            keep_ref[x * SEC + s, ROWS:, :] = mine[:, LANES:]
            send_ref[x * SEC + s, :ROWS, :] = theirs[:, :LANES]
            send_ref[x * SEC + s, ROWS:, :] = theirs[:, LANES:]


def first_kernel(count_ref, from_ref, to_ref, at_ref, own_ref, other_ref, left_ref, right_ref,
                 v_ref, piece_ref, keep_ref, send_ref, sums_ref, x_ref, acc_ref):
    i = pl.program_id(0)
    core, sector = at_ref[0], at_ref[1]

    @pl.when(i == 0)
    def _():
        def squares(s, total):
            return total + fold(own_ref[s] * own_ref[s]) + fold(other_ref[s] * other_ref[s])

        total = lax.fori_loop(0, SEC, squares, jnp.zeros((8, LANES), F32))
        scale = 1.0 / jnp.sqrt(jnp.sum(total, keepdims=True) / ENTRIES + 1e-06)

        @pl.loop(0, SEC)
        def _(s):
            for x in range(CHIPS_X):
                for ref, at in ((own_ref, core), (other_ref, 1 - core)):
                    block = ref[s, x * ROWS:(x + 1) * ROWS, :] * scale
                    v_ref[s, block_rows(x, at), :] = block
                    x_ref[s, block_rows(x, at), :] = block.astype(BF16)
            acc_ref[s] = jnp.zeros((B, B), F32)

    apply_terms(i, count_ref, from_ref, to_ref, x_ref, left_ref, right_ref, acc_ref)

    @pl.when(i == pl.num_programs(0) - 1)
    def _():
        split_out(core, acc_ref, keep_ref, send_ref)

        def inner(s, total):
            return total + fold(v_ref[s] * acc_ref[s])

        theta = lax.fori_loop(0, SEC, inner, jnp.zeros((8, LANES), F32))
        sums_ref[0] = theta
        sums_ref[1] = jnp.zeros_like(theta)
        block = v_ref[sector, block_rows(at_ref[2], core), :]
        piece_ref[:ROWS, :] = block[:, :LANES]
        piece_ref[ROWS:, :] = block[:, LANES:]


def second_kernel(count_ref, from_ref, to_ref, at_ref, own_ref, other_ref, v_ref, left_ref, right_ref,
                  v2s_ref, keep_ref, send_ref, sums_ref, v2_ref, x_ref, acc_ref):
    i = pl.program_id(0)
    core, sector = at_ref[0], at_ref[1]
    zero = jnp.zeros((8, LANES), F32)

    def blocks(s):
        for x in range(CHIPS_X):
            for ref, at in ((own_ref, core), (other_ref, 1 - core)):
                for h in range(2):
                    corr = ref[x * SEC + s, h * ROWS:(h + 1) * ROWS, :]
                    yield corr, (s, block_rows(x, at), slice(h * LANES, (h + 1) * LANES))

    @pl.when(i == 0)
    def _():
        def project(s, total):
            for corr, at in blocks(s):
                total = total + fold(v_ref[at] * corr)
            return total

        along = jnp.sum(lax.fori_loop(0, SEC, project, zero), keepdims=True) / ENTRIES

        def remove(s, total):
            for corr, at in blocks(s):
                ortho = corr - along * v_ref[at]
                v2_ref[at] = ortho
                total = total + fold(ortho * ortho)
            acc_ref[s] = jnp.zeros((B, B), F32)
            return total

        ortho_sq = jnp.sum(lax.fori_loop(0, SEC, remove, zero), keepdims=True) / ENTRIES
        scale = 1.0 / jnp.sqrt(ortho_sq + 1e-06)

        @pl.loop(0, SEC)
        def _(s):
            block = v2_ref[s] * scale
            v2_ref[s] = block
            x_ref[s] = block.astype(BF16)

        v2s_ref[...] = v2_ref[sector]

    apply_terms(i, count_ref, from_ref, to_ref, x_ref, left_ref, right_ref, acc_ref)

    @pl.when(i == pl.num_programs(0) - 1)
    def _():
        split_out(core, acc_ref, keep_ref, send_ref)

        def inner(s, totals):
            return totals[0] + fold(v_ref[s] * acc_ref[s]), totals[1] + fold(v2_ref[s] * acc_ref[s])

        sums_ref[0], sums_ref[1] = lax.fori_loop(0, SEC, inner, (zero, zero))


def join_kernel(keep_ref, got_ref, sums_ref, got_sums_ref, out_ref):
    row = lax.broadcasted_iota(jnp.int32, (16, LANES), 0)
    tile = jnp.zeros((16, LANES), F32)
    for k in range(2):
        rest = jnp.sum(sums_ref[k] + got_sums_ref[k], keepdims=True)
        for part in range(3):
            top = rest.astype(BF16).astype(F32)
            tile = jnp.where(row == 3 * k + part, top, tile)
            rest = rest - top
    tile = tile.astype(BF16)

    @pl.loop(0, PIECES)
    def _(p):
        out_ref[p, :2 * ROWS, :] = (keep_ref[p] + got_ref[p].astype(F32)).astype(BF16)
        out_ref[p, 2 * ROWS:, :] = tile


def gathered_sum(got_ref):
    def add(p, total):
        return total + got_ref[p].astype(F32)

    total = lax.fori_loop(0, PIECES, add, jnp.zeros((2 * ROWS + 16, LANES), F32))
    row = lax.broadcasted_iota(jnp.int32, (16, LANES), 0)
    tile = total[2 * ROWS:, :]
    scalars = [
        jnp.sum(jnp.where((row >= 3 * k) & (row < 3 * k + 3), tile, 0.0), keepdims=True) / (LANES * ENTRIES)
        for k in range(2)
    ]
    return total[:2 * ROWS, :], scalars


def correct_kernel(got_ref, v_ref, diag_ref, corr_ref, w_ref, theta_ref):
    sigma, (theta, _) = gathered_sum(got_ref)
    w_ref[...] = sigma
    theta_ref[...] = jnp.broadcast_to(theta, theta_ref.shape)
    corr = (sigma - theta * v_ref[...]) / jnp.maximum(jnp.abs(diag_ref[...] - theta), 1.0)

    @pl.loop(0, PIECES)
    def _(p):
        corr_ref[p] = corr


def ritz_kernel(at_ref, got_ref, v_ref, v2s_ref, w_ref, theta_ref, out_ref, coef_ref):
    sigma, (beta, gamma) = gathered_sum(got_ref)
    theta = theta_ref[:1, :1]
    lowest = 0.5 * (theta + gamma) - jnp.sqrt((0.5 * (theta - gamma)) ** 2 + beta * beta)
    norm = jnp.sqrt(beta * beta + (lowest - theta) ** 2)
    one, two = beta / norm, (lowest - theta) / norm
    coef_ref[0] = jnp.broadcast_to(one, (8, LANES))
    coef_ref[1] = jnp.broadcast_to(two, (8, LANES))
    v2 = v2s_ref[block_rows(at_ref[2], at_ref[0]), :]
    for h in range(2):
        rows, lanes = slice(h * ROWS, (h + 1) * ROWS), slice(h * LANES, (h + 1) * LANES)
        ritz = one * v_ref[rows, :] + two * v2[:, lanes]
        resid = one * w_ref[rows, :] + two * sigma[rows, :] - lowest * ritz
        for p in range(N_OP):
            out_ref[p, :, lanes] = resid


def shape(*dims, dtype=F32):
    return jax.ShapeDtypeStruct(dims, dtype)


SMEM = pl.BlockSpec(memory_space=pltpu.SMEM)
WHOLE = pl.BlockSpec(memory_space=pltpu.VMEM)
TERM_BLOCK = pl.BlockSpec((STEP, B, B), lambda i: (i, 0, 0))


def swap(x):
    return lax.ppermute(x, "op", CORE_SWAP)


def exchange(x):
    return lax.all_to_all(x, ("op", "sec"), 0, 0, tiled=True, axis_index_groups=GROUPS)


def two_lanes(rows):
    return jnp.concatenate([rows[:, :LANES], rows[:, LANES:]], axis=0)


def reduce_partial(keep, send, sums):
    payload = pl.pallas_call(
        join_kernel,
        out_shape=shape(PIECES, 2 * ROWS + 16, LANES, dtype=BF16),
        in_specs=[WHOLE] * 4,
        out_specs=WHOLE,
        compiler_params=VMEM,
        name="join",
    )(keep, swap(send), sums, swap(sums))
    return exchange(payload)


def per_device(start_vector, diag_guess, left_env, right_env, sector_from, sector_to, term_count):
    op, sector = lax.axis_index("op"), lax.axis_index("sec")
    core, chip = op % 2, op // 2
    at = jnp.stack([core, sector, chip]).astype(jnp.int32)
    terms = (term_count, sector_from, sector_to, at)

    mine = lax.dynamic_index_in_dim(start_vector.reshape(CHIPS_X, 2, ROWS, B), core, 1, keepdims=False)
    mine = jnp.broadcast_to(mine.reshape(1, B // 2, B), (SEC, B // 2, B))
    own = lax.all_to_all(mine, "sec", 0, 0, tiled=True)
    other = swap(own)
    diag = two_lanes(lax.dynamic_slice_in_dim(diag_guess[0], op * ROWS, ROWS, 0))

    split_shapes = [shape(PIECES, 2 * ROWS, LANES), shape(PIECES, 2 * ROWS, LANES, dtype=BF16), shape(2, 8, LANES)]
    vec, piece, keep, send, sums = pl.pallas_call(
        first_kernel,
        grid=(TERMS // STEP,),
        out_shape=[shape(SEC, B, B), shape(2 * ROWS, LANES)] + split_shapes,
        in_specs=[SMEM] * 4 + [WHOLE] * 2 + [TERM_BLOCK] * 2,
        out_specs=[WHOLE] * 5,
        scratch_shapes=[pltpu.VMEM((SEC, B, B), BF16), pltpu.VMEM((SEC, B, B), F32)],
        compiler_params=VMEM,
        name="first_apply",
    )(*terms, own, other, left_env, right_env)

    got = reduce_partial(keep, send, sums)
    corr, sigma_one, theta = pl.pallas_call(
        correct_kernel,
        out_shape=[shape(PIECES, 2 * ROWS, LANES), shape(2 * ROWS, LANES), shape(8, LANES)],
        in_specs=[WHOLE] * 3,
        out_specs=[WHOLE] * 3,
        compiler_params=VMEM,
        name="correct",
    )(got, piece, diag)

    own = exchange(corr)
    other = swap(own)
    vec_two, keep, send, sums = pl.pallas_call(
        second_kernel,
        grid=(TERMS // STEP,),
        out_shape=[shape(B, B)] + split_shapes,
        in_specs=[SMEM] * 4 + [WHOLE] * 3 + [TERM_BLOCK] * 2,
        out_specs=[WHOLE] * 4,
        scratch_shapes=[
            pltpu.VMEM((SEC, B, B), F32),
            pltpu.VMEM((SEC, B, B), BF16),
            pltpu.VMEM((SEC, B, B), F32),
        ],
        compiler_params=VMEM,
        name="second_apply",
    )(*terms, own, other, vec, left_env, right_env)

    got = reduce_partial(keep, send, sums)
    resid, coefs = pl.pallas_call(
        ritz_kernel,
        out_shape=[shape(N_OP, ROWS, B), shape(2, 8, LANES)],
        in_specs=[SMEM] + [WHOLE] * 5,
        out_specs=[WHOLE] * 2,
        compiler_params=VMEM,
        name="ritz",
    )(at, got, piece, vec_two, sigma_one, theta)

    ritz_residual = lax.all_to_all(resid, "op", 0, 0, tiled=True).reshape(1, B, B)
    vec_one = lax.dynamic_index_in_dim(vec, sector, 0, keepdims=True)
    ritz_vector = coefs[0, 0, 0] * vec_one + coefs[1, 0, 0] * vec_two[None]
    return (ritz_vector, ritz_residual)


def solution(mesh):
    return jax.shard_map(
        per_device,
        mesh=mesh,
        in_specs=(
            P("sec", None, None),
            P("sec", None, None),
            P(("op", "sec"), None, None),
            P(("op", "sec"), None, None),
            P(("op", "sec")),
            P(("op", "sec")),
            P(("op", "sec")),
        ),
        out_specs=(P("sec", None, None), P("sec", None, None)),
        check_vma=False,
    )
```

time: 2160 us -> 218 us (0.10)
  matrix products: 722 us -> 0 us
  loops' own time: 577 us -> 0 us
  waiting for transfers between devices: 384 us -> 53.2 us
  local copies, waits for them, and re-layouts: 161 us -> 9.54 us
  other arithmetic: 111 us -> 4.27 us
  blocking collectives: 164 us -> 67.7 us
  Pallas kernels: 0 us -> 51.6 us
  starting transfers between devices: 0.24 us -> 30 us
    dot_general x256 -> x0, matrix products: 722 us -> none  [the longest x128 364 us: add_term(): backward = jnp.dot(second, right_block, preferred_element_type=jnp.float32)]
    another operation x2 -> x0, loops' own time: 577 us -> none  [apply_ham(): lax.fori_loop(0, live_terms, add_term, jnp.zeros(blocks.shape, jnp.float32))]
    psum x5 -> x0, blocking collectives: 164 us -> none  [the longest x1 36.1 us: per_device(): start_sq = lax.psum(jnp.sum(start_vector * start_vector), 'sec') / entries]
    dynamic_slice x256 -> x2, local copies, waits for them, and re-layouts: 156 us -> 0.78 us  [the longest x1 0.77 us: per_device(): lax.dynamic_slice_in_dim(diag_guess[0], op * ROWS, ROWS, 0)]
    unnamed x8 -> x0, waiting for transfers between devices: 153 us -> none
    psum x2 -> x0, waiting for transfers between devices: 122 us -> none  [apply_ham(): return lax.psum(owned, 'op')]
    all_gather x2 -> x0, waiting for transfers between devices: 109 us -> none  [apply_ham(): lax.all_gather(vector.astype(jnp.bfloat16), 'sec', axis=0, tiled=True)]
    another operation x128 -> x1, other arithmetic: 99.2 us -> 0.65 us  [per_device(): at = jnp.stack([core, sector, chip]).astype(jnp.int32)]
  transfers between devices with their start and end apart: 6 -> 9, of which waited for: 6 -> 7; matrix products, arithmetic and copies ran while one was open for 0% -> 2% of each run, Pallas kernels for 0% -> 0%
where the time goes in v1:
time: 218 us
  blocking collectives  67.7 us (31%)
  waiting for transfers between devices  53.2 us (24%)
  Pallas kernels  51.6 us (24%)
  starting transfers between devices  30 us (14%)
  local copies, waits for them, and re-layouts  9.54 us (4%)
  other arithmetic  4.27 us (2%)
    all_to_all x2, waiting for transfers between devices, exchange(): lax.all_to_all(x, ('op', 'sec'), 0, 0, tiled=True, axis_index_groups=GROUPS)  38.5 us
    all_to_all x1, blocking collectives, per_device(): own = lax.all_to_all(mine, 'sec', 0, 0, tiled=True)  35.8 us
    all_to_all x1, blocking collectives, exchange(): lax.all_to_all(x, ('op', 'sec'), 0, 0, tiled=True, axis_index_groups=GROUPS)  31.9 us
    pallas_call x1, Pallas kernels, per_device(): pl.pallas_call(second_kernel, grid=(TERMS // STEP,), out_shape=[shape(B,...  19.2 us
    pallas_call x1, Pallas kernels, per_device(): pl.pallas_call(first_kernel, grid=(TERMS // STEP,), out_shape=[shape(SEC,...  18.6 us
    ppermute x6, starting transfers between devices, swap(): return lax.ppermute(x, 'op', CORE_SWAP)  12.5 us
    all_to_all x2, starting transfers between devices, exchange(): lax.all_to_all(x, ('op', 'sec'), 0, 0, tiled=True, axis_index_groups=GROUPS)  11.6 us
    ppermute x6, waiting for transfers between devices, swap(): return lax.ppermute(x, 'op', CORE_SWAP)  11.2 us
  transfers between devices with their start and end apart: 9, of which 7 were waited for; matrix products, arithmetic and copies ran while one was open for 2% of the time, Pallas kernels for 0%

profile of v1, /device:TPU:1, one launch (start us, length us, event | category | flops | bytes accessed | tf_op | source)
XLA Modules:
  0.0 217.6 jit_solution(8552077215308397376)
XLA Ops:
  0.7 0.9 copy-done
  1.8 35.8 %all_to_all.25.own_ref = f32[16,128,256]{2,1,0:T(8,128)S(1)} all-to-all(f32[16,128,256]{2,1,0:T(8,128)S(1)} %broadcast_in_dim.9), channel_id=1, replica_groups=mesh['op'=8,'sec'=16] {'sec'}, dimensions={0} | all-to-all | bytes 4194304 | tf_op jit(solution)/shard_map/all_to_all | solution.py:264
  37.6 2.0 collective-permute-start
  40.2 0.7 pad_add_fusion.at_ref
  40.9 2.6 %collective-permute-done.other_ref = f32[16,128,256]{2,1,0:T(8,128)} collective-permute-done((f32[16,128,256]{2,1,0:T(8,128)S(1)}, f32[16,128,256]{2,1,0:T(8,128)}, u32[]{:S(2)}, u32[]{:S(2)}) %collective-permute-start) | collective-permute-done | bytes 2097184 | tf_op jit(solution)/shard_map/ppermute | solution.py:233
  43.5 18.6 %first_apply.1 = (f32[16,256,256]{2,1,0:T(8,128)}, f32[64,128]{1,0:T(8,128)}, f32[64,64,128]{2,1,0:T(8,128)}, bf16[64,64,128]{2,1,0:T(8,128)(2,1)}, f32[2,8,128]{2,1,0:T(8,128)}) custom-call(s32[1]{0:T(128)S(6)} %copy.10.count_ref, s32[64]{0:T(128)} %from_ref.3, s32[64]{0:T(128)} %to_ref.3, s32[3]{0:T(128)} %pad_add_fusion.at_ref, ...), custom_call_target="tpu_custom_call" | custom-call | tf_op jit(solution)/shard_map/first_apply/pallas_call | solution.py:269
  62.1 3.0 %collective-permute-start.1 = (bf16[64,64,128]{2,1,0:T(8,128)(2,1)}, bf16[64,64,128]{2,1,0:T(8,128)(2,1)S(1)}, u32[]{:S(2)}, u32[]{:S(2)}) collective-permute-start(bf16[64,64,128]{2,1,0:T(8,128)(2,1)} %get-tuple-element.17), channel_id=1, source_target_pairs={{0,16},{16,0},{32,48},{48,32},{64,80},{80,64},{96,112},{112,96},{1... | collective-permute-start | bytes 3145736 | tf_op jit(solution)/shard_map/ppermute | solution.py:233
  65.1 2.4 %collective-permute-done.2.got_sums_ref = f32[2,8,128]{2,1,0:T(8,128)S(1)} collective-permute-done((f32[2,8,128]{2,1,0:T(8,128)}, f32[2,8,128]{2,1,0:T(8,128)S(1)}, u32[]{:S(2)}, u32[]{:S(2)}) %collective-permute-start.2) | collective-permute-done | bytes 8224 | tf_op jit(solution)/shard_map/ppermute | solution.py:233
  68.6 3.6 %join.2 = bf16[64,80,128]{2,1,0:T(8,128)(2,1)} custom-call(f32[64,64,128]{2,1,0:T(8,128)} %get-tuple-element.16.keep_ref, bf16[64,64,128]{2,1,0:T(8,128)(2,1)} %copy-done.6, f32[2,8,128]{2,1,0:T(8,128)} %get-tuple-element.18.sums_ref, f32[2,8,128]{2,1,0:T(8,128)} %copy-done.9), custom_call_target="tpu_custom_call" | custom-call | tf_op jit(solution)/shard_map/join/pallas_call | solution.py:245
  72.3 6.0 %all-to-all-start.1 = ((bf16[64,80,128]{2,1,0:T(8,128)(2,1)}), bf16[64,80,128]{2,1,0:T(8,128)(2,1)S(1)}, u32[]{:S(2)}, u32[]{:S(2)}) async-start(bf16[64,80,128]{2,1,0:T(8,128)(2,1)} %join.2), calls=%async_computation.1 | async-start | bytes 2621440 | tf_op jit(solution)/shard_map/all_to_all | solution.py:237
  78.2 0.8 dynamic-slice_bitcast_fusion
  79.0 0.6 pad_maximum_fusion.diag_ref
  79.6 18.5 %all-to-all-done.1.got_ref = bf16[64,80,128]{2,1,0:T(8,128)(2,1)S(1)} async-done(((bf16[64,80,128]{2,1,0:T(8,128)(2,1)}), bf16[64,80,128]{2,1,0:T(8,128)(2,1)S(1)}, u32[]{:S(2)}, u32[]{:S(2)}) %all-to-all-start.1) | async-done | bytes 1310752 | tf_op jit(solution)/shard_map/all_to_all | solution.py:237
  98.2 1.1 copy-done.3
  99.2 3.7 %correct.1 = (f32[64,64,128]{2,1,0:T(8,128)}, f32[64,128]{1,0:T(8,128)}, f32[8,128]{1,0:T(8,128)}) custom-call(bf16[64,80,128]{2,1,0:T(8,128)(2,1)} %copy-done.3, f32[64,128]{1,0:T(8,128)} %get-tuple-element.19.v_ref, f32[64,128]{1,0:T(8,128)} %pad_maximum_fusion.diag_ref), custom_call_target="tpu_custom_call" | custom-call | tf_op jit(solution)/shard_map/correct/pallas_call | solution.py:281
  102.9 31.9 %all_to_all.26.own_ref = f32[64,64,128]{2,1,0:T(8,128)S(1)} all-to-all(f32[64,64,128]{2,1,0:T(8,128)} %get-tuple-element.20), channel_id=1, replica_groups={{0,1,2,3,4,5,6,7,8,9,10,11,12,13,14,15,32,33,34,35,36,37,38,39,40,41,42..., dimensions={0} | all-to-all | bytes 4194304 | tf_op jit(solution)/shard_map/all_to_all | solution.py:237
  134.9 4.5 %collective-permute-start.3 = (f32[64,64,128]{2,1,0:T(8,128)S(1)}, f32[64,64,128]{2,1,0:T(8,128)S(1)}, u32[]{:S(2)}, u32[]{:S(2)}) collective-permute-start(f32[64,64,128]{2,1,0:T(8,128)S(1)} %all_to_all.26.own_ref), channel_id=1, source_target_pairs={{0,16},{16,0},{32,48},{48,32},{64,80},{80,64},{96,112},{112,96},{1... | collective-permute-start | bytes 6291464 | tf_op jit(solution)/shard_map/ppermute | solution.py:233
  139.3 3.8 %collective-permute-done.3.other_ref = f32[64,64,128]{2,1,0:T(8,128)S(1)} collective-permute-done((f32[64,64,128]{2,1,0:T(8,128)S(1)}, f32[64,64,128]{2,1,0:T(8,128)S(1)}, u32[]{:S(2)}, u32[]{:S(2)}) %collective-permute-start.3) | collective-permute-done | bytes 2097184 | tf_op jit(solution)/shard_map/ppermute | solution.py:233
  143.1 1.4 copy-done.5
  144.5 19.2 %second_apply.1 = (f32[256,256]{1,0:T(8,128)}, f32[64,64,128]{2,1,0:T(8,128)}, bf16[64,64,128]{2,1,0:T(8,128)(2,1)}, f32[2,8,128]{2,1,0:T(8,128)}) custom-call(s32[1]{0:T(128)S(6)} %copy.10.count_ref, s32[64]{0:T(128)} %from_ref.3, s32[64]{0:T(128)} %to_ref.3, s32[3]{0:T(128)} %pad_add_fusion.at_ref, f32[64,64,128]{2,1,0:T(8,128)} %copy-done.1, ...), custom_call_target="tpu_custom_call" | custom-call | tf_op jit(solution)/shard_map/second_apply/pallas_call | solution.py:292
  163.7 2.9 %collective-permute-start.4 = (bf16[64,64,128]{2,1,0:T(8,128)(2,1)}, bf16[64,64,128]{2,1,0:T(8,128)(2,1)S(1)}, u32[]{:S(2)}, u32[]{:S(2)}) collective-permute-start(bf16[64,64,128]{2,1,0:T(8,128)(2,1)} %get-tuple-element.23), channel_id=1, source_target_pairs={{0,16},{16,0},{32,48},{48,32},{64,80},{80,64},{96,112},{112,96},{1... | collective-permute-start | bytes 3145736 | tf_op jit(solution)/shard_map/ppermute | solution.py:233
  166.8 2.4 %collective-permute-done.5.got_sums_ref = f32[2,8,128]{2,1,0:T(8,128)S(1)} collective-permute-done((f32[2,8,128]{2,1,0:T(8,128)}, f32[2,8,128]{2,1,0:T(8,128)S(1)}, u32[]{:S(2)}, u32[]{:S(2)}) %collective-permute-start.5) | collective-permute-done | bytes 8224 | tf_op jit(solution)/shard_map/ppermute | solution.py:233
  170.3 3.6 %join.3 = bf16[64,80,128]{2,1,0:T(8,128)(2,1)} custom-call(f32[64,64,128]{2,1,0:T(8,128)} %get-tuple-element.22.keep_ref, bf16[64,64,128]{2,1,0:T(8,128)(2,1)} %copy-done.7, f32[2,8,128]{2,1,0:T(8,128)} %get-tuple-element.24.sums_ref, f32[2,8,128]{2,1,0:T(8,128)} %copy-done.10), custom_call_target="tpu_custom_call" | custom-call | tf_op jit(solution)/shard_map/join/pallas_call | solution.py:245
  173.9 5.7 %all-to-all-start.3 = ((bf16[64,80,128]{2,1,0:T(8,128)(2,1)}), bf16[64,80,128]{2,1,0:T(8,128)(2,1)S(1)}, u32[]{:S(2)}, u32[]{:S(2)}) async-start(bf16[64,80,128]{2,1,0:T(8,128)(2,1)} %join.3), calls=%async_computation.3 | async-start | bytes 2621440 | tf_op jit(solution)/shard_map/all_to_all | solution.py:237
  179.6 19.9 %all-to-all-done.3.got_ref = bf16[64,80,128]{2,1,0:T(8,128)(2,1)S(1)} async-done(((bf16[64,80,128]{2,1,0:T(8,128)(2,1)}), bf16[64,80,128]{2,1,0:T(8,128)(2,1)S(1)}, u32[]{:S(2)}, u32[]{:S(2)}) %all-to-all-start.3) | async-done | bytes 1310752 | tf_op jit(solution)/shard_map/all_to_all | solution.py:237
  199.5 1.1 copy-done.4
  200.6 2.8 %ritz.1 = (f32[8,32,256]{2,1,0:T(8,128)}, f32[2,8,128]{2,1,0:T(8,128)}) custom-call(s32[3]{0:T(128)} %pad_add_fusion.at_ref, bf16[64,80,128]{2,1,0:T(8,128)(2,1)} %copy-done.4, f32[64,128]{1,0:T(8,128)} %get-tuple-element.19.v_ref, f32[256,256]{1,0:T(8,128)} %get-tuple-element.25.v2s_ref, f32[64,128]{1,0:T(8,128)} %get-tuple-element.26.w_ref, ...), custom_call_target="tpu_custom_call" | custom-call | tf_op jit(solution)/shard_map/ritz/pallas_call | solution.py:308
  203.4 1.3 fusion.1
  204.6 5.8 %all-to-all-start.4 = ((f32[8,32,256]{2,1,0:T(8,128)}), f32[8,32,256]{2,1,0:T(8,128)S(1)}, u32[]{:S(2)}, u32[]{:S(2)}) async-start(f32[8,32,256]{2,1,0:T(8,128)} %get-tuple-element.29), calls=%async_computation.4 | async-start | bytes 524288 | tf_op jit(solution)/shard_map/all_to_all | solution.py:317
  210.4 3.0 %bitcast_add_fusion = f32[1,256,256]{2,1,0:T(8,128)} fusion(f32[256,256]{1,0:T(8,128)S(1)} %copy-done.8, f32[16,256,256]{2,1,0:T(8,128)} %get-tuple-element.21.v_ref, s32[]{:T(128)S(6)} %select_n.26, f32[]{:T(128)} %bitcast.7, f32[]{:T(128)} %bitcast.6), kind=kLoop, calls=%fused_computation | loop fusion | flops 196608 | bytes 786444 | tf_op jit(solution)/shard_map/add | solution.py:319
  213.4 3.5 %all-to-all-done.4 = f32[8,32,256]{2,1,0:T(8,128)S(1)} async-done(((f32[8,32,256]{2,1,0:T(8,128)}), f32[8,32,256]{2,1,0:T(8,128)S(1)}, u32[]{:S(2)}, u32[]{:S(2)}) %all-to-all-start.4) | async-done | bytes 262176 | tf_op jit(solution)/shard_map/all_to_all | solution.py:317
  216.9 0.7 copy.11
  (25 shorter events, 2.5 us)
Async XLA Ops:
  0.6 1.0 copy-start
  37.6 5.9 %copy-start.2 = (f32[16,128,256]{2,1,0:T(8,128)}, f32[16,128,256]{2,1,0:T(8,128)S(1)}, u32[]{:S(2)}) copy-start(f32[16,128,256]{2,1,0:T(8,128)S(1)} %all_to_all.25.own_ref) | copy-start | bytes 6291460
  37.6 5.9 %collective-permute-start = (f32[16,128,256]{2,1,0:T(8,128)S(1)}, f32[16,128,256]{2,1,0:T(8,128)}, u32[]{:S(2)}, u32[]{:S(2)}) collective-permute-start(f32[16,128,256]{2,1,0:T(8,128)S(1)} %all_to_all.25.own_ref), channel_id=1, source_target_pairs={{0,16},{16,0},{32,48},{48,32},{64,80},{80,64},{96,112},{112,96},{1... | collective-permute-start | bytes 6291464 | tf_op jit(solution)/shard_map/ppermute | solution.py:233
  62.1 5.5 %collective-permute-start.1 = (bf16[64,64,128]{2,1,0:T(8,128)(2,1)}, bf16[64,64,128]{2,1,0:T(8,128)(2,1)S(1)}, u32[]{:S(2)}, u32[]{:S(2)}) collective-permute-start(bf16[64,64,128]{2,1,0:T(8,128)(2,1)} %get-tuple-element.17), channel_id=1, source_target_pairs={{0,16},{16,0},{32,48},{48,32},{64,80},{80,64},{96,112},{112,96},{1... | collective-permute-start | bytes 3145736 | tf_op jit(solution)/shard_map/ppermute | solution.py:233
  65.1 2.5 %collective-permute-start.2 = (f32[2,8,128]{2,1,0:T(8,128)}, f32[2,8,128]{2,1,0:T(8,128)S(1)}, u32[]{:S(2)}, u32[]{:S(2)}) collective-permute-start(f32[2,8,128]{2,1,0:T(8,128)} %get-tuple-element.18.sums_ref), channel_id=1, source_target_pairs={{0,16},{16,0},{32,48},{48,32},{64,80},{80,64},{96,112},{112,96},{1... | collective-permute-start | bytes 24584 | tf_op jit(solution)/shard_map/ppermute | solution.py:233
  67.6 0.6 copy-start.9
  67.6 1.1 copy-start.6
  72.3 25.9 %all-to-all-start.1 = ((bf16[64,80,128]{2,1,0:T(8,128)(2,1)}), bf16[64,80,128]{2,1,0:T(8,128)(2,1)S(1)}, u32[]{:S(2)}, u32[]{:S(2)}) async-start(bf16[64,80,128]{2,1,0:T(8,128)(2,1)} %join.2), calls=%async_computation.1 | async-start | bytes 2621440 | tf_op jit(solution)/shard_map/all_to_all | solution.py:237
  98.2 1.1 copy-start.3
  134.9 8.3 %copy-start.1 = (f32[64,64,128]{2,1,0:T(8,128)}, f32[64,64,128]{2,1,0:T(8,128)S(1)}, u32[]{:S(2)}) copy-start(f32[64,64,128]{2,1,0:T(8,128)S(1)} %all_to_all.26.own_ref) | copy-start | bytes 6291460
  134.9 8.3 %collective-permute-start.3 = (f32[64,64,128]{2,1,0:T(8,128)S(1)}, f32[64,64,128]{2,1,0:T(8,128)S(1)}, u32[]{:S(2)}, u32[]{:S(2)}) collective-permute-start(f32[64,64,128]{2,1,0:T(8,128)S(1)} %all_to_all.26.own_ref), channel_id=1, source_target_pairs={{0,16},{16,0},{32,48},{48,32},{64,80},{80,64},{96,112},{112,96},{1... | collective-permute-start | bytes 6291464 | tf_op jit(solution)/shard_map/ppermute | solution.py:233
  143.1 1.4 copy-start.5
  163.7 5.5 %collective-permute-start.4 = (bf16[64,64,128]{2,1,0:T(8,128)(2,1)}, bf16[64,64,128]{2,1,0:T(8,128)(2,1)S(1)}, u32[]{:S(2)}, u32[]{:S(2)}) collective-permute-start(bf16[64,64,128]{2,1,0:T(8,128)(2,1)} %get-tuple-element.23), channel_id=1, source_target_pairs={{0,16},{16,0},{32,48},{48,32},{64,80},{80,64},{96,112},{112,96},{1... | collective-permute-start | bytes 3145736 | tf_op jit(solution)/shard_map/ppermute | solution.py:233
  166.7 2.5 %collective-permute-start.5 = (f32[2,8,128]{2,1,0:T(8,128)}, f32[2,8,128]{2,1,0:T(8,128)S(1)}, u32[]{:S(2)}, u32[]{:S(2)}) collective-permute-start(f32[2,8,128]{2,1,0:T(8,128)} %get-tuple-element.24.sums_ref), channel_id=1, source_target_pairs={{0,16},{16,0},{32,48},{48,32},{64,80},{80,64},{96,112},{112,96},{1... | collective-permute-start | bytes 24584 | tf_op jit(solution)/shard_map/ppermute | solution.py:233
  169.2 0.6 copy-start.10
  169.2 1.1 copy-start.7
  173.9 36.5 %copy-start.8 = (f32[256,256]{1,0:T(8,128)S(1)}, f32[256,256]{1,0:T(8,128)}, u32[]{:S(2)}) copy-start(f32[256,256]{1,0:T(8,128)} %get-tuple-element.25.v2s_ref) | copy-start | bytes 786436
  173.9 25.6 %all-to-all-start.3 = ((bf16[64,80,128]{2,1,0:T(8,128)(2,1)}), bf16[64,80,128]{2,1,0:T(8,128)(2,1)S(1)}, u32[]{:S(2)}, u32[]{:S(2)}) async-start(bf16[64,80,128]{2,1,0:T(8,128)(2,1)} %join.3), calls=%async_computation.3 | async-start | bytes 2621440 | tf_op jit(solution)/shard_map/all_to_all | solution.py:237
  199.5 1.1 copy-start.4
  204.6 12.3 %all-to-all-start.4 = ((f32[8,32,256]{2,1,0:T(8,128)}), f32[8,32,256]{2,1,0:T(8,128)S(1)}, u32[]{:S(2)}, u32[]{:S(2)}) async-start(f32[8,32,256]{2,1,0:T(8,128)} %get-tuple-element.29), calls=%async_computation.4 | async-start | bytes 524288 | tf_op jit(solution)/shard_map/all_to_all | solution.py:317

commit v2 on v0

v2 whole, which is shorter than its diff:
```python
import jax
import jax.numpy as jnp
from jax import lax
from jax.experimental import pallas as pl
from jax.experimental.pallas import tpu as pltpu
from jax.sharding import PartitionSpec as P

F32, BF16 = jnp.float32, jnp.bfloat16
SEC, B, ROWS, LANES = 16, 256, 32, 128
CHIPS_X, N_OP = 4, 8
PIECES = CHIPS_X * SEC
TERMS, GROUP, STEP = 64, 8, 16
ENTRIES = SEC * B * B
CORE_SWAP = [(i, i ^ 1) for i in range(N_OP)]
GROUPS = [[(2 * x + core) * SEC + s for x in range(CHIPS_X) for s in range(SEC)] for core in range(2)]


def dot(a, b, contract):
    return lax.dot_general(a, b, ((contract[:1], contract[1:]), ((), ())), preferred_element_type=F32)


def fold(block):
    block = block.reshape(-1, 8, block.shape[-1])
    block = jnp.sum(block, axis=0)
    return sum(block[:, k:k + LANES] for k in range(0, block.shape[-1], LANES))


def block_rows(x, core):
    return pl.ds(pl.multiple_of((2 * x + core) * ROWS, ROWS), ROWS)


def term_copies(i, left_ref, right_ref, left, right, sems):
    at = pl.ds(i * GROUP, GROUP)
    return (
        pltpu.make_async_copy(left_ref.at[at], left.at[at], sems.at[0, i]),
        pltpu.make_async_copy(right_ref.at[at], right.at[at], sems.at[1, i]),
    )


def start_terms(count_ref, *refs):
    for i in range(TERMS // GROUP):
        @pl.when(i * GROUP < count_ref[0])
        def _():
            for copy in term_copies(i, *refs):
                copy.start()


def apply_terms(count_ref, from_ref, to_ref, x_ref, acc_ref, *refs):
    left, right = refs[2:4]

    def halves(t):
        source, target = from_ref[t], to_ref[t]
        first = dot(left[t], x_ref[source], (1, 0)).astype(BF16)
        second = dot(left[t], x_ref[target], (0, 0)).astype(BF16)
        return t, source, target, first, second

    def add(t, source, target, first, second):
        acc_ref[target] += dot(first, right[t], (1, 1))
        acc_ref[source] += dot(second, right[t], (1, 0))

    @pl.loop(0, TERMS // STEP)
    def _(i):
        live = count_ref[0] - i * STEP
        for k in range(STEP // GROUP):
            @pl.when(live > k * GROUP)
            def _():
                for copy in term_copies(i * (STEP // GROUP) + k, *refs):
                    copy.wait()

        @pl.when(live >= STEP)
        def _():
            held = halves(i * STEP)
            for j in range(1, STEP):
                ahead = halves(i * STEP + j)
                add(*held)
                held = ahead
            add(*held)

        @pl.when((live > 0) & (live < STEP))
        def _():
            @pl.loop(0, live)
            def _(j):
                add(*halves(i * STEP + j))


def keep_copies(core, acc_ref, keep_ref, sems):
    return [
        pltpu.make_async_copy(
            acc_ref.at[:, block_rows(x, core), :], keep_ref.at[pl.ds(x * SEC, SEC)], sems.at[x]
        )
        for x in range(CHIPS_X)
    ]


def split_out(core, acc_ref, send, send_ref, sems):
    copies = []
    for x in range(CHIPS_X):
        @pl.loop(0, SEC)
        def _(s):
            send[x * SEC + s] = acc_ref[s, block_rows(x, 1 - core), :].astype(BF16)

        at = pl.ds(x * SEC, SEC)
        copies.append(pltpu.make_async_copy(send.at[at], send_ref.at[at], sems.at[CHIPS_X + x]))
        copies[-1].start()
    return copies


def total_of(terms):
    return lax.fori_loop(0, SEC, lambda s, total: total + fold(terms(s)), jnp.zeros((8, LANES), F32))


def first_kernel(count_ref, from_ref, to_ref, at_ref, own_ref, other_ref, left_ref, right_ref,
                 keep_ref, send_ref, sums_ref, norm_ref, start, x_ref, acc_ref, send, left, right, term_sems, sems):
    core = at_ref[0]
    gathers = [
        pltpu.make_async_copy(
            ref.at[:, pl.ds(x * ROWS, ROWS), :], start.at[:, block_rows(x, at), :], sems.at[2 * x + k]
        )
        for x in range(CHIPS_X) for k, (ref, at) in enumerate(((own_ref, core), (other_ref, 1 - core)))
    ]
    for copy in gathers:
        copy.start()
    start_terms(count_ref, left_ref, right_ref, left, right, term_sems)

    @pl.loop(0, SEC)
    def _(s):
        acc_ref[s] = jnp.zeros((B, B), F32)

    for copy in gathers:
        copy.wait()
    mean_sq = jnp.sum(total_of(lambda s: start[s] * start[s]), keepdims=True) / ENTRIES
    scale = 1.0 / jnp.sqrt(mean_sq + 1e-06)
    norm_ref[0] = jnp.broadcast_to(scale, (8, LANES))
    norm_ref[1] = jnp.broadcast_to(mean_sq, (8, LANES))

    @pl.loop(0, SEC)
    def _(s):
        x_ref[s] = (start[s] * scale).astype(BF16)

    apply_terms(count_ref, from_ref, to_ref, x_ref, acc_ref, left_ref, right_ref, left, right, term_sems)

    copies = keep_copies(core, acc_ref, keep_ref, sems)
    for copy in copies:
        copy.start()
    copies += split_out(core, acc_ref, send, send_ref, sems)
    sums_ref[0] = scale * total_of(lambda s: start[s] * acc_ref[s])
    for copy in copies:
        copy.wait()


def second_kernel(count_ref, from_ref, to_ref, at_ref, own_ref, other_ref, more_ref, left_ref, right_ref,
                  keep_ref, send_ref, sums_ref, mine_ref, x_ref, acc_ref, send, left, right, term_sems, sems):
    core = at_ref[0]
    gathers = [
        pltpu.make_async_copy(
            ref.at[pl.ds(x * SEC, SEC)], x_ref.at[:, block_rows(x, at), :], sems.at[2 * x + k]
        )
        for x in range(CHIPS_X) for k, (ref, at) in enumerate(((own_ref, core), (other_ref, 1 - core)))
    ]
    for copy in gathers:
        copy.start()
    start_terms(count_ref, left_ref, right_ref, left, right, term_sems)

    @pl.loop(0, SEC)
    def _(s):
        acc_ref[s] = jnp.zeros((B, B), F32)

    for copy in gathers:
        copy.wait()
    apply_terms(count_ref, from_ref, to_ref, x_ref, acc_ref, left_ref, right_ref, left, right, term_sems)

    copies = keep_copies(core, acc_ref, keep_ref, sems)
    for copy in copies:
        copy.start()
    copies += split_out(core, acc_ref, send, send_ref, sems)
    mine_ref[...] = x_ref[at_ref[1]].astype(F32)
    sums_ref[0] = total_of(lambda s: x_ref[s].astype(F32) * acc_ref[s])
    sums_ref[1:] = more_ref[...]
    for copy in copies:
        copy.wait()


def join_kernel(keep_ref, got_ref, sums_ref, got_sums_ref, out_ref):
    row = lax.broadcasted_iota(jnp.int32, (16, LANES), 0)
    tile = jnp.zeros((16, LANES), F32)
    for k in range(sums_ref.shape[0]):
        rest = jnp.sum(sums_ref[k] + got_sums_ref[k], keepdims=True)
        for part in range(3):
            top = rest.astype(BF16).astype(F32)
            tile = jnp.where(row == 3 * k + part, top, tile)
            rest = rest - top
    tile = tile.astype(BF16)

    @pl.loop(0, PIECES)
    def _(p):
        block = (keep_ref[p] + got_ref[p].astype(F32)).astype(BF16)
        out_ref[p, :ROWS, :] = block[:, :LANES]
        out_ref[p, ROWS:2 * ROWS, :] = block[:, LANES:]
        out_ref[p, 2 * ROWS:, :] = tile


def gathered_sum(got_ref, scalars):
    def add(p, total):
        return total + got_ref[p].astype(F32)

    total = lax.fori_loop(0, PIECES, add, jnp.zeros((2 * ROWS + 16, LANES), F32))
    row = lax.broadcasted_iota(jnp.int32, (16, LANES), 0)
    tile = total[2 * ROWS:, :]
    means = [
        jnp.sum(jnp.where((row >= 3 * k) & (row < 3 * k + 3), tile, 0.0), keepdims=True) / (LANES * ENTRIES)
        for k in range(scalars)
    ]
    return total[:2 * ROWS, :], means


def correct_kernel(got_ref, start_ref, diag_ref, norm_ref, copies_ref, sums_ref, corr_ref, sigma_ref, theta_ref):
    sigma, (theta,) = gathered_sum(got_ref, 1)
    vec = start_ref[...] * norm_ref[0, :1, :1]
    corr = (sigma - theta * vec) / jnp.maximum(jnp.abs(diag_ref[...] - theta), 1.0)
    sigma_ref[...] = sigma
    corr_ref[...] = corr
    theta_ref[...] = jnp.broadcast_to(theta, theta_ref.shape)
    for k, other in enumerate((vec, corr, sigma)):
        sums_ref[k] = fold(other * corr)
    rounded = corr.astype(BF16)

    @pl.loop(0, PIECES)
    def _(p):
        copies_ref[p, :, :LANES] = rounded[:ROWS, :]
        copies_ref[p, :, LANES:] = rounded[ROWS:, :]


def ritz_kernel(got_ref, start_ref, norm_ref, corr_ref, sigma_ref, theta_ref, out_ref, coef_ref):
    h_corr, (quad, along, corr_sq, cross) = gathered_sum(got_ref, 4)
    theta, scale, mean_sq = theta_ref[:1, :1], norm_ref[0, :1, :1], norm_ref[1, :1, :1]
    vec_sq = mean_sq * scale * scale
    ortho_sq = jnp.maximum(corr_sq - along * along * (2.0 - vec_sq), 0.0)
    inv = 1.0 / jnp.sqrt(ortho_sq + 1e-06)
    beta = (cross - along * theta) * inv
    gamma = (quad - 2.0 * along * cross + along * along * theta) * inv * inv
    lowest = 0.5 * (theta + gamma) - jnp.sqrt((0.5 * (theta - gamma)) ** 2 + beta * beta)
    norm = jnp.sqrt(beta * beta + (lowest - theta) ** 2)
    one, two = beta / norm, (lowest - theta) / norm
    coef_ref[0] = jnp.broadcast_to(scale * (one - two * along * inv), (8, LANES))
    coef_ref[1] = jnp.broadcast_to(two * inv, (8, LANES))
    vec, sigma = start_ref[...] * scale, sigma_ref[...]
    vec_two, sigma_two = (corr_ref[...] - along * vec) * inv, (h_corr - along * sigma) * inv
    resid = one * sigma + two * sigma_two - lowest * (one * vec + two * vec_two)
    for p in range(N_OP):
        out_ref[p, :, :LANES] = resid[:ROWS, :]
        out_ref[p, :, LANES:] = resid[ROWS:, :]


def shape(*dims, dtype=F32):
    return jax.ShapeDtypeStruct(dims, dtype)


SMEM = pl.BlockSpec(memory_space=pltpu.SMEM)
WHOLE = pl.BlockSpec(memory_space=pltpu.VMEM)
ANY = pl.BlockSpec(memory_space=pl.ANY)
TERM_SCRATCH = [
    pltpu.VMEM((SEC, B, B), BF16),
    pltpu.VMEM((SEC, B, B), F32),
    pltpu.VMEM((PIECES, ROWS, B), BF16),
    pltpu.VMEM((TERMS, B, B), BF16),
    pltpu.VMEM((TERMS, B, B), BF16),
    pltpu.SemaphoreType.DMA((2, TERMS // GROUP)),
    pltpu.SemaphoreType.DMA((2 * CHIPS_X,)),
]
SPLIT_SHAPES = [shape(PIECES, ROWS, B), shape(PIECES, ROWS, B, dtype=BF16)]


def call(kernel, mib, **kwargs):
    return pl.pallas_call(
        kernel, compiler_params=pltpu.CompilerParams(vmem_limit_bytes=mib << 20), name=kernel.__name__, **kwargs
    )


def swap(x):
    return lax.ppermute(x, "op", CORE_SWAP)


def exchange(x):
    return lax.all_to_all(x, ("op", "sec"), 0, 0, tiled=True, axis_index_groups=GROUPS)


def own_rows(block, op):
    rows = lax.dynamic_slice_in_dim(block, op * ROWS, ROWS, 0)
    return jnp.concatenate([rows[:, :LANES], rows[:, LANES:]], axis=0)


def reduce_partial(keep, send, sums):
    payload = call(
        join_kernel,
        16,
        out_shape=shape(PIECES, 2 * ROWS + 16, LANES, dtype=BF16),
        in_specs=[WHOLE] * 4,
        out_specs=WHOLE,
    )(keep, swap(send), sums, swap(sums))
    return exchange(payload)


def per_device(start_vector, diag_guess, left_env, right_env, sector_from, sector_to, term_count):
    op, sector = lax.axis_index("op"), lax.axis_index("sec")
    core = op % 2
    at = jnp.stack([core, sector]).astype(jnp.int32)
    terms = (term_count, sector_from, sector_to, at)

    mine = lax.dynamic_index_in_dim(start_vector.reshape(CHIPS_X, 2, ROWS, B), core, 1, keepdims=False)
    mine = jnp.broadcast_to(mine.reshape(1, B // 2, B), (SEC, B // 2, B))
    own = lax.all_to_all(mine, "sec", 0, 0, tiled=True)
    start, diag = own_rows(start_vector[0], op), own_rows(diag_guess[0], op)

    keep, send, sums, norm = call(
        first_kernel,
        32,
        out_shape=SPLIT_SHAPES + [shape(1, 8, LANES), shape(2, 8, LANES)],
        in_specs=[SMEM] * 4 + [ANY] * 4,
        out_specs=[ANY] * 2 + [WHOLE] * 2,
        scratch_shapes=[pltpu.VMEM((SEC, B, B), F32)] + TERM_SCRATCH,
    )(*terms, own, swap(own), left_env, right_env)

    got = reduce_partial(keep, send, sums)
    copies, more, corr, sigma, theta = call(
        correct_kernel,
        16,
        out_shape=[
            shape(PIECES, ROWS, B, dtype=BF16),
            shape(3, 8, LANES),
            shape(2 * ROWS, LANES),
            shape(2 * ROWS, LANES),
            shape(8, LANES),
        ],
        in_specs=[WHOLE] * 4,
        out_specs=[WHOLE] * 5,
    )(got, start, diag, norm)

    own = exchange(copies)
    keep, send, sums, corr_mine = call(
        second_kernel,
        28,
        out_shape=SPLIT_SHAPES + [shape(4, 8, LANES), shape(B, B)],
        in_specs=[SMEM] * 4 + [ANY] * 2 + [WHOLE] + [ANY] * 2,
        out_specs=[ANY] * 2 + [WHOLE] * 2,
        scratch_shapes=TERM_SCRATCH,
    )(*terms, own, swap(own), more, left_env, right_env)

    got = reduce_partial(keep, send, sums)
    resid, coefs = call(
        ritz_kernel,
        16,
        out_shape=[shape(N_OP, ROWS, B), shape(2, 8, LANES)],
        in_specs=[WHOLE] * 6,
        out_specs=[WHOLE] * 2,
    )(got, start, norm, corr, sigma, theta)

    ritz_residual = lax.all_to_all(resid, "op", 0, 0, tiled=True).reshape(1, B, B)
    ritz_vector = coefs[0, 0, 0] * start_vector + coefs[1, 0, 0] * corr_mine[None]
    return (ritz_vector, ritz_residual)


def solution(mesh):
    return jax.shard_map(
        per_device,
        mesh=mesh,
        in_specs=(
            P("sec", None, None),
            P("sec", None, None),
            P(("op", "sec"), None, None),
            P(("op", "sec"), None, None),
            P(("op", "sec")),
            P(("op", "sec")),
            P(("op", "sec")),
        ),
        out_specs=(P("sec", None, None), P("sec", None, None)),
        check_vma=False,
    )
```

time: 2160 us -> 183 us (0.08)
  matrix products: 722 us -> 0 us
  loops' own time: 577 us -> 0 us
  waiting for transfers between devices: 384 us -> 32.7 us
  local copies, waits for them, and re-layouts: 161 us -> 13.3 us
  other arithmetic: 111 us -> 2.07 us
  blocking collectives: 164 us -> 81.4 us
  starting transfers between devices: 0.24 us -> 34.6 us
    dot_general x256 -> x0, matrix products: 722 us -> none  [the longest x128 364 us: add_term(): backward = jnp.dot(second, right_block, preferred_element_type=jnp.float32)]
    another operation x2 -> x0, loops' own time: 577 us -> none  [apply_ham(): lax.fori_loop(0, live_terms, add_term, jnp.zeros(blocks.shape, jnp.float32))]
    psum x5 -> x0, blocking collectives: 164 us -> none  [the longest x1 36.1 us: per_device(): start_sq = lax.psum(jnp.sum(start_vector * start_vector), 'sec') / entries]
    dynamic_slice x256 -> x2, local copies, waits for them, and re-layouts: 156 us -> 1.69 us  [the longest x1 0.92 us: per_device(): lax.dynamic_index_in_dim(start_vector.reshape(CHIPS_X, 2, ROWS, B), core,...]
    unnamed x8 -> x0, waiting for transfers between devices: 153 us -> none
    psum x2 -> x0, waiting for transfers between devices: 122 us -> none  [apply_ham(): return lax.psum(owned, 'op')]
    all_gather x2 -> x0, waiting for transfers between devices: 109 us -> none  [apply_ham(): lax.all_gather(vector.astype(jnp.bfloat16), 'sec', axis=0, tiled=True)]
    another operation x128 -> x1, other arithmetic: 99.2 us -> 0.08 us  [per_device(): at = jnp.stack([core, sector]).astype(jnp.int32)]
  transfers between devices with their start and end apart: 6 -> 8, of which waited for: 6 -> 6; matrix products, arithmetic and copies ran while one was open for 0% -> 2% of each run, Pallas kernels for 0% -> 0%
where the time goes in v2:
time: 183 us
  blocking collectives  81.4 us (44%)
  starting transfers between devices  34.6 us (19%)
  waiting for transfers between devices  32.7 us (18%)
  Pallas kernels  17.5 us (10%)
  local copies, waits for them, and re-layouts  13.3 us (7%)
  other arithmetic  2.07 us (1%)
    all_to_all x2, blocking collectives, exchange(): lax.all_to_all(x, ('op', 'sec'), 0, 0, tiled=True, axis_index_groups=GROUPS)  45.7 us
    all_to_all x1, blocking collectives, per_device(): own = lax.all_to_all(mine, 'sec', 0, 0, tiled=True)  35.8 us
    ppermute x6, starting transfers between devices, swap(): return lax.ppermute(x, 'op', CORE_SWAP)  22.4 us
    all_to_all x1, waiting for transfers between devices, exchange(): lax.all_to_all(x, ('op', 'sec'), 0, 0, tiled=True, axis_index_groups=GROUPS)  18.8 us
    unnamed x13, local copies, waits for them, and re-layouts  10.9 us
    ppermute x6, waiting for transfers between devices, swap(): return lax.ppermute(x, 'op', CORE_SWAP)  9.9 us
    pallas_call x1, Pallas kernels, per_device(): call(first_kernel, 32, out_shape=SPLIT_SHAPES + [shape(1, 8, LANES), shap...  7.31 us
    all_to_all x1, starting transfers between devices, per_device(): lax.all_to_all(resid, 'op', 0, 0, tiled=True).reshape(1, B, B)  6.11 us
  transfers between devices with their start and end apart: 8, of which 6 were waited for; matrix products, arithmetic and copies ran while one was open for 2% of the time, Pallas kernels for 0%

profile of v2, /device:TPU:1, one launch (start us, length us, event | category | flops | bytes accessed | tf_op | source)
XLA Modules:
  0.0 183.0 jit_solution(11020336058113002599)
XLA Ops:
  0.6 0.9 constant_dynamic-slice_fusion
  1.6 0.2 broadcast_in_dim.9
  1.8 35.8 %all_to_all.25.own_ref = f32[16,128,256]{2,1,0:T(8,128)S(1)} all-to-all(f32[16,128,256]{2,1,0:T(8,128)S(1)} %broadcast_in_dim.9), channel_id=1, replica_groups=mesh['op'=8,'sec'=16] {'sec'}, dimensions={0} | all-to-all | bytes 4194304 | tf_op jit(solution)/shard_map/all_to_all | solution.py:311
  37.6 2.0 %collective-permute-start = (f32[16,128,256]{2,1,0:T(8,128)S(1)}, f32[16,128,256]{2,1,0:T(8,128)}, u32[]{:S(2)}, u32[]{:S(2)}) collective-permute-start(f32[16,128,256]{2,1,0:T(8,128)S(1)} %all_to_all.25.own_ref), channel_id=1, source_target_pairs={{0,16},{16,0},{32,48},{48,32},{64,80},{80,64},{96,112},{112,96},{1... | collective-permute-start | bytes 6291464 | tf_op jit(solution)/shard_map/ppermute | solution.py:280
  40.3 3.2 %collective-permute-done.other_ref = f32[16,128,256]{2,1,0:T(8,128)} collective-permute-done((f32[16,128,256]{2,1,0:T(8,128)S(1)}, f32[16,128,256]{2,1,0:T(8,128)}, u32[]{:S(2)}, u32[]{:S(2)}) %collective-permute-start) | collective-permute-done | bytes 2097184 | tf_op jit(solution)/shard_map/ppermute | solution.py:280
  43.5 3.4 %copy-done = bf16[64,256,256]{2,1,0:T(8,128)(2,1)S(1)} copy-done((bf16[64,256,256]{2,1,0:T(8,128)(2,1)S(1)}, bf16[64,256,256]{2,1,0:T(8,128)(2,1)}, u32[]{:S(2)}) %copy-start) | copy-done | bytes 8388632
  46.8 7.3 %first_kernel.1 = (f32[64,32,256]{2,1,0:T(8,128)S(1)}, bf16[64,32,256]{2,1,0:T(8,128)(2,1)S(1)}, f32[1,8,128]{2,1,0:T(8,128)S(1)}, f32[2,8,128]{2,1,0:T(8,128)S(1)}) custom-call(s32[1]{0:T(128)S(6)} %copy.10.count_ref, s32[64]{0:T(128)S(1)} %copy-done.3, s32[64]{0:T(128)S(1)} %copy-done.4, s32[2]{0:T(128)S(1)} %pad_add_fusion.at_ref, ...), custom_call_target="tpu_custom_call" | custom-call | tf_op jit(solution)/shard_map/first_kernel/pallas_call | solution.py:314
  54.2 8.1 %collective-permute-start.1 = (bf16[64,32,256]{2,1,0:T(8,128)(2,1)S(1)}, bf16[64,32,256]{2,1,0:T(8,128)(2,1)S(1)}, u32[]{:S(2)}, u32[]{:S(2)}) collective-permute-start(bf16[64,32,256]{2,1,0:T(8,128)(2,1)S(1)} %get-tuple-element.18), channel_id=1, source_target_pairs={{0,16},{16,0},{32,48},{48,32},{64,80},{80,64},{96,112},{112,96},{1... | collective-permute-start | bytes 3145736 | tf_op jit(solution)/shard_map/ppermute | solution.py:280
  62.2 0.1 collective-permute-start.2
  62.3 2.2 %collective-permute-done.2.got_sums_ref = f32[1,8,128]{2,1,0:T(8,128)S(1)} collective-permute-done((f32[1,8,128]{2,1,0:T(8,128)S(1)}, f32[1,8,128]{2,1,0:T(8,128)S(1)}, u32[]{:S(2)}, u32[]{:S(2)}) %collective-permute-start.2) | collective-permute-done | bytes 4128 | tf_op jit(solution)/shard_map/ppermute | solution.py:280
  64.5 1.7 join_kernel.2
  66.2 6.1 %all-to-all-start.1 = ((bf16[64,80,128]{2,1,0:T(8,128)(2,1)}), bf16[64,80,128]{2,1,0:T(8,128)(2,1)S(1)}, u32[]{:S(2)}, u32[]{:S(2)}) async-start(bf16[64,80,128]{2,1,0:T(8,128)(2,1)} %join_kernel.2), calls=%async_computation.1 | async-start | bytes 2621440 | tf_op jit(solution)/shard_map/all_to_all | solution.py:284
  72.3 0.8 dynamic-slice_bitcast_fusion
  73.1 18.8 %all-to-all-done.1.got_ref = bf16[64,80,128]{2,1,0:T(8,128)(2,1)S(1)} async-done(((bf16[64,80,128]{2,1,0:T(8,128)(2,1)}), bf16[64,80,128]{2,1,0:T(8,128)(2,1)S(1)}, u32[]{:S(2)}, u32[]{:S(2)}) %all-to-all-start.1) | async-done | bytes 1310752 | tf_op jit(solution)/shard_map/all_to_all | solution.py:284
  92.0 0.9 correct_kernel.1
  92.9 21.7 %all_to_all.26.own_ref = bf16[64,32,256]{2,1,0:T(8,128)(2,1)S(1)} all-to-all(bf16[64,32,256]{2,1,0:T(8,128)(2,1)S(1)} %get-tuple-element.21), channel_id=1, replica_groups={{0,1,2,3,4,5,6,7,8,9,10,11,12,13,14,15,32,33,34,35,36,37,38,39,40,41,42..., dimensions={0} | all-to-all | bytes 2097152 | tf_op jit(solution)/shard_map/all_to_all | solution.py:284
  114.6 3.3 %collective-permute-start.3 = (bf16[64,32,256]{2,1,0:T(8,128)(2,1)S(1)}, bf16[64,32,256]{2,1,0:T(8,128)(2,1)S(1)}, u32[]{:S(2)}, u32[]{:S(2)}) collective-permute-start(bf16[64,32,256]{2,1,0:T(8,128)(2,1)S(1)} %all_to_all.26.own_ref), channel_id=1, source_target_pairs={{0,16},{16,0},{32,48},{48,32},{64,80},{80,64},{96,112},{112,96},{1... | collective-permute-start | bytes 3145736 | tf_op jit(solution)/shard_map/ppermute | solution.py:280
  117.9 2.3 %collective-permute-done.3.other_ref = bf16[64,32,256]{2,1,0:T(8,128)(2,1)S(1)} collective-permute-done((bf16[64,32,256]{2,1,0:T(8,128)(2,1)S(1)}, bf16[64,32,256]{2,1,0:T(8,128)(2,1)S(1)}, u32[]{:S(2)}, u32[]{:S(2)}) %collective-permute-start.3) | collective-permute-done | bytes 1048608 | tf_op jit(solution)/shard_map/ppermute | solution.py:280
  120.2 3.4 %copy-done.1 = bf16[64,256,256]{2,1,0:T(8,128)(2,1)S(1)} copy-done((bf16[64,256,256]{2,1,0:T(8,128)(2,1)S(1)}, bf16[64,256,256]{2,1,0:T(8,128)(2,1)}, u32[]{:S(2)}) %copy-start.1) | copy-done | bytes 8388632
  123.6 3.4 %copy-done.2 = bf16[64,256,256]{2,1,0:T(8,128)(2,1)S(1)} copy-done((bf16[64,256,256]{2,1,0:T(8,128)(2,1)S(1)}, bf16[64,256,256]{2,1,0:T(8,128)(2,1)}, u32[]{:S(2)}) %copy-start.2) | copy-done | bytes 8388632
  127.0 5.5 %second_kernel.1 = (f32[64,32,256]{2,1,0:T(8,128)S(1)}, bf16[64,32,256]{2,1,0:T(8,128)(2,1)S(1)}, f32[4,8,128]{2,1,0:T(8,128)S(1)}, f32[256,256]{1,0:T(8,128)S(1)}) custom-call(s32[1]{0:T(128)S(6)} %copy.10.count_ref, s32[64]{0:T(128)S(1)} %copy-done.3, s32[64]{0:T(128)S(1)} %copy-done.4, s32[2]{0:T(128)S(1)} %pad_add_fusion.at_ref, ...), custom_call_target="tpu_custom_call" | custom-call | tf_op jit(solution)/shard_map/second_kernel/pallas_call | solution.py:339
  132.5 8.9 %collective-permute-start.4 = (bf16[64,32,256]{2,1,0:T(8,128)(2,1)S(1)}, bf16[64,32,256]{2,1,0:T(8,128)(2,1)S(1)}, u32[]{:S(2)}, u32[]{:S(2)}) collective-permute-start(bf16[64,32,256]{2,1,0:T(8,128)(2,1)S(1)} %get-tuple-element.24), channel_id=1, source_target_pairs={{0,16},{16,0},{32,48},{48,32},{64,80},{80,64},{96,112},{112,96},{1... | collective-permute-start | bytes 3145736 | tf_op jit(solution)/shard_map/ppermute | solution.py:280
  141.4 0.1 collective-permute-start.5
  141.4 2.2 %collective-permute-done.5.got_sums_ref = f32[4,8,128]{2,1,0:T(8,128)S(1)} collective-permute-done((f32[4,8,128]{2,1,0:T(8,128)S(1)}, f32[4,8,128]{2,1,0:T(8,128)S(1)}, u32[]{:S(2)}, u32[]{:S(2)}) %collective-permute-start.5) | collective-permute-done | bytes 16416 | tf_op jit(solution)/shard_map/ppermute | solution.py:280
  143.7 0.6 join_kernel.3
  144.3 23.9 %all_to_all.27.got_ref = bf16[64,80,128]{2,1,0:T(8,128)(2,1)S(1)} all-to-all(bf16[64,80,128]{2,1,0:T(8,128)(2,1)S(1)} %join_kernel.3), channel_id=1, replica_groups={{0,1,2,3,4,5,6,7,8,9,10,11,12,13,14,15,32,33,34,35,36,37,38,39,40,41,42..., dimensions={0} | all-to-all | bytes 2621440 | tf_op jit(solution)/shard_map/all_to_all | solution.py:284
  168.2 1.4 ritz_kernel.1
  169.7 6.1 %all-to-all-start.4 = ((f32[8,32,256]{2,1,0:T(8,128)}), f32[8,32,256]{2,1,0:T(8,128)S(1)}, u32[]{:S(2)}, u32[]{:S(2)}) async-start(f32[8,32,256]{2,1,0:T(8,128)} %get-tuple-element.31), calls=%async_computation.4 | async-start | bytes 524288 | tf_op jit(solution)/shard_map/all_to_all | solution.py:357
  175.8 0.6 fusion.2
  176.4 2.0 %bitcast_add_fusion = f32[1,256,256]{2,1,0:T(8,128)} fusion(f32[256,256]{1,0:T(8,128)S(1)} %get-tuple-element.30, f32[1,256,256]{2,1,0:T(8,128)S(1)} %copy-done.5, f32[]{:T(128)} %bitcast.7, f32[]{:T(128)} %bitcast.6), kind=kLoop, calls=%fused_computation | loop fusion | flops 196608 | bytes 786440 | tf_op jit(solution)/shard_map/add | solution.py:358
  178.4 4.0 %all-to-all-done.4 = f32[8,32,256]{2,1,0:T(8,128)S(1)} async-done(((f32[8,32,256]{2,1,0:T(8,128)}), f32[8,32,256]{2,1,0:T(8,128)S(1)}, u32[]{:S(2)}, u32[]{:S(2)}) %all-to-all-start.4) | async-done | bytes 262176 | tf_op jit(solution)/shard_map/all_to_all | solution.py:357
  182.3 0.7 copy.11
  (16 shorter events, 0.1 us)
Async XLA Ops:
  1.8 41.7 %copy-start.3 = (s32[64]{0:T(128)S(1)}, s32[64]{0:T(128)}, u32[]{:S(2)}) copy-start(s32[64]{0:T(128)} %from_ref.3) | copy-start | bytes 772
  1.8 41.7 %copy-start.4 = (s32[64]{0:T(128)S(1)}, s32[64]{0:T(128)}, u32[]{:S(2)}) copy-start(s32[64]{0:T(128)} %to_ref.3) | copy-start | bytes 772
  37.6 5.9 %collective-permute-start = (f32[16,128,256]{2,1,0:T(8,128)S(1)}, f32[16,128,256]{2,1,0:T(8,128)}, u32[]{:S(2)}, u32[]{:S(2)}) collective-permute-start(f32[16,128,256]{2,1,0:T(8,128)S(1)} %all_to_all.25.own_ref), channel_id=1, source_target_pairs={{0,16},{16,0},{32,48},{48,32},{64,80},{80,64},{96,112},{112,96},{1... | collective-permute-start | bytes 6291464 | tf_op jit(solution)/shard_map/ppermute | solution.py:280
  43.5 3.4 %copy-start = (bf16[64,256,256]{2,1,0:T(8,128)(2,1)S(1)}, bf16[64,256,256]{2,1,0:T(8,128)(2,1)}, u32[]{:S(2)}) copy-start(bf16[64,256,256]{2,1,0:T(8,128)(2,1)} %left_ref.3) | copy-start | bytes 25165828
  54.2 10.3 %collective-permute-start.1 = (bf16[64,32,256]{2,1,0:T(8,128)(2,1)S(1)}, bf16[64,32,256]{2,1,0:T(8,128)(2,1)S(1)}, u32[]{:S(2)}, u32[]{:S(2)}) collective-permute-start(bf16[64,32,256]{2,1,0:T(8,128)(2,1)S(1)} %get-tuple-element.18), channel_id=1, source_target_pairs={{0,16},{16,0},{32,48},{48,32},{64,80},{80,64},{96,112},{112,96},{1... | collective-permute-start | bytes 3145736 | tf_op jit(solution)/shard_map/ppermute | solution.py:280
  62.2 2.3 %collective-permute-start.2 = (f32[1,8,128]{2,1,0:T(8,128)S(1)}, f32[1,8,128]{2,1,0:T(8,128)S(1)}, u32[]{:S(2)}, u32[]{:S(2)}) collective-permute-start(f32[1,8,128]{2,1,0:T(8,128)S(1)} %get-tuple-element.19.sums_ref), channel_id=1, source_target_pairs={{0,16},{16,0},{32,48},{48,32},{64,80},{80,64},{96,112},{112,96},{1... | collective-permute-start | bytes 12296 | tf_op jit(solution)/shard_map/ppermute | solution.py:280
  66.2 6.1 %copy-start.5 = (f32[1,256,256]{2,1,0:T(8,128)S(1)}, f32[1,256,256]{2,1,0:T(8,128)}, u32[]{:S(2)}) copy-start(f32[1,256,256]{2,1,0:T(8,128)} %param.7) | copy-start | bytes 786436
  66.2 25.8 %all-to-all-start.1 = ((bf16[64,80,128]{2,1,0:T(8,128)(2,1)}), bf16[64,80,128]{2,1,0:T(8,128)(2,1)S(1)}, u32[]{:S(2)}, u32[]{:S(2)}) async-start(bf16[64,80,128]{2,1,0:T(8,128)(2,1)} %join_kernel.2), calls=%async_computation.1 | async-start | bytes 2621440 | tf_op jit(solution)/shard_map/all_to_all | solution.py:284
  114.6 5.6 %collective-permute-start.3 = (bf16[64,32,256]{2,1,0:T(8,128)(2,1)S(1)}, bf16[64,32,256]{2,1,0:T(8,128)(2,1)S(1)}, u32[]{:S(2)}, u32[]{:S(2)}) collective-permute-start(bf16[64,32,256]{2,1,0:T(8,128)(2,1)S(1)} %all_to_all.26.own_ref), channel_id=1, source_target_pairs={{0,16},{16,0},{32,48},{48,32},{64,80},{80,64},{96,112},{112,96},{1... | collective-permute-start | bytes 3145736 | tf_op jit(solution)/shard_map/ppermute | solution.py:280
  120.2 3.4 %copy-start.1 = (bf16[64,256,256]{2,1,0:T(8,128)(2,1)S(1)}, bf16[64,256,256]{2,1,0:T(8,128)(2,1)}, u32[]{:S(2)}) copy-start(bf16[64,256,256]{2,1,0:T(8,128)(2,1)} %left_ref.3) | copy-start | bytes 25165828
  123.6 3.4 %copy-start.2 = (bf16[64,256,256]{2,1,0:T(8,128)(2,1)S(1)}, bf16[64,256,256]{2,1,0:T(8,128)(2,1)}, u32[]{:S(2)}) copy-start(bf16[64,256,256]{2,1,0:T(8,128)(2,1)} %right_ref.3) | copy-start | bytes 25165828
  132.5 11.2 %collective-permute-start.4 = (bf16[64,32,256]{2,1,0:T(8,128)(2,1)S(1)}, bf16[64,32,256]{2,1,0:T(8,128)(2,1)S(1)}, u32[]{:S(2)}, u32[]{:S(2)}) collective-permute-start(bf16[64,32,256]{2,1,0:T(8,128)(2,1)S(1)} %get-tuple-element.24), channel_id=1, source_target_pairs={{0,16},{16,0},{32,48},{48,32},{64,80},{80,64},{96,112},{112,96},{1... | collective-permute-start | bytes 3145736 | tf_op jit(solution)/shard_map/ppermute | solution.py:280
  141.4 2.3 %collective-permute-start.5 = (f32[4,8,128]{2,1,0:T(8,128)S(1)}, f32[4,8,128]{2,1,0:T(8,128)S(1)}, u32[]{:S(2)}, u32[]{:S(2)}) collective-permute-start(f32[4,8,128]{2,1,0:T(8,128)S(1)} %get-tuple-element.25.sums_ref), channel_id=1, source_target_pairs={{0,16},{16,0},{32,48},{48,32},{64,80},{80,64},{96,112},{112,96},{1... | collective-permute-start | bytes 49160 | tf_op jit(solution)/shard_map/ppermute | solution.py:280
  169.7 12.6 %all-to-all-start.4 = ((f32[8,32,256]{2,1,0:T(8,128)}), f32[8,32,256]{2,1,0:T(8,128)S(1)}, u32[]{:S(2)}, u32[]{:S(2)}) async-start(f32[8,32,256]{2,1,0:T(8,128)} %get-tuple-element.31), calls=%async_computation.4 | async-start | bytes 524288 | tf_op jit(solution)/shard_map/all_to_all | solution.py:357

commit v3 on v0

v3 whole, which is shorter than its diff:
```python
import jax
import jax.numpy as jnp
from jax import lax
from jax.experimental import pallas as pl
from jax.experimental.pallas import tpu as pltpu
from jax.sharding import PartitionSpec as P

F32, BF16 = jnp.float32, jnp.bfloat16
SEC, B, LANES = 16, 256, 128
HALF = B // 2
CHIPS_X, N_OP = 4, 8
TERMS, GROUP, STEP = 64, 8, 16
ENTRIES = SEC * B * B
CORE_SWAP = [(i, i ^ 1) for i in range(N_OP)]
ALONG_X = [[2 * x + core for x in range(CHIPS_X)] for core in range(2)]
SCALARS = 16


def dot(a, b, contract):
    return lax.dot_general(a, b, ((contract[:1], contract[1:]), ((), ())), preferred_element_type=F32)


def fold(block):
    block = jnp.sum(block.reshape(-1, 8, block.shape[-1]), axis=0)
    return sum(block[:, k:k + LANES] for k in range(0, block.shape[-1], LANES))


def half_rows(core):
    return pl.ds(pl.multiple_of(core * HALF, HALF), HALF)


def fold_columns(half):
    return jnp.concatenate([half[:, :LANES], half[:, LANES:]], axis=0)


def store_half(ref, at, columns):
    ref[at, :, :LANES] = columns[:HALF, :]
    ref[at, :, LANES:] = columns[HALF:, :]


def total_of(ref):
    return jnp.sum(ref, keepdims=True)


def square_kernel(start_ref, out_ref):
    squares = fold(start_ref[0] * start_ref[0])
    for s in range(SEC):
        out_ref[s] = squares


def scale_kernel(at_ref, got_ref, start_ref, copies_ref, sums_ref, start_half_ref, norm_ref):
    squares = got_ref[0]
    for s in range(1, SEC):
        squares = squares + got_ref[s]
    mean_sq = total_of(squares) / ENTRIES
    scale = 1.0 / jnp.sqrt(mean_sq + 1e-06)
    norm_ref[0] = jnp.broadcast_to(scale, (8, LANES))
    norm_ref[1] = jnp.broadcast_to(mean_sq, (8, LANES))
    start = start_ref[0, half_rows(at_ref[0]), :]
    start_half_ref[...] = fold_columns(start)
    vec = start * scale
    rounded = vec.astype(BF16)
    for s in range(SEC):
        copies_ref[s] = rounded
    wide = rounded.astype(F32)
    sums_ref[0] = fold(vec * wide) / CHIPS_X
    sums_ref[1] = fold(wide * wide) / CHIPS_X


def apply_kernel(count_ref, from_ref, to_ref, at_ref, own_ref, other_ref, more_ref, left_ref, right_ref,
                 keep_ref, send_ref, sums_ref, x_ref, acc_ref, send, left, right, term_sems, sems):
    core = at_ref[0]

    def term_copies(i):
        at = pl.ds(i * GROUP, GROUP)
        return (
            pltpu.make_async_copy(left_ref.at[at], left.at[at], term_sems.at[0, i]),
            pltpu.make_async_copy(right_ref.at[at], right.at[at], term_sems.at[1, i]),
        )

    gathers = [
        pltpu.make_async_copy(own_ref, x_ref.at[:, half_rows(core), :], sems.at[0]),
        pltpu.make_async_copy(other_ref, x_ref.at[:, half_rows(1 - core), :], sems.at[1]),
    ]
    for copy in gathers:
        copy.start()
    for i in range(TERMS // GROUP):
        @pl.when(i * GROUP < count_ref[0])
        def _():
            for copy in term_copies(i):
                copy.start()

    @pl.loop(0, SEC)
    def _(s):
        acc_ref[s] = jnp.zeros((B, B), F32)

    for copy in gathers:
        copy.wait()

    def halves(t):
        source, target = from_ref[t], to_ref[t]
        first = dot(left[t], x_ref[source], (1, 0)).astype(BF16)
        second = dot(left[t], x_ref[target], (0, 0)).astype(BF16)
        return t, source, target, first, second

    def add(t, source, target, first, second):
        acc_ref[target] += dot(first, right[t], (1, 1))
        acc_ref[source] += dot(second, right[t], (1, 0))

    @pl.loop(0, TERMS // STEP)
    def _(i):
        live = count_ref[0] - i * STEP
        for k in range(STEP // GROUP):
            @pl.when(live > k * GROUP)
            def _():
                for copy in term_copies(i * (STEP // GROUP) + k):
                    copy.wait()

        @pl.when(live >= STEP)
        def _():
            held = halves(i * STEP)
            for j in range(1, STEP):
                ahead = halves(i * STEP + j)
                add(*held)
                held = ahead
            add(*held)

        @pl.when((live > 0) & (live < STEP))
        def _():
            @pl.loop(0, live)
            def _(j):
                add(*halves(i * STEP + j))

    keep_copy = pltpu.make_async_copy(acc_ref.at[:, half_rows(core), :], keep_ref, sems.at[0])
    keep_copy.start()

    @pl.loop(0, SEC)
    def _(s):
        send[s] = acc_ref[s, half_rows(1 - core), :].astype(BF16)

    send_copy = pltpu.make_async_copy(send, send_ref, sems.at[1])
    send_copy.start()

    def inner(s, total):
        return total + fold(x_ref[s].astype(F32) * acc_ref[s])

    sums_ref[0] = lax.fori_loop(0, SEC, inner, jnp.zeros((8, LANES), F32))
    sums_ref[1:] = more_ref[...]
    keep_copy.wait()
    send_copy.wait()


def join_kernel(keep_ref, got_ref, sums_ref, got_sums_ref, out_ref):
    row = lax.broadcasted_iota(jnp.int32, (SCALARS, LANES), 0)
    lane = lax.broadcasted_iota(jnp.int32, (SCALARS, LANES), 1)
    tile = jnp.zeros((SCALARS, LANES), F32)
    for k in range(sums_ref.shape[0]):
        rest = total_of(sums_ref[k] + got_sums_ref[k])
        for part in range(3):
            top = rest.astype(BF16).astype(F32)
            tile = jnp.where((row == part) & (lane == k), top, tile)
            rest = rest - top
    tile = tile.astype(BF16)

    @pl.loop(0, SEC)
    def _(s):
        block = (keep_ref[s] + got_ref[s].astype(F32)).astype(BF16)
        out_ref[s, :HALF, :] = block[:, :LANES]
        out_ref[s, HALF:B, :] = block[:, LANES:]
        out_ref[s, B:, :] = tile


def sum_kernel(got_ref, out_ref):
    for k in range(0, B, HALF):
        total = got_ref[0, k:k + HALF, :].astype(F32)
        for s in range(1, SEC):
            total = total + got_ref[s, k:k + HALF, :].astype(F32)
        for x in range(CHIPS_X):
            out_ref[x, k:k + HALF, :] = total
    tile = got_ref[0, B:, :].astype(F32)
    for s in range(1, SEC):
        tile = tile + got_ref[s, B:, :].astype(F32)
    tile = tile[:8, :] + tile[8:, :]
    for x in range(CHIPS_X):
        out_ref[x, B:, :] = tile


def sum_of_chips(got_ref, scalars):
    total = got_ref[0]
    for x in range(1, CHIPS_X):
        total = total + got_ref[x]
    tile = total[B:, :]
    lane = lax.broadcasted_iota(jnp.int32, tile.shape, 1)
    means = [total_of(jnp.where(lane == k, tile, 0.0)) / ENTRIES for k in range(scalars)]
    return total[:B, :], means


def ratio(whole, part):
    return jnp.where(part > 0.0, whole / jnp.where(part > 0.0, part, 1.0), 1.0)


def correct_kernel(at_ref, got_ref, start_ref, diag_ref, norm_ref, copies_ref, sums_ref, corr_ref, sigma_ref, theta_ref):
    sigma, (theta, vec_round, round_sq) = sum_of_chips(got_ref, 3)
    theta = theta * ratio(vec_round, round_sq)
    vec = start_ref[...] * norm_ref[0, :1, :1]
    diag = fold_columns(diag_ref[0, half_rows(at_ref[0]), :])
    corr = (sigma - theta * vec) / jnp.maximum(jnp.abs(diag - theta), 1.0)
    sigma_ref[...] = sigma
    corr_ref[...] = corr
    theta_ref[...] = jnp.broadcast_to(theta, theta_ref.shape)
    rounded = corr.astype(BF16)
    for s in range(SEC):
        store_half(copies_ref, s, rounded)
    wide = rounded.astype(F32)
    pairs = ((vec, corr), (corr, corr), (sigma, corr), (corr, wide), (wide, wide))
    for k, (one, two) in enumerate(pairs):
        sums_ref[k] = fold(one * two) / CHIPS_X


def ritz_kernel(got_ref, start_ref, norm_ref, corr_ref, sigma_ref, theta_ref, out_ref):
    h_corr, (quad, along, corr_sq, cross, corr_round, round_sq) = sum_of_chips(got_ref, 6)
    theta, scale, mean_sq = theta_ref[:1, :1], norm_ref[0, :1, :1], norm_ref[1, :1, :1]
    quad = quad * ratio(corr_round, round_sq)
    vec_sq = mean_sq * scale * scale
    ortho_sq = jnp.maximum(corr_sq - along * along * (2.0 - vec_sq), 0.0)
    inv = 1.0 / jnp.sqrt(ortho_sq + 1e-06)
    beta = (cross - along * theta) * inv
    gamma = (quad - 2.0 * along * cross + along * along * theta) * inv * inv
    lowest = 0.5 * (theta + gamma) - jnp.sqrt((0.5 * (theta - gamma)) ** 2 + beta * beta)
    norm = jnp.sqrt(beta * beta + (lowest - theta) ** 2)
    one, two = beta / norm, (lowest - theta) / norm
    vec, sigma = start_ref[...] * scale, sigma_ref[...]
    vec_two, sigma_two = (corr_ref[...] - along * vec) * inv, (h_corr - along * sigma) * inv
    ritz = one * vec + two * vec_two
    store_half(out_ref, 0, ritz)
    store_half(out_ref, 1, one * sigma + two * sigma_two - lowest * ritz)


def place_kernel(at_ref, own_ref, other_ref, vector_ref, residual_ref):
    core = at_ref[0]
    for k, ref in enumerate((vector_ref, residual_ref)):
        ref[0, half_rows(core), :] = own_ref[k]
        ref[0, half_rows(1 - core), :] = other_ref[k]


def shape(*dims, dtype=F32):
    return jax.ShapeDtypeStruct(dims, dtype)


SMEM = pl.BlockSpec(memory_space=pltpu.SMEM)
WHOLE = pl.BlockSpec(memory_space=pltpu.VMEM)
ANY = pl.BlockSpec(memory_space=pl.ANY)
GATHER = shape(SEC, HALF, B, dtype=BF16)
COLUMNS = shape(B, LANES)


def call(kernel, mib, ins, outs, *args, **kwargs):
    return pl.pallas_call(
        kernel,
        out_shape=outs,
        in_specs=ins,
        compiler_params=pltpu.CompilerParams(vmem_limit_bytes=mib << 20),
        name=kernel.__name__,
        **kwargs,
    )(*args)


def swap(x):
    return lax.ppermute(x, "op", CORE_SWAP)


def over_sectors(x):
    return lax.all_to_all(x, "sec", 0, 0, tiled=True)


def apply_ham(terms, copies, more, left_env, right_env):
    own = over_sectors(copies)
    keep, send, sums = call(
        apply_kernel,
        58,
        [SMEM] * 4 + [ANY] * 2 + [WHOLE] + [ANY] * 2,
        [shape(SEC, HALF, B), GATHER, shape(more.shape[0] + 1, 8, LANES)],
        *terms, own, swap(own), more, left_env, right_env,
        out_specs=[ANY] * 2 + [WHOLE],
        scratch_shapes=[
            pltpu.VMEM((SEC, B, B), BF16),
            pltpu.VMEM((SEC, B, B), F32),
            pltpu.VMEM((SEC, HALF, B), BF16),
            pltpu.VMEM((TERMS, B, B), BF16),
            pltpu.VMEM((TERMS, B, B), BF16),
            pltpu.SemaphoreType.DMA((2, TERMS // GROUP)),
            pltpu.SemaphoreType.DMA((2,)),
        ],
    )
    payload = call(
        join_kernel, 16, [WHOLE] * 4, shape(SEC, B + SCALARS, LANES, dtype=BF16),
        keep, swap(send), sums, swap(sums),
    )
    chips = call(sum_kernel, 16, [WHOLE], shape(CHIPS_X, B + 8, LANES), over_sectors(payload))
    return lax.all_to_all(chips, "op", 0, 0, tiled=True, axis_index_groups=ALONG_X)


def per_device(start_vector, diag_guess, left_env, right_env, sector_from, sector_to, term_count):
    at = (lax.axis_index("op") % 2).astype(jnp.int32).reshape(1)
    terms = (term_count, sector_from, sector_to, at)
    squares = call(square_kernel, 16, [WHOLE], shape(SEC, 8, LANES), start_vector)
    copies, more, start, norm = call(
        scale_kernel, 16, [SMEM] + [WHOLE] * 2,
        [GATHER, shape(2, 8, LANES), COLUMNS, shape(2, 8, LANES)],
        at, over_sectors(squares), start_vector,
    )
    got = apply_ham(terms, copies, more, left_env, right_env)
    copies, more, corr, sigma, theta = call(
        correct_kernel, 16, [SMEM] + [WHOLE] * 4,
        [GATHER, shape(5, 8, LANES), COLUMNS, COLUMNS, shape(8, LANES)],
        at, got, start, diag_guess, norm,
    )
    got = apply_ham(terms, copies, more, left_env, right_env)
    halves = call(ritz_kernel, 16, [WHOLE] * 6, shape(2, HALF, B), got, start, norm, corr, sigma, theta)
    return call(
        place_kernel, 16, [SMEM] + [WHOLE] * 2, [shape(1, B, B), shape(1, B, B)], at, halves, swap(halves)
    )


def solution(mesh):
    return jax.shard_map(
        per_device,
        mesh=mesh,
        in_specs=(
            P("sec", None, None),
            P("sec", None, None),
            P(("op", "sec"), None, None),
            P(("op", "sec"), None, None),
            P(("op", "sec")),
            P(("op", "sec")),
            P(("op", "sec")),
        ),
        out_specs=(P("sec", None, None), P("sec", None, None)),
        check_vma=False,
    )
```

time: 2160 us -> 187 us (0.09)
  matrix products: 722 us -> 0 us
  loops' own time: 577 us -> 0 us
  waiting for transfers between devices: 384 us -> 16.4 us
  local copies, waits for them, and re-layouts: 161 us -> 8.47 us
  other arithmetic: 111 us -> 0 us
  blocking collectives: 164 us -> 112 us
  Pallas kernels: 0 us -> 28.2 us
    dot_general x256 -> x0, matrix products: 722 us -> none  [the longest x128 364 us: add_term(): backward = jnp.dot(second, right_block, preferred_element_type=jnp.float32)]
    another operation x2 -> x0, loops' own time: 577 us -> none  [apply_ham(): lax.fori_loop(0, live_terms, add_term, jnp.zeros(blocks.shape, jnp.float32))]
    psum x5 -> x0, blocking collectives: 164 us -> none  [the longest x1 36.1 us: per_device(): start_sq = lax.psum(jnp.sum(start_vector * start_vector), 'sec') / entries]
    dynamic_slice x256 -> x0, local copies, waits for them, and re-layouts: 156 us -> none  [the longest x128 81 us: add_term(): source = sector_from[term_index]]
    unnamed x8 -> x0, waiting for transfers between devices: 153 us -> none
    psum x2 -> x0, waiting for transfers between devices: 122 us -> none  [apply_ham(): return lax.psum(owned, 'op')]
    all_to_all x0 -> x6, blocking collectives: none -> 112 us  [the longest x4 88.4 us: over_sectors(): return lax.all_to_all(x, 'sec', 0, 0, tiled=True)]
    all_gather x2 -> x0, waiting for transfers between devices: 109 us -> none  [apply_ham(): lax.all_gather(vector.astype(jnp.bfloat16), 'sec', axis=0, tiled=True)]
  transfers between devices with their start and end apart: 6 -> 8, of which waited for: 6 -> 6; matrix products, arithmetic and copies ran while one was open for 0% -> 0% of each run, Pallas kernels for 0% -> 0%
where the time goes in v3:
time: 187 us; the launch traced here: 186 us
  blocking collectives  112 us (60%)
  Pallas kernels  28.2 us (15%)
  starting transfers between devices  19.7 us (11%)
  waiting for transfers between devices  16.4 us (9%)
  local copies, waits for them, and re-layouts  8.47 us (5%)
    all_to_all x4, blocking collectives, over_sectors(): return lax.all_to_all(x, 'sec', 0, 0, tiled=True)  88.4 us
    pallas_call x11, Pallas kernels, call(): pl.pallas_call(kernel, out_shape=outs, in_specs=ins, compiler_params=pltp...  28.2 us
    all_to_all x2, blocking collectives, apply_ham(): lax.all_to_all(chips, 'op', 0, 0, tiled=True, axis_index_groups=ALONG_X)  23.5 us
    ppermute x7, starting transfers between devices, swap(): return lax.ppermute(x, 'op', CORE_SWAP)  11.1 us
    ppermute x7, waiting for transfers between devices, swap(): return lax.ppermute(x, 'op', CORE_SWAP)  9.86 us
    all_to_all x1, starting transfers between devices, over_sectors(): return lax.all_to_all(x, 'sec', 0, 0, tiled=True)  8.6 us
    unnamed x26, local copies, waits for them, and re-layouts  8.47 us
    all_to_all x1, waiting for transfers between devices, over_sectors(): return lax.all_to_all(x, 'sec', 0, 0, tiled=True)  6.51 us
  transfers between devices with their start and end apart: 8, of which 6 were waited for; matrix products, arithmetic and copies ran while one was open for 0% of the time, Pallas kernels for 0%

profile of v3, /device:TPU:1, one launch (start us, length us, event | category | flops | bytes accessed | tf_op | source)
XLA Modules:
  0.0 186.1 jit_solution(7502575389700020309)
XLA Ops:
  0.6 0.9 copy-done.2
  1.6 0.7 square_kernel.1
  2.3 8.6 %all-to-all-start = ((f32[16,8,128]{2,1,0:T(8,128)}), f32[16,8,128]{2,1,0:T(8,128)S(1)}, u32[]{:S(2)}, u32[]{:S(2)}) async-start(f32[16,8,128]{2,1,0:T(8,128)} %square_kernel.1), calls=%async_computation | async-start | bytes 131072 | tf_op jit(solution)/shard_map/all_to_all | solution.py:273
  10.9 6.5 %all-to-all-done.got_ref = f32[16,8,128]{2,1,0:T(8,128)S(1)} async-done(((f32[16,8,128]{2,1,0:T(8,128)}), f32[16,8,128]{2,1,0:T(8,128)S(1)}, u32[]{:S(2)}, u32[]{:S(2)}) %all-to-all-start) | async-done | bytes 65568 | tf_op jit(solution)/shard_map/all_to_all | solution.py:273
  17.4 0.9 copy-done.3
  18.6 18.5 %all_to_all.35.own_ref = bf16[16,128,256]{2,1,0:T(8,128)(2,1)S(1)} all-to-all(bf16[16,128,256]{2,1,0:T(8,128)(2,1)S(1)} %get-tuple-element.17), channel_id=1, replica_groups=mesh['op'=8,'sec'=16] {'sec'}, dimensions={0} | all-to-all | bytes 2097152 | tf_op jit(solution)/shard_map/all_to_all | solution.py:273
  37.1 3.0 %collective-permute-start = (bf16[16,128,256]{2,1,0:T(8,128)(2,1)S(1)}, bf16[16,128,256]{2,1,0:T(8,128)(2,1)S(1)}, u32[]{:S(2)}, u32[]{:S(2)}) collective-permute-start(bf16[16,128,256]{2,1,0:T(8,128)(2,1)S(1)} %all_to_all.35.own_ref), channel_id=1, source_target_pairs={{0,16},{16,0},{32,48},{48,32},{64,80},{80,64},{96,112},{112,96},{1... | collective-permute-start | bytes 3145736 | tf_op jit(solution)/shard_map/ppermute | solution.py:269
  40.7 1.6 collective-permute-done.other_ref
  42.4 1.0 copy-done.11
  43.3 12.3 %apply_kernel.2 = (f32[16,128,256]{2,1,0:T(8,128)}, bf16[16,128,256]{2,1,0:T(8,128)(2,1)}, f32[3,8,128]{2,1,0:T(8,128)}) custom-call(s32[1]{0:T(128)S(6)} %copy.9.count_ref, s32[64]{0:T(128)} %from_ref.3, s32[64]{0:T(128)} %to_ref.3, s32[1]{0:T(128)} %bitcast.at_ref, bf16[16,128,256]{2,1,0:T(8,128)(2,1)} %copy-done.9, bf16[16,128,256]{2,1,0:T(8,128)(2,1)} %copy-done.11, ...), custom_call_target="tpu_custom_call" | custom-call | tf_op jit(solution)/shard_map/apply_kernel/pallas_call | solution.py:258
  55.7 0.5 collective-permute-start.2
  56.2 2.4 %collective-permute-done.2.got_sums_ref = f32[3,8,128]{2,1,0:T(8,128)S(1)} collective-permute-done((f32[3,8,128]{2,1,0:T(8,128)}, f32[3,8,128]{2,1,0:T(8,128)S(1)}, u32[]{:S(2)}, u32[]{:S(2)}) %collective-permute-start.2) | collective-permute-done | bytes 12320 | tf_op jit(solution)/shard_map/ppermute | solution.py:269
  58.6 1.6 copy-done.1
  60.2 0.7 copy-done.7
  60.9 0.4 join_kernel.2
  61.4 26.6 %all_to_all.36.got_ref = bf16[16,272,128]{2,1,0:T(8,128)(2,1)S(1)} all-to-all(bf16[16,272,128]{2,1,0:T(8,128)(2,1)S(1)} %join_kernel.2), channel_id=1, replica_groups=mesh['op'=8,'sec'=16] {'sec'}, dimensions={0} | all-to-all | bytes 2228224 | tf_op jit(solution)/shard_map/all_to_all | solution.py:273
  88.1 12.7 %all_to_all.37.got_ref = f32[4,264,128]{2,1,0:T(8,128)S(1)} all-to-all(f32[4,264,128]{2,1,0:T(8,128)S(1)} %sum_kernel.2), channel_id=1, replica_groups={{0,32,64,96},{16,48,80,112},{1,33,65,97},{17,49,81,113},{2,34,66,98},{1..., dimensions={0} | all-to-all | bytes 1081344 | tf_op jit(solution)/shard_map/all_to_all | solution.py:300
  100.8 0.4 correct_kernel.1
  101.2 16.8 %all_to_all.38.own_ref = bf16[16,128,256]{2,1,0:T(8,128)(2,1)S(1)} all-to-all(bf16[16,128,256]{2,1,0:T(8,128)(2,1)S(1)} %get-tuple-element.24), channel_id=1, replica_groups=mesh['op'=8,'sec'=16] {'sec'}, dimensions={0} | all-to-all | bytes 2097152 | tf_op jit(solution)/shard_map/all_to_all | solution.py:273
  118.0 4.2 %collective-permute-start.3 = (bf16[16,128,256]{2,1,0:T(8,128)(2,1)S(1)}, bf16[16,128,256]{2,1,0:T(8,128)(2,1)S(1)}, u32[]{:S(2)}, u32[]{:S(2)}) collective-permute-start(bf16[16,128,256]{2,1,0:T(8,128)(2,1)S(1)} %all_to_all.38.own_ref), channel_id=1, source_target_pairs={{0,16},{16,0},{32,48},{48,32},{64,80},{80,64},{96,112},{112,96},{1... | collective-permute-start | bytes 3145736 | tf_op jit(solution)/shard_map/ppermute | solution.py:269
  122.2 2.3 %collective-permute-done.3.other_ref = bf16[16,128,256]{2,1,0:T(8,128)(2,1)S(1)} collective-permute-done((bf16[16,128,256]{2,1,0:T(8,128)(2,1)S(1)}, bf16[16,128,256]{2,1,0:T(8,128)(2,1)S(1)}, u32[]{:S(2)}, u32[]{:S(2)}) %collective-permute-start.3) | collective-permute-done | bytes 1048608 | tf_op jit(solution)/shard_map/ppermute | solution.py:269
  124.5 1.0 copy-done.12
  125.5 12.3 %apply_kernel.3 = (f32[16,128,256]{2,1,0:T(8,128)}, bf16[16,128,256]{2,1,0:T(8,128)(2,1)}, f32[6,8,128]{2,1,0:T(8,128)}) custom-call(s32[1]{0:T(128)S(6)} %copy.9.count_ref, s32[64]{0:T(128)} %from_ref.3, s32[64]{0:T(128)} %to_ref.3, s32[1]{0:T(128)} %bitcast.at_ref, bf16[16,128,256]{2,1,0:T(8,128)(2,1)} %copy-done.10, bf16[16,128,256]{2,1,0:T(8,128)(2,1)} %copy-done.12, ...), custom_call_target="tpu_custom_call" | custom-call | tf_op jit(solution)/shard_map/apply_kernel/pallas_call | solution.py:258
  137.9 0.5 collective-permute-start.5
  138.4 2.4 %collective-permute-done.5.got_sums_ref = f32[6,8,128]{2,1,0:T(8,128)S(1)} collective-permute-done((f32[6,8,128]{2,1,0:T(8,128)}, f32[6,8,128]{2,1,0:T(8,128)S(1)}, u32[]{:S(2)}, u32[]{:S(2)}) %collective-permute-start.5) | collective-permute-done | bytes 24608 | tf_op jit(solution)/shard_map/ppermute | solution.py:269
  140.8 1.6 copy-done
  142.4 0.7 copy-done.5
  143.5 26.5 %all_to_all.39.got_ref = bf16[16,272,128]{2,1,0:T(8,128)(2,1)S(1)} all-to-all(bf16[16,272,128]{2,1,0:T(8,128)(2,1)S(1)} %join_kernel.3), channel_id=1, replica_groups=mesh['op'=8,'sec'=16] {'sec'}, dimensions={0} | all-to-all | bytes 2228224 | tf_op jit(solution)/shard_map/all_to_all | solution.py:273
  170.2 10.9 %all_to_all.40.got_ref = f32[4,264,128]{2,1,0:T(8,128)S(1)} all-to-all(f32[4,264,128]{2,1,0:T(8,128)S(1)} %sum_kernel.3), channel_id=1, replica_groups={{0,32,64,96},{16,48,80,112},{1,33,65,97},{17,49,81,113},{2,34,66,98},{1..., dimensions={0} | all-to-all | bytes 1081344 | tf_op jit(solution)/shard_map/all_to_all | solution.py:300
  181.4 2.8 %collective-permute-start.6 = (f32[2,128,256]{2,1,0:T(8,128)S(1)}, f32[2,128,256]{2,1,0:T(8,128)S(1)}, u32[]{:S(2)}, u32[]{:S(2)}) collective-permute-start(f32[2,128,256]{2,1,0:T(8,128)S(1)} %ritz_kernel.1.own_ref), channel_id=1, source_target_pairs={{0,16},{16,0},{32,48},{48,32},{64,80},{80,64},{96,112},{112,96},{1... | collective-permute-start | bytes 786440 | tf_op jit(solution)/shard_map/ppermute | solution.py:269
  184.1 1.2 collective-permute-done.6.other_ref
  185.3 0.8 place_kernel.1
  (27 shorter events, 1.4 us)
Async XLA Ops:
  0.6 1.0 copy-start.2
  2.3 15.1 %all-to-all-start = ((f32[16,8,128]{2,1,0:T(8,128)}), f32[16,8,128]{2,1,0:T(8,128)S(1)}, u32[]{:S(2)}, u32[]{:S(2)}) async-start(f32[16,8,128]{2,1,0:T(8,128)} %square_kernel.1), calls=%async_computation | async-start | bytes 131072 | tf_op jit(solution)/shard_map/all_to_all | solution.py:273
  17.4 1.0 copy-start.3
  18.6 18.5 %copy-start.8 = (f32[2,8,128]{2,1,0:T(8,128)}, f32[2,8,128]{2,1,0:T(8,128)S(1)}, u32[]{:S(2)}) copy-start(f32[2,8,128]{2,1,0:T(8,128)S(1)} %get-tuple-element.18.more_ref) | copy-start | bytes 24580
  37.1 5.3 %copy-start.9 = (bf16[16,128,256]{2,1,0:T(8,128)(2,1)}, bf16[16,128,256]{2,1,0:T(8,128)(2,1)S(1)}, u32[]{:S(2)}) copy-start(bf16[16,128,256]{2,1,0:T(8,128)(2,1)S(1)} %all_to_all.35.own_ref) | copy-start | bytes 3145732
  37.1 5.3 %collective-permute-start = (bf16[16,128,256]{2,1,0:T(8,128)(2,1)S(1)}, bf16[16,128,256]{2,1,0:T(8,128)(2,1)S(1)}, u32[]{:S(2)}, u32[]{:S(2)}) collective-permute-start(bf16[16,128,256]{2,1,0:T(8,128)(2,1)S(1)} %all_to_all.35.own_ref), channel_id=1, source_target_pairs={{0,16},{16,0},{32,48},{48,32},{64,80},{80,64},{96,112},{112,96},{1... | collective-permute-start | bytes 3145736 | tf_op jit(solution)/shard_map/ppermute | solution.py:269
  42.4 1.0 copy-start.11
  55.6 3.0 %collective-permute-start.1 = (bf16[16,128,256]{2,1,0:T(8,128)(2,1)}, bf16[16,128,256]{2,1,0:T(8,128)(2,1)S(1)}, u32[]{:S(2)}, u32[]{:S(2)}) collective-permute-start(bf16[16,128,256]{2,1,0:T(8,128)(2,1)} %get-tuple-element.20), channel_id=1, source_target_pairs={{0,16},{16,0},{32,48},{48,32},{64,80},{80,64},{96,112},{112,96},{1... | collective-permute-start | bytes 3145736 | tf_op jit(solution)/shard_map/ppermute | solution.py:269
  55.7 2.9 %collective-permute-start.2 = (f32[3,8,128]{2,1,0:T(8,128)}, f32[3,8,128]{2,1,0:T(8,128)S(1)}, u32[]{:S(2)}, u32[]{:S(2)}) collective-permute-start(f32[3,8,128]{2,1,0:T(8,128)} %get-tuple-element.21.sums_ref), channel_id=1, source_target_pairs={{0,16},{16,0},{32,48},{48,32},{64,80},{80,64},{96,112},{112,96},{1... | collective-permute-start | bytes 36872 | tf_op jit(solution)/shard_map/ppermute | solution.py:269
  58.6 1.6 copy-start.1
  60.2 0.7 copy-start.7
  61.4 39.4 %copy-start.4 = (f32[1,256,256]{2,1,0:T(8,128)S(1)}, f32[1,256,256]{2,1,0:T(8,128)}, u32[]{:S(2)}) copy-start(f32[1,256,256]{2,1,0:T(8,128)} %diag_ref.1) | copy-start | bytes 786436
  101.2 16.8 %copy-start.6 = (f32[5,8,128]{2,1,0:T(8,128)}, f32[5,8,128]{2,1,0:T(8,128)S(1)}, u32[]{:S(2)}) copy-start(f32[5,8,128]{2,1,0:T(8,128)S(1)} %get-tuple-element.25.more_ref) | copy-start | bytes 61444
  118.0 6.5 %copy-start.10 = (bf16[16,128,256]{2,1,0:T(8,128)(2,1)}, bf16[16,128,256]{2,1,0:T(8,128)(2,1)S(1)}, u32[]{:S(2)}) copy-start(bf16[16,128,256]{2,1,0:T(8,128)(2,1)S(1)} %all_to_all.38.own_ref) | copy-start | bytes 3145732
  118.0 6.5 %collective-permute-start.3 = (bf16[16,128,256]{2,1,0:T(8,128)(2,1)S(1)}, bf16[16,128,256]{2,1,0:T(8,128)(2,1)S(1)}, u32[]{:S(2)}, u32[]{:S(2)}) collective-permute-start(bf16[16,128,256]{2,1,0:T(8,128)(2,1)S(1)} %all_to_all.38.own_ref), channel_id=1, source_target_pairs={{0,16},{16,0},{32,48},{48,32},{64,80},{80,64},{96,112},{112,96},{1... | collective-permute-start | bytes 3145736 | tf_op jit(solution)/shard_map/ppermute | solution.py:269
  124.5 1.0 copy-start.12
  137.8 3.0 %collective-permute-start.4 = (bf16[16,128,256]{2,1,0:T(8,128)(2,1)}, bf16[16,128,256]{2,1,0:T(8,128)(2,1)S(1)}, u32[]{:S(2)}, u32[]{:S(2)}) collective-permute-start(bf16[16,128,256]{2,1,0:T(8,128)(2,1)} %get-tuple-element.27), channel_id=1, source_target_pairs={{0,16},{16,0},{32,48},{48,32},{64,80},{80,64},{96,112},{112,96},{1... | collective-permute-start | bytes 3145736 | tf_op jit(solution)/shard_map/ppermute | solution.py:269
  137.9 2.9 %collective-permute-start.5 = (f32[6,8,128]{2,1,0:T(8,128)}, f32[6,8,128]{2,1,0:T(8,128)S(1)}, u32[]{:S(2)}, u32[]{:S(2)}) collective-permute-start(f32[6,8,128]{2,1,0:T(8,128)} %get-tuple-element.28.sums_ref), channel_id=1, source_target_pairs={{0,16},{16,0},{32,48},{48,32},{64,80},{80,64},{96,112},{112,96},{1... | collective-permute-start | bytes 73736 | tf_op jit(solution)/shard_map/ppermute | solution.py:269
  140.8 1.6 copy-start
  142.4 0.7 copy-start.5
  181.4 3.9 %collective-permute-start.6 = (f32[2,128,256]{2,1,0:T(8,128)S(1)}, f32[2,128,256]{2,1,0:T(8,128)S(1)}, u32[]{:S(2)}, u32[]{:S(2)}) collective-permute-start(f32[2,128,256]{2,1,0:T(8,128)S(1)} %ritz_kernel.1.own_ref), channel_id=1, source_target_pairs={{0,16},{16,0},{32,48},{48,32},{64,80},{80,64},{96,112},{112,96},{1... | collective-permute-start | bytes 786440 | tf_op jit(solution)/shard_map/ppermute | solution.py:269

commit v4 on v3

--- a/solution.py
+++ b/solution.py
@@ -9,10 +9,10 @@
 SEC, B, LANES = 16, 256, 128
 HALF = B // 2
 CHIPS_X, N_OP = 4, 8
-TERMS, GROUP, STEP = 64, 8, 16
+TERMS, GROUP, STEP, AHEAD = 64, 8, 16, 3
 ENTRIES = SEC * B * B
 CORE_SWAP = [(i, i ^ 1) for i in range(N_OP)]
-ALONG_X = [[2 * x + core for x in range(CHIPS_X)] for core in range(2)]
+ALONG_X = [[(i, (i + 2 * hops) % N_OP) for i in range(N_OP)] for hops in range(1, CHIPS_X)]
 SCALARS = 16
 
 
@@ -42,13 +42,14 @@
     return jnp.sum(ref, keepdims=True)
 
 
-def square_kernel(start_ref, out_ref):
+def square_kernel(at_ref, start_ref, out_ref, half_ref):
     squares = fold(start_ref[0] * start_ref[0])
     for s in range(SEC):
         out_ref[s] = squares
-
-
-def scale_kernel(at_ref, got_ref, start_ref, copies_ref, sums_ref, start_half_ref, norm_ref):
+    half_ref[...] = start_ref[0, half_rows(at_ref[0]), :]
+
+
+def scale_kernel(got_ref, start_ref, copies_ref, sums_ref, start_half_ref, norm_ref):
     squares = got_ref[0]
     for s in range(1, SEC):
         squares = squares + got_ref[s]
@@ -56,7 +57,7 @@
     scale = 1.0 / jnp.sqrt(mean_sq + 1e-06)
     norm_ref[0] = jnp.broadcast_to(scale, (8, LANES))
     norm_ref[1] = jnp.broadcast_to(mean_sq, (8, LANES))
-    start = start_ref[0, half_rows(at_ref[0]), :]
+    start = start_ref[...]
     start_half_ref[...] = fold_columns(start)
     vec = start * scale
     rounded = vec.astype(BF16)
@@ -68,15 +69,24 @@
 
 
 def apply_kernel(count_ref, from_ref, to_ref, at_ref, own_ref, other_ref, more_ref, left_ref, right_ref,
-                 keep_ref, send_ref, sums_ref, x_ref, acc_ref, send, left, right, term_sems, sems):
+                 keep_ref, send_ref, sums_ref, *rest):
     core = at_ref[0]
+    fetched = len(rest) > 4
+    left, right = rest[:2] if fetched else (left_ref, right_ref)
+    x_ref, acc_ref, send, sems = rest[2:6] if fetched else rest
 
     def term_copies(i):
         at = pl.ds(i * GROUP, GROUP)
-        return (
-            pltpu.make_async_copy(left_ref.at[at], left.at[at], term_sems.at[0, i]),
-            pltpu.make_async_copy(right_ref.at[at], right.at[at], term_sems.at[1, i]),
-        )
+        return [
+            pltpu.make_async_copy(ref.at[at], held.at[at], rest[6].at[k, i])
+            for k, (ref, held) in enumerate(((left_ref, left), (right_ref, right)))
+        ]
+
+    def fetch(i):
+        @pl.when((i < TERMS // GROUP) & (i * GROUP < count_ref[0]))
+        def _():
+            for copy in term_copies(i):
+                copy.start()
 
     gathers = [
         pltpu.make_async_copy(own_ref, x_ref.at[:, half_rows(core), :], sems.at[0]),
@@ -84,11 +94,9 @@
     ]
     for copy in gathers:
         copy.start()
-    for i in range(TERMS // GROUP):
-        @pl.when(i * GROUP < count_ref[0])
-        def _():
-            for copy in term_copies(i):
-                copy.start()
+    if fetched:
+        for i in range(AHEAD):
+            fetch(i)
 
     @pl.loop(0, SEC)
     def _(s):
@@ -110,11 +118,13 @@
     @pl.loop(0, TERMS // STEP)
     def _(i):
         live = count_ref[0] - i * STEP
-        for k in range(STEP // GROUP):
+        for k in range(STEP // GROUP if fetched else 0):
             @pl.when(live > k * GROUP)
             def _():
                 for copy in term_copies(i * (STEP // GROUP) + k):
                     copy.wait()
+
+            fetch(i * (STEP // GROUP) + k + AHEAD)
 
         @pl.when(live >= STEP)
         def _():
@@ -175,20 +185,16 @@
         total = got_ref[0, k:k + HALF, :].astype(F32)
         for s in range(1, SEC):
             total = total + got_ref[s, k:k + HALF, :].astype(F32)
-        for x in range(CHIPS_X):
-            out_ref[x, k:k + HALF, :] = total
+        out_ref[k:k + HALF, :] = total
     tile = got_ref[0, B:, :].astype(F32)
     for s in range(1, SEC):
         tile = tile + got_ref[s, B:, :].astype(F32)
-    tile = tile[:8, :] + tile[8:, :]
-    for x in range(CHIPS_X):
-        out_ref[x, B:, :] = tile
-
-
-def sum_of_chips(got_ref, scalars):
-    total = got_ref[0]
-    for x in range(1, CHIPS_X):
-        total = total + got_ref[x]
+    out_ref[B:, :] = tile[:8, :] + tile[8:, :]
+
+
+def sum_of_chips(part_refs, scalars):
+    own, near, across, far = (ref[...] for ref in part_refs)
+    total = (own + across) + (near + far)
     tile = total[B:, :]
     lane = lax.broadcasted_iota(jnp.int32, tile.shape, 1)
     means = [total_of(jnp.where(lane == k, tile, 0.0)) / ENTRIES for k in range(scalars)]
@@ -199,8 +205,8 @@
     return jnp.where(part > 0.0, whole / jnp.where(part > 0.0, part, 1.0), 1.0)
 
 
-def correct_kernel(at_ref, got_ref, start_ref, diag_ref, norm_ref, copies_ref, sums_ref, corr_ref, sigma_ref, theta_ref):
-    sigma, (theta, vec_round, round_sq) = sum_of_chips(got_ref, 3)
+def correct_kernel(at_ref, own_ref, near_ref, across_ref, far_ref, start_ref, diag_ref, norm_ref, copies_ref, sums_ref, corr_ref, sigma_ref, theta_ref):
+    sigma, (theta, vec_round, round_sq) = sum_of_chips((own_ref, near_ref, across_ref, far_ref), 3)
     theta = theta * ratio(vec_round, round_sq)
     vec = start_ref[...] * norm_ref[0, :1, :1]
     diag = fold_columns(diag_ref[0, half_rows(at_ref[0]), :])
@@ -217,8 +223,8 @@
         sums_ref[k] = fold(one * two) / CHIPS_X
 
 
-def ritz_kernel(got_ref, start_ref, norm_ref, corr_ref, sigma_ref, theta_ref, out_ref):
-    h_corr, (quad, along, corr_sq, cross, corr_round, round_sq) = sum_of_chips(got_ref, 6)
+def ritz_kernel(own_ref, near_ref, across_ref, far_ref, start_ref, norm_ref, corr_ref, sigma_ref, theta_ref, out_ref):
+    h_corr, (quad, along, corr_sq, cross, corr_round, round_sq) = sum_of_chips((own_ref, near_ref, across_ref, far_ref), 6)
     theta, scale, mean_sq = theta_ref[:1, :1], norm_ref[0, :1, :1], norm_ref[1, :1, :1]
     quad = quad * ratio(corr_round, round_sq)
     vec_sq = mean_sq * scale * scale
@@ -273,50 +279,55 @@
     return lax.all_to_all(x, "sec", 0, 0, tiled=True)
 
 
-def apply_ham(terms, copies, more, left_env, right_env):
-    own = over_sectors(copies)
-    keep, send, sums = call(
+def apply_call(terms, own, other, more, left_env, right_env, fetch):
+    if fetch:
+        left_env, right_env = (pltpu.with_memory_space_constraint(x, pltpu.HBM) for x in (left_env, right_env))
+    return call(
         apply_kernel,
-        58,
-        [SMEM] * 4 + [ANY] * 2 + [WHOLE] + [ANY] * 2,
-        [shape(SEC, HALF, B), GATHER, shape(more.shape[0] + 1, 8, LANES)],
-        *terms, own, swap(own), more, left_env, right_env,
-        out_specs=[ANY] * 2 + [WHOLE],
+        28,
+        [SMEM] * 4 + [ANY] * 2 + [WHOLE] + [ANY if fetch else WHOLE] * 2,
+        [shape(SEC, HALF, B), GATHER, shape(more.shape[0] + 1, 8, LANES)] + [shape(TERMS, B, B, dtype=BF16)] * (2 * fetch),
+        *terms, own, other, more, left_env, right_env,
+        out_specs=[ANY] * 2 + [WHOLE] * (3 if fetch else 1),
         scratch_shapes=[
             pltpu.VMEM((SEC, B, B), BF16),
             pltpu.VMEM((SEC, B, B), F32),
             pltpu.VMEM((SEC, HALF, B), BF16),
-            pltpu.VMEM((TERMS, B, B), BF16),
-            pltpu.VMEM((TERMS, B, B), BF16),
-            pltpu.SemaphoreType.DMA((2, TERMS // GROUP)),
             pltpu.SemaphoreType.DMA((2,)),
-        ],
-    )
+        ] + [pltpu.SemaphoreType.DMA((2, TERMS // GROUP))] * fetch,
+    )
+
+
+def apply_ham(terms, copies, more, left_env, right_env, fetch):
+    own = over_sectors(copies)
+    keep, send, sums, *held = apply_call(terms, own, swap(own), more, left_env, right_env, fetch)
     payload = call(
         join_kernel, 16, [WHOLE] * 4, shape(SEC, B + SCALARS, LANES, dtype=BF16),
         keep, swap(send), sums, swap(sums),
     )
-    chips = call(sum_kernel, 16, [WHOLE], shape(CHIPS_X, B + 8, LANES), over_sectors(payload))
-    return lax.all_to_all(chips, "op", 0, 0, tiled=True, axis_index_groups=ALONG_X)
+    part = call(sum_kernel, 16, [WHOLE], shape(B + 8, LANES), over_sectors(payload))
+    return (part, *(lax.ppermute(part, "op", perm) for perm in ALONG_X)), held
 
 
 def per_device(start_vector, diag_guess, left_env, right_env, sector_from, sector_to, term_count):
     at = (lax.axis_index("op") % 2).astype(jnp.int32).reshape(1)
     terms = (term_count, sector_from, sector_to, at)
-    squares = call(square_kernel, 16, [WHOLE], shape(SEC, 8, LANES), start_vector)
+    squares, half = call(
+        square_kernel, 16, [SMEM, WHOLE], [shape(SEC, 8, LANES), shape(HALF, B)], at, start_vector
+    )
     copies, more, start, norm = call(
-        scale_kernel, 16, [SMEM] + [WHOLE] * 2,
+        scale_kernel, 16, [WHOLE] * 2,
         [GATHER, shape(2, 8, LANES), COLUMNS, shape(2, 8, LANES)],
-        at, over_sectors(squares), start_vector,
-    )
-    got = apply_ham(terms, copies, more, left_env, right_env)
+        over_sectors(squares), half,
+    )
+    got, held = apply_ham(terms, copies, more, left_env, right_env, True)
     copies, more, corr, sigma, theta = call(
-        correct_kernel, 16, [SMEM] + [WHOLE] * 4,
+        correct_kernel, 16, [SMEM] + [WHOLE] * 7,
         [GATHER, shape(5, 8, LANES), COLUMNS, COLUMNS, shape(8, LANES)],
-        at, got, start, diag_guess, norm,
-    )
-    got = apply_ham(terms, copies, more, left_env, right_env)
-    halves = call(ritz_kernel, 16, [WHOLE] * 6, shape(2, HALF, B), got, start, norm, corr, sigma, theta)
+        at, *got, start, diag_guess, norm,
+    )
+    got, _ = apply_ham(terms, copies, more, *held, False)
+    halves = call(ritz_kernel, 16, [WHOLE] * 9, shape(2, HALF, B), *got, start, norm, corr, sigma, theta)
     return call(
         place_kernel, 16, [SMEM] + [WHOLE] * 2, [shape(1, B, B), shape(1, B, B)], at, halves, swap(halves)
     )

time: 187 us -> 163 us (0.87)
  blocking collectives: 112 us -> 92.5 us
  Pallas kernels: 28.2 us -> 14.4 us
  waiting for transfers between devices: 16.4 us -> 26 us
  starting transfers between devices: 19.7 us -> 28.1 us
  local copies, waits for them, and re-layouts: 8.47 us -> 0.96 us
    all_to_all x2 -> x0, blocking collectives: 23.5 us -> none  [apply_ham(): lax.all_to_all(chips, 'op', 0, 0, tiled=True, axis_index_groups=ALONG_X)]
    ppermute x0 -> x6, waiting for transfers between devices: none -> 16.4 us  [apply_ham(): return ((part, *(lax.ppermute(part, 'op', perm) for perm in ALONG_X)), held)]
    pallas_call x11, Pallas kernels: 28.2 us -> 14.4 us  [call(): pl.pallas_call(kernel, out_shape=outs, in_specs=ins, compiler_params=pltp...]
    ppermute x7, starting transfers between devices: 11.1 us -> 23.4 us  [swap(): return lax.ppermute(x, 'op', CORE_SWAP)]
    all_to_all x1 -> x0, starting transfers between devices: 8.6 us -> none  [over_sectors(): return lax.all_to_all(x, 'sec', 0, 0, tiled=True)]
    unnamed x26 -> x8, local copies, waits for them, and re-layouts: 8.47 us -> 0.96 us
    all_to_all x1 -> x0, waiting for transfers between devices: 6.51 us -> none  [over_sectors(): return lax.all_to_all(x, 'sec', 0, 0, tiled=True)]
    ppermute x0 -> x6, starting transfers between devices: none -> 4.74 us  [apply_ham(): return ((part, *(lax.ppermute(part, 'op', perm) for perm in ALONG_X)), held)]
  transfers between devices with their start and end apart: 8 -> 13, of which waited for: 6 -> 11; matrix products, arithmetic and copies ran while one was open for 0% -> 0% of each run, Pallas kernels for 0% -> 0%
where the time goes in v4:
time: 163 us
  blocking collectives  92.5 us (57%)
  starting transfers between devices  28.1 us (17%)
  waiting for transfers between devices  26 us (16%)
  Pallas kernels  14.4 us (9%)
    all_to_all x5, blocking collectives, over_sectors(): return lax.all_to_all(x, 'sec', 0, 0, tiled=True)  92.5 us
    ppermute x7, starting transfers between devices, swap(): return lax.ppermute(x, 'op', CORE_SWAP)  23.4 us
    ppermute x6, waiting for transfers between devices, apply_ham(): return ((part, *(lax.ppermute(part, 'op', perm) for perm in ALONG_X)), held)  16.4 us
    pallas_call x11, Pallas kernels, call(): pl.pallas_call(kernel, out_shape=outs, in_specs=ins, compiler_params=pltp...  14.4 us
    ppermute x7, waiting for transfers between devices, swap(): return lax.ppermute(x, 'op', CORE_SWAP)  9.53 us
    ppermute x6, starting transfers between devices, apply_ham(): return ((part, *(lax.ppermute(part, 'op', perm) for perm in ALONG_X)), held)  4.74 us
  transfers between devices with their start and end apart: 13, of which 11 were waited for; matrix products, arithmetic and copies ran while one was open for 0% of the time, Pallas kernels for 0%

profile of v4, /device:TPU:1, one launch (start us, length us, event | category | flops | bytes accessed | tf_op | source)
XLA Modules:
  0.0 163.4 jit_solution(13509638847176729970)
XLA Ops:
  0.7 0.9 copy-done.1
  1.7 14.9 %all_to_all.25.got_ref = f32[16,8,128]{2,1,0:T(8,128)S(1)} all-to-all(f32[16,8,128]{2,1,0:T(8,128)S(1)} %get-tuple-element.21), channel_id=1, replica_groups=mesh['op'=8,'sec'=16] {'sec'}, dimensions={0} | all-to-all | bytes 131072 | tf_op jit(solution)/shard_map/all_to_all | solution.py:279
  16.8 18.5 %all_to_all.26.own_ref = bf16[16,128,256]{2,1,0:T(8,128)(2,1)S(1)} all-to-all(bf16[16,128,256]{2,1,0:T(8,128)(2,1)S(1)} %get-tuple-element.23), channel_id=1, replica_groups=mesh['op'=8,'sec'=16] {'sec'}, dimensions={0} | all-to-all | bytes 2097152 | tf_op jit(solution)/shard_map/all_to_all | solution.py:279
  35.3 3.0 %collective-permute-start = (bf16[16,128,256]{2,1,0:T(8,128)(2,1)S(1)}, bf16[16,128,256]{2,1,0:T(8,128)(2,1)S(1)}, u32[]{:S(2)}, u32[]{:S(2)}) collective-permute-start(bf16[16,128,256]{2,1,0:T(8,128)(2,1)S(1)} %all_to_all.26.own_ref), channel_id=1, source_target_pairs={{0,16},{16,0},{32,48},{48,32},{64,80},{80,64},{96,112},{112,96},{1... | collective-permute-start | bytes 3145736 | tf_op jit(solution)/shard_map/ppermute | solution.py:275
  39.0 1.6 %collective-permute-done.other_ref = bf16[16,128,256]{2,1,0:T(8,128)(2,1)S(1)} collective-permute-done((bf16[16,128,256]{2,1,0:T(8,128)(2,1)S(1)}, bf16[16,128,256]{2,1,0:T(8,128)(2,1)S(1)}, u32[]{:S(2)}, u32[]{:S(2)}) %collective-permute-start) | collective-permute-done | bytes 1048608 | tf_op jit(solution)/shard_map/ppermute | solution.py:275
  40.6 6.8 %apply_kernel.2 = (f32[16,128,256]{2,1,0:T(8,128)S(1)}, bf16[16,128,256]{2,1,0:T(8,128)(2,1)S(1)}, f32[3,8,128]{2,1,0:T(8,128)S(1)}, bf16[64,256,256]{2,1,0:T(8,128)(2,1)S(1)}, bf16[64,256,256]{2,1,0:T(8,128)(2,1)S(1)}) custom-call(s32[1]{0:T(128)S(6)} %copy.9.count_ref, s32[64]{0:T(128)S(1)} %copy-done.2, s32[64]{0:T(128)S(1)} %copy-done.3, s32[1]{0:T(128)} %bitcast.at_ref, ...), custom_call_target="tpu_custom_call" | custom-call | tf_op jit(solution)/shard_map/apply_kernel/pallas_call | solution.py:264
  47.4 8.4 %collective-permute-start.1 = (bf16[16,128,256]{2,1,0:T(8,128)(2,1)S(1)}, bf16[16,128,256]{2,1,0:T(8,128)(2,1)S(1)}, u32[]{:S(2)}, u32[]{:S(2)}) collective-permute-start(bf16[16,128,256]{2,1,0:T(8,128)(2,1)S(1)} %get-tuple-element.26), channel_id=1, source_target_pairs={{0,16},{16,0},{32,48},{48,32},{64,80},{80,64},{96,112},{112,96},{1... | collective-permute-start | bytes 3145736 | tf_op jit(solution)/shard_map/ppermute | solution.py:275
  55.9 2.2 %collective-permute-done.2.got_sums_ref = f32[3,8,128]{2,1,0:T(8,128)S(1)} collective-permute-done((f32[3,8,128]{2,1,0:T(8,128)S(1)}, f32[3,8,128]{2,1,0:T(8,128)S(1)}, u32[]{:S(2)}, u32[]{:S(2)}) %collective-permute-start.2) | collective-permute-done | bytes 12320 | tf_op jit(solution)/shard_map/ppermute | solution.py:275
  58.1 0.4 join_kernel.2
  58.5 20.4 %all_to_all.27.got_ref = bf16[16,272,128]{2,1,0:T(8,128)(2,1)S(1)} all-to-all(bf16[16,272,128]{2,1,0:T(8,128)(2,1)S(1)} %join_kernel.2), channel_id=1, replica_groups=mesh['op'=8,'sec'=16] {'sec'}, dimensions={0} | all-to-all | bytes 2228224 | tf_op jit(solution)/shard_map/all_to_all | solution.py:279
  79.0 2.5 %collective-permute-start.5 = (f32[264,128]{1,0:T(8,128)S(1)}, f32[264,128]{1,0:T(8,128)S(1)}, u32[]{:S(2)}, u32[]{:S(2)}) collective-permute-start(f32[264,128]{1,0:T(8,128)S(1)} %sum_kernel.2.own_ref), channel_id=1, source_target_pairs={{0,96},{16,112},{32,0},{48,16},{64,32},{80,48},{96,64},{112,80},{1... | collective-permute-start | bytes 405512 | tf_op jit(solution)/shard_map/ppermute | solution.py:309
  81.6 0.5 collective-permute-start.4
  82.2 2.6 %collective-permute-done.5.far_ref = f32[264,128]{1,0:T(8,128)S(1)} collective-permute-done((f32[264,128]{1,0:T(8,128)S(1)}, f32[264,128]{1,0:T(8,128)S(1)}, u32[]{:S(2)}, u32[]{:S(2)}) %collective-permute-start.5) | collective-permute-done | bytes 135200 | tf_op jit(solution)/shard_map/ppermute | solution.py:309
  84.8 2.2 %collective-permute-done.4.across_ref = f32[264,128]{1,0:T(8,128)S(1)} collective-permute-done((f32[264,128]{1,0:T(8,128)S(1)}, f32[264,128]{1,0:T(8,128)S(1)}, u32[]{:S(2)}, u32[]{:S(2)}) %collective-permute-start.4) | collective-permute-done | bytes 135200 | tf_op jit(solution)/shard_map/ppermute | solution.py:309
  87.0 3.7 %collective-permute-done.3.near_ref = f32[264,128]{1,0:T(8,128)S(1)} collective-permute-done((f32[264,128]{1,0:T(8,128)S(1)}, f32[264,128]{1,0:T(8,128)S(1)}, u32[]{:S(2)}, u32[]{:S(2)}) %collective-permute-start.3) | collective-permute-done | bytes 135200 | tf_op jit(solution)/shard_map/ppermute | solution.py:309
  90.7 0.5 correct_kernel.1
  91.2 18.5 %all_to_all.28.own_ref = bf16[16,128,256]{2,1,0:T(8,128)(2,1)S(1)} all-to-all(bf16[16,128,256]{2,1,0:T(8,128)(2,1)S(1)} %get-tuple-element.30), channel_id=1, replica_groups=mesh['op'=8,'sec'=16] {'sec'}, dimensions={0} | all-to-all | bytes 2097152 | tf_op jit(solution)/shard_map/all_to_all | solution.py:279
  109.6 2.4 %collective-permute-start.6 = (bf16[16,128,256]{2,1,0:T(8,128)(2,1)S(1)}, bf16[16,128,256]{2,1,0:T(8,128)(2,1)S(1)}, u32[]{:S(2)}, u32[]{:S(2)}) collective-permute-start(bf16[16,128,256]{2,1,0:T(8,128)(2,1)S(1)} %all_to_all.28.own_ref), channel_id=1, source_target_pairs={{0,16},{16,0},{32,48},{48,32},{64,80},{80,64},{96,112},{112,96},{1... | collective-permute-start | bytes 3145736 | tf_op jit(solution)/shard_map/ppermute | solution.py:275
  112.0 2.3 %collective-permute-done.6.other_ref = bf16[16,128,256]{2,1,0:T(8,128)(2,1)S(1)} collective-permute-done((bf16[16,128,256]{2,1,0:T(8,128)(2,1)S(1)}, bf16[16,128,256]{2,1,0:T(8,128)(2,1)S(1)}, u32[]{:S(2)}, u32[]{:S(2)}) %collective-permute-start.6) | collective-permute-done | bytes 1048608 | tf_op jit(solution)/shard_map/ppermute | solution.py:275
  114.3 4.7 %apply_kernel.3 = (f32[16,128,256]{2,1,0:T(8,128)S(1)}, bf16[16,128,256]{2,1,0:T(8,128)(2,1)S(1)}, f32[6,8,128]{2,1,0:T(8,128)S(1)}) custom-call(s32[1]{0:T(128)S(6)} %copy.9.count_ref, s32[64]{0:T(128)S(1)} %copy-done.2, s32[64]{0:T(128)S(1)} %copy-done.3, s32[1]{0:T(128)} %bitcast.at_ref, bf16[16,128,256]{2,1,0:T(8,128)(2,1)S(1)} %all_to_all.28.own_ref, ...), custom_call_target="tpu_custom_call" | custom-call | tf_op jit(solution)/shard_map/apply_kernel/pallas_call | solution.py:264
  119.0 8.3 %collective-permute-start.7 = (bf16[16,128,256]{2,1,0:T(8,128)(2,1)S(1)}, bf16[16,128,256]{2,1,0:T(8,128)(2,1)S(1)}, u32[]{:S(2)}, u32[]{:S(2)}) collective-permute-start(bf16[16,128,256]{2,1,0:T(8,128)(2,1)S(1)} %get-tuple-element.35), channel_id=1, source_target_pairs={{0,16},{16,0},{32,48},{48,32},{64,80},{80,64},{96,112},{112,96},{1... | collective-permute-start | bytes 3145736 | tf_op jit(solution)/shard_map/ppermute | solution.py:275
  127.4 2.2 %collective-permute-done.8.got_sums_ref = f32[6,8,128]{2,1,0:T(8,128)S(1)} collective-permute-done((f32[6,8,128]{2,1,0:T(8,128)S(1)}, f32[6,8,128]{2,1,0:T(8,128)S(1)}, u32[]{:S(2)}, u32[]{:S(2)}) %collective-permute-start.8) | collective-permute-done | bytes 24608 | tf_op jit(solution)/shard_map/ppermute | solution.py:275
  129.6 0.4 join_kernel.3
  130.0 20.2 %all_to_all.29.got_ref = bf16[16,272,128]{2,1,0:T(8,128)(2,1)S(1)} all-to-all(bf16[16,272,128]{2,1,0:T(8,128)(2,1)S(1)} %join_kernel.3), channel_id=1, replica_groups=mesh['op'=8,'sec'=16] {'sec'}, dimensions={0} | all-to-all | bytes 2228224 | tf_op jit(solution)/shard_map/all_to_all | solution.py:279
  150.6 1.4 collective-permute-start.9
  152.0 2.4 %collective-permute-done.11.far_ref = f32[264,128]{1,0:T(8,128)S(1)} collective-permute-done((f32[264,128]{1,0:T(8,128)S(1)}, f32[264,128]{1,0:T(8,128)S(1)}, u32[]{:S(2)}, u32[]{:S(2)}) %collective-permute-start.11) | collective-permute-done | bytes 135200 | tf_op jit(solution)/shard_map/ppermute | solution.py:309
  154.4 1.7 %collective-permute-done.10.across_ref = f32[264,128]{1,0:T(8,128)S(1)} collective-permute-done((f32[264,128]{1,0:T(8,128)S(1)}, f32[264,128]{1,0:T(8,128)S(1)}, u32[]{:S(2)}, u32[]{:S(2)}) %collective-permute-start.10) | collective-permute-done | bytes 135200 | tf_op jit(solution)/shard_map/ppermute | solution.py:309
  156.0 3.9 %collective-permute-done.9.near_ref = f32[264,128]{1,0:T(8,128)S(1)} collective-permute-done((f32[264,128]{1,0:T(8,128)S(1)}, f32[264,128]{1,0:T(8,128)S(1)}, u32[]{:S(2)}, u32[]{:S(2)}) %collective-permute-start.9) | collective-permute-done | bytes 135200 | tf_op jit(solution)/shard_map/ppermute | solution.py:309
  159.9 0.3 ritz_kernel.1.own_ref
  160.2 1.1 collective-permute-start.12
  161.4 1.2 collective-permute-done.12.other_ref
  162.5 0.8 place_kernel.1
  (18 shorter events, 1.1 us)
Async XLA Ops:
  0.6 40.0 %copy-start.3 = (s32[64]{0:T(128)S(1)}, s32[64]{0:T(128)}, u32[]{:S(2)}) copy-start(s32[64]{0:T(128)} %to_ref.3) | copy-start | bytes 772
  0.6 40.0 %copy-start.2 = (s32[64]{0:T(128)S(1)}, s32[64]{0:T(128)}, u32[]{:S(2)}) copy-start(s32[64]{0:T(128)} %from_ref.3) | copy-start | bytes 772
  0.7 1.0 copy-start.1
  35.3 5.3 %collective-permute-start = (bf16[16,128,256]{2,1,0:T(8,128)(2,1)S(1)}, bf16[16,128,256]{2,1,0:T(8,128)(2,1)S(1)}, u32[]{:S(2)}, u32[]{:S(2)}) collective-permute-start(bf16[16,128,256]{2,1,0:T(8,128)(2,1)S(1)} %all_to_all.26.own_ref), channel_id=1, source_target_pairs={{0,16},{16,0},{32,48},{48,32},{64,80},{80,64},{96,112},{112,96},{1... | collective-permute-start | bytes 3145736 | tf_op jit(solution)/shard_map/ppermute | solution.py:275
  47.4 10.7 %collective-permute-start.1 = (bf16[16,128,256]{2,1,0:T(8,128)(2,1)S(1)}, bf16[16,128,256]{2,1,0:T(8,128)(2,1)S(1)}, u32[]{:S(2)}, u32[]{:S(2)}) collective-permute-start(bf16[16,128,256]{2,1,0:T(8,128)(2,1)S(1)} %get-tuple-element.26), channel_id=1, source_target_pairs={{0,16},{16,0},{32,48},{48,32},{64,80},{80,64},{96,112},{112,96},{1... | collective-permute-start | bytes 3145736 | tf_op jit(solution)/shard_map/ppermute | solution.py:275
  55.8 2.3 %collective-permute-start.2 = (f32[3,8,128]{2,1,0:T(8,128)S(1)}, f32[3,8,128]{2,1,0:T(8,128)S(1)}, u32[]{:S(2)}, u32[]{:S(2)}) collective-permute-start(f32[3,8,128]{2,1,0:T(8,128)S(1)} %get-tuple-element.27.sums_ref), channel_id=1, source_target_pairs={{0,16},{16,0},{32,48},{48,32},{64,80},{80,64},{96,112},{112,96},{1... | collective-permute-start | bytes 36872 | tf_op jit(solution)/shard_map/ppermute | solution.py:275
  58.5 32.2 %copy-start = (f32[1,256,256]{2,1,0:T(8,128)S(1)}, f32[1,256,256]{2,1,0:T(8,128)}, u32[]{:S(2)}) copy-start(f32[1,256,256]{2,1,0:T(8,128)} %diag_ref.1) | copy-start | bytes 786436
  79.0 5.8 %collective-permute-start.5 = (f32[264,128]{1,0:T(8,128)S(1)}, f32[264,128]{1,0:T(8,128)S(1)}, u32[]{:S(2)}, u32[]{:S(2)}) collective-permute-start(f32[264,128]{1,0:T(8,128)S(1)} %sum_kernel.2.own_ref), channel_id=1, source_target_pairs={{0,96},{16,112},{32,0},{48,16},{64,32},{80,48},{96,64},{112,80},{1... | collective-permute-start | bytes 405512 | tf_op jit(solution)/shard_map/ppermute | solution.py:309
  81.6 5.5 %collective-permute-start.4 = (f32[264,128]{1,0:T(8,128)S(1)}, f32[264,128]{1,0:T(8,128)S(1)}, u32[]{:S(2)}, u32[]{:S(2)}) collective-permute-start(f32[264,128]{1,0:T(8,128)S(1)} %sum_kernel.2.own_ref), channel_id=1, source_target_pairs={{0,64},{16,80},{32,96},{48,112},{64,0},{80,16},{96,32},{112,48},{1... | collective-permute-start | bytes 405512 | tf_op jit(solution)/shard_map/ppermute | solution.py:309
  82.1 8.6 %collective-permute-start.3 = (f32[264,128]{1,0:T(8,128)S(1)}, f32[264,128]{1,0:T(8,128)S(1)}, u32[]{:S(2)}, u32[]{:S(2)}) collective-permute-start(f32[264,128]{1,0:T(8,128)S(1)} %sum_kernel.2.own_ref), channel_id=1, source_target_pairs={{0,32},{16,48},{32,64},{48,80},{64,96},{80,112},{96,0},{112,16},{1... | collective-permute-start | bytes 405512 | tf_op jit(solution)/shard_map/ppermute | solution.py:309
  109.6 4.7 %collective-permute-start.6 = (bf16[16,128,256]{2,1,0:T(8,128)(2,1)S(1)}, bf16[16,128,256]{2,1,0:T(8,128)(2,1)S(1)}, u32[]{:S(2)}, u32[]{:S(2)}) collective-permute-start(bf16[16,128,256]{2,1,0:T(8,128)(2,1)S(1)} %all_to_all.28.own_ref), channel_id=1, source_target_pairs={{0,16},{16,0},{32,48},{48,32},{64,80},{80,64},{96,112},{112,96},{1... | collective-permute-start | bytes 3145736 | tf_op jit(solution)/shard_map/ppermute | solution.py:275
  119.0 10.6 %collective-permute-start.7 = (bf16[16,128,256]{2,1,0:T(8,128)(2,1)S(1)}, bf16[16,128,256]{2,1,0:T(8,128)(2,1)S(1)}, u32[]{:S(2)}, u32[]{:S(2)}) collective-permute-start(bf16[16,128,256]{2,1,0:T(8,128)(2,1)S(1)} %get-tuple-element.35), channel_id=1, source_target_pairs={{0,16},{16,0},{32,48},{48,32},{64,80},{80,64},{96,112},{112,96},{1... | collective-permute-start | bytes 3145736 | tf_op jit(solution)/shard_map/ppermute | solution.py:275
  127.3 2.3 %collective-permute-start.8 = (f32[6,8,128]{2,1,0:T(8,128)S(1)}, f32[6,8,128]{2,1,0:T(8,128)S(1)}, u32[]{:S(2)}, u32[]{:S(2)}) collective-permute-start(f32[6,8,128]{2,1,0:T(8,128)S(1)} %get-tuple-element.36.sums_ref), channel_id=1, source_target_pairs={{0,16},{16,0},{32,48},{48,32},{64,80},{80,64},{96,112},{112,96},{1... | collective-permute-start | bytes 73736 | tf_op jit(solution)/shard_map/ppermute | solution.py:275
  150.4 3.9 %collective-permute-start.11 = (f32[264,128]{1,0:T(8,128)S(1)}, f32[264,128]{1,0:T(8,128)S(1)}, u32[]{:S(2)}, u32[]{:S(2)}) collective-permute-start(f32[264,128]{1,0:T(8,128)S(1)} %sum_kernel.3.own_ref), channel_id=1, source_target_pairs={{0,96},{16,112},{32,0},{48,16},{64,32},{80,48},{96,64},{112,80},{1... | collective-permute-start | bytes 405512 | tf_op jit(solution)/shard_map/ppermute | solution.py:309
  150.5 5.5 %collective-permute-start.10 = (f32[264,128]{1,0:T(8,128)S(1)}, f32[264,128]{1,0:T(8,128)S(1)}, u32[]{:S(2)}, u32[]{:S(2)}) collective-permute-start(f32[264,128]{1,0:T(8,128)S(1)} %sum_kernel.3.own_ref), channel_id=1, source_target_pairs={{0,64},{16,80},{32,96},{48,112},{64,0},{80,16},{96,32},{112,48},{1... | collective-permute-start | bytes 405512 | tf_op jit(solution)/shard_map/ppermute | solution.py:309
  150.6 9.3 %collective-permute-start.9 = (f32[264,128]{1,0:T(8,128)S(1)}, f32[264,128]{1,0:T(8,128)S(1)}, u32[]{:S(2)}, u32[]{:S(2)}) collective-permute-start(f32[264,128]{1,0:T(8,128)S(1)} %sum_kernel.3.own_ref), channel_id=1, source_target_pairs={{0,32},{16,48},{32,64},{48,80},{64,96},{80,112},{96,0},{112,16},{1... | collective-permute-start | bytes 405512 | tf_op jit(solution)/shard_map/ppermute | solution.py:309
  160.2 2.3 %collective-permute-start.12 = (f32[2,128,256]{2,1,0:T(8,128)S(1)}, f32[2,128,256]{2,1,0:T(8,128)S(1)}, u32[]{:S(2)}, u32[]{:S(2)}) collective-permute-start(f32[2,128,256]{2,1,0:T(8,128)S(1)} %ritz_kernel.1.own_ref), channel_id=1, source_target_pairs={{0,16},{16,0},{32,48},{48,32},{64,80},{80,64},{96,112},{112,96},{1... | collective-permute-start | bytes 786440 | tf_op jit(solution)/shard_map/ppermute | solution.py:275

commit v5 on v4

--- a/solution.py
+++ b/solution.py
@@ -9,7 +9,8 @@
 SEC, B, LANES = 16, 256, 128
 HALF = B // 2
 CHIPS_X, N_OP = 4, 8
-TERMS, GROUP, STEP, AHEAD = 64, 8, 16, 3
+TERMS, GROUP, STEP, AHEAD = 64, 8, 16, 2
+GROUPS = TERMS // GROUP - STEP // GROUP
 ENTRIES = SEC * B * B
 CORE_SWAP = [(i, i ^ 1) for i in range(N_OP)]
 ALONG_X = [[(i, (i + 2 * hops) % N_OP) for i in range(N_OP)] for hops in range(1, CHIPS_X)]
@@ -42,11 +43,14 @@
     return jnp.sum(ref, keepdims=True)
 
 
-def square_kernel(at_ref, start_ref, out_ref, half_ref):
-    squares = fold(start_ref[0] * start_ref[0])
+def square_kernel(at_ref, start_ref, out_ref, half_ref, start, sem):
+    copy = pltpu.make_async_copy(start_ref, start, sem)
+    copy.start()
+    copy.wait()
+    squares = fold(start[0] * start[0])
     for s in range(SEC):
         out_ref[s] = squares
-    half_ref[...] = start_ref[0, half_rows(at_ref[0]), :]
+    half_ref[...] = start[0, half_rows(at_ref[0]), :]
 
 
 def scale_kernel(got_ref, start_ref, copies_ref, sums_ref, start_half_ref, norm_ref):
@@ -68,22 +72,34 @@
     sums_ref[1] = fold(wide * wide) / CHIPS_X
 
 
-def apply_kernel(count_ref, from_ref, to_ref, at_ref, own_ref, other_ref, more_ref, left_ref, right_ref,
-                 keep_ref, send_ref, sums_ref, *rest):
+def head_kernel(left_ref, right_ref, left_out, right_out, sems):
+    copies = [
+        pltpu.make_async_copy(ref.at[pl.ds(0, STEP)], out, sems.at[k])
+        for k, (ref, out) in enumerate(((left_ref, left_out), (right_ref, right_out)))
+    ]
+    for copy in copies:
+        copy.start()
+    for copy in copies:
+        copy.wait()
+
+
+def apply_kernel(count_ref, from_ref, to_ref, at_ref, own_ref, other_ref, more_ref, left_head, right_head,
+                 left_ref, right_ref, keep_ref, send_ref, sums_ref, *rest):
     core = at_ref[0]
     fetched = len(rest) > 4
     left, right = rest[:2] if fetched else (left_ref, right_ref)
-    x_ref, acc_ref, send, sems = rest[2:6] if fetched else rest
+    x_ref, acc_ref, halves_ref, sems = rest[2:6] if fetched else rest
 
     def term_copies(i):
-        at = pl.ds(i * GROUP, GROUP)
+        out = pl.ds(i * GROUP, GROUP)
+        at = pl.ds(STEP + i * GROUP, GROUP)
         return [
-            pltpu.make_async_copy(ref.at[at], held.at[at], rest[6].at[k, i])
+            pltpu.make_async_copy(ref.at[at], held.at[out], rest[6].at[k, i])
             for k, (ref, held) in enumerate(((left_ref, left), (right_ref, right)))
         ]
 
     def fetch(i):
-        @pl.when((i < TERMS // GROUP) & (i * GROUP < count_ref[0]))
+        @pl.when((i < GROUPS) & (STEP + i * GROUP < count_ref[0]))
         def _():
             for copy in term_copies(i):
                 copy.start()
@@ -105,59 +121,62 @@
     for copy in gathers:
         copy.wait()
 
-    def halves(t):
-        source, target = from_ref[t], to_ref[t]
-        first = dot(left[t], x_ref[source], (1, 0)).astype(BF16)
-        second = dot(left[t], x_ref[target], (0, 0)).astype(BF16)
-        return t, source, target, first, second
-
-    def add(t, source, target, first, second):
-        acc_ref[target] += dot(first, right[t], (1, 1))
-        acc_ref[source] += dot(second, right[t], (1, 0))
-
-    @pl.loop(0, TERMS // STEP)
-    def _(i):
+    def step(i, lefts, rights, base):
         live = count_ref[0] - i * STEP
-        for k in range(STEP // GROUP if fetched else 0):
-            @pl.when(live > k * GROUP)
-            def _():
-                for copy in term_copies(i * (STEP // GROUP) + k):
-                    copy.wait()
-
-            fetch(i * (STEP // GROUP) + k + AHEAD)
+
+        def first_half(j):
+            t = i * STEP + j
+            block = lefts[base + j]
+            halves_ref[2 * j] = dot(block, x_ref[from_ref[t]], (1, 0)).astype(BF16)
+            halves_ref[2 * j + 1] = dot(block, x_ref[to_ref[t]], (0, 0)).astype(BF16)
+
+        def second_half(j):
+            t = i * STEP + j
+            block = rights[base + j]
+            acc_ref[to_ref[t]] += dot(halves_ref[2 * j], block, (1, 1))
+            acc_ref[from_ref[t]] += dot(halves_ref[2 * j + 1], block, (1, 0))
 
         @pl.when(live >= STEP)
         def _():
-            held = halves(i * STEP)
-            for j in range(1, STEP):
-                ahead = halves(i * STEP + j)
-                add(*held)
-                held = ahead
-            add(*held)
+            for j in range(STEP):
+                first_half(j)
+            for j in range(STEP):
+                second_half(j)
 
         @pl.when((live > 0) & (live < STEP))
         def _():
             @pl.loop(0, live)
             def _(j):
-                add(*halves(i * STEP + j))
+                first_half(j)
+                second_half(j)
+
+    step(0, left_head, right_head, 0)
+
+    @pl.loop(0, TERMS // STEP - 1)
+    def _(i):
+        for k in range(STEP // GROUP if fetched else 0):
+            @pl.when(count_ref[0] > (i + 1) * STEP + k * GROUP)
+            def _():
+                for copy in term_copies(i * (STEP // GROUP) + k):
+                    copy.wait()
+
+            fetch(i * (STEP // GROUP) + k + AHEAD)
+
+        step(i + 1, left, right, i * STEP)
 
     keep_copy = pltpu.make_async_copy(acc_ref.at[:, half_rows(core), :], keep_ref, sems.at[0])
     keep_copy.start()
 
-    @pl.loop(0, SEC)
-    def _(s):
-        send[s] = acc_ref[s, half_rows(1 - core), :].astype(BF16)
-
-    send_copy = pltpu.make_async_copy(send, send_ref, sems.at[1])
-    send_copy.start()
-
     def inner(s, total):
-        return total + fold(x_ref[s].astype(F32) * acc_ref[s])
+        mine, theirs = half_rows(core), half_rows(1 - core)
+        part = acc_ref[s, theirs, :]
+        send_ref[s] = part.astype(BF16)
+        total = total + fold(x_ref[s, theirs, :].astype(F32) * part)
+        return total + fold(x_ref[s, mine, :].astype(F32) * acc_ref[s, mine, :])
 
     sums_ref[0] = lax.fori_loop(0, SEC, inner, jnp.zeros((8, LANES), F32))
     sums_ref[1:] = more_ref[...]
     keep_copy.wait()
-    send_copy.wait()
 
 
 def join_kernel(keep_ref, got_ref, sums_ref, got_sums_ref, out_ref):
@@ -279,28 +298,30 @@
     return lax.all_to_all(x, "sec", 0, 0, tiled=True)
 
 
-def apply_call(terms, own, other, more, left_env, right_env, fetch):
-    if fetch:
-        left_env, right_env = (pltpu.with_memory_space_constraint(x, pltpu.HBM) for x in (left_env, right_env))
-    return call(
+def in_hbm(*arrays):
+    return [pltpu.with_memory_space_constraint(x, pltpu.HBM) for x in arrays]
+
+
+def terms_shape(count):
+    return [shape(count, B, B, dtype=BF16)] * 2
+
+
+def apply_ham(terms, copies, more, head, left, right, fetch):
+    own = over_sectors(copies)
+    keep, send, sums, *held = call(
         apply_kernel,
         28,
-        [SMEM] * 4 + [ANY] * 2 + [WHOLE] + [ANY if fetch else WHOLE] * 2,
-        [shape(SEC, HALF, B), GATHER, shape(more.shape[0] + 1, 8, LANES)] + [shape(TERMS, B, B, dtype=BF16)] * (2 * fetch),
-        *terms, own, other, more, left_env, right_env,
-        out_specs=[ANY] * 2 + [WHOLE] * (3 if fetch else 1),
+        [SMEM] * 4 + [ANY] * 2 + [WHOLE] * 3 + [ANY if fetch else WHOLE] * 2,
+        [shape(SEC, HALF, B), GATHER, shape(more.shape[0] + 1, 8, LANES)] + terms_shape(TERMS - STEP) * fetch,
+        *terms, own, swap(own), more, *head, left, right,
+        out_specs=[ANY] + [WHOLE] * (4 if fetch else 2),
         scratch_shapes=[
             pltpu.VMEM((SEC, B, B), BF16),
             pltpu.VMEM((SEC, B, B), F32),
-            pltpu.VMEM((SEC, HALF, B), BF16),
+            pltpu.VMEM((2 * STEP, B, B), BF16),
             pltpu.SemaphoreType.DMA((2,)),
-        ] + [pltpu.SemaphoreType.DMA((2, TERMS // GROUP))] * fetch,
-    )
-
-
-def apply_ham(terms, copies, more, left_env, right_env, fetch):
-    own = over_sectors(copies)
-    keep, send, sums, *held = apply_call(terms, own, swap(own), more, left_env, right_env, fetch)
+        ] + [pltpu.SemaphoreType.DMA((2, GROUPS))] * fetch,
+    )
     payload = call(
         join_kernel, 16, [WHOLE] * 4, shape(SEC, B + SCALARS, LANES, dtype=BF16),
         keep, swap(send), sums, swap(sums),
@@ -313,20 +334,26 @@
     at = (lax.axis_index("op") % 2).astype(jnp.int32).reshape(1)
     terms = (term_count, sector_from, sector_to, at)
     squares, half = call(
-        square_kernel, 16, [SMEM, WHOLE], [shape(SEC, 8, LANES), shape(HALF, B)], at, start_vector
+        square_kernel, 16, [SMEM, ANY], [shape(SEC, 8, LANES), shape(HALF, B)], at, *in_hbm(start_vector),
+        scratch_shapes=[pltpu.VMEM((1, B, B), F32), pltpu.SemaphoreType.DMA],
     )
     copies, more, start, norm = call(
         scale_kernel, 16, [WHOLE] * 2,
         [GATHER, shape(2, 8, LANES), COLUMNS, shape(2, 8, LANES)],
         over_sectors(squares), half,
     )
-    got, held = apply_ham(terms, copies, more, left_env, right_env, True)
+    far = in_hbm(left_env, right_env)
+    head = call(
+        head_kernel, 16, [ANY] * 2, terms_shape(STEP), *far,
+        out_specs=[WHOLE] * 2, scratch_shapes=[pltpu.SemaphoreType.DMA((2,))],
+    )
+    got, held = apply_ham(terms, copies, more, head, *far, True)
     copies, more, corr, sigma, theta = call(
         correct_kernel, 16, [SMEM] + [WHOLE] * 7,
         [GATHER, shape(5, 8, LANES), COLUMNS, COLUMNS, shape(8, LANES)],
         at, *got, start, diag_guess, norm,
     )
-    got, _ = apply_ham(terms, copies, more, *held, False)
+    got, _ = apply_ham(terms, copies, more, head, *held, False)
     halves = call(ritz_kernel, 16, [WHOLE] * 9, shape(2, HALF, B), *got, start, norm, corr, sigma, theta)
     return call(
         place_kernel, 16, [SMEM] + [WHOLE] * 2, [shape(1, B, B), shape(1, B, B)], at, halves, swap(halves)

time: 163 us -> 160 us (0.982)
  Pallas kernels: 14.4 us -> 30.1 us
  starting transfers between devices: 28.1 us -> 15.6 us
  waiting for transfers between devices: 26 us -> 18.7 us
    pallas_call x11 -> x12, Pallas kernels: 14.4 us -> 30.1 us  [call(): pl.pallas_call(kernel, out_shape=outs, in_specs=ins, compiler_params=pltp...]
    ppermute x7, starting transfers between devices: 23.4 us -> 9.7 us  [swap(): return lax.ppermute(x, 'op', CORE_SWAP)]
    ppermute x6, waiting for transfers between devices: 16.4 us -> 10.9 us  [apply_ham(): return ((part, *(lax.ppermute(part, 'op', perm) for perm in ALONG_X)), held)]
    ppermute x7, waiting for transfers between devices: 9.53 us -> 7.81 us  [swap(): return lax.ppermute(x, 'op', CORE_SWAP)]
  transfers between devices with their start and end apart: 13 -> 13, of which waited for: 11 -> 10; matrix products, arithmetic and copies ran while one was open for 0% -> 0% of each run, Pallas kernels for 0% -> 1%
where the time goes in v5:
time: 160 us; the launch traced here: 159 us
  blocking collectives  93.4 us (58%)
  Pallas kernels  30.1 us (19%)
  waiting for transfers between devices  18.7 us (12%)
  starting transfers between devices  15.6 us (10%)
    all_to_all x5, blocking collectives, over_sectors(): return lax.all_to_all(x, 'sec', 0, 0, tiled=True)  93.4 us
    pallas_call x12, Pallas kernels, call(): pl.pallas_call(kernel, out_shape=outs, in_specs=ins, compiler_params=pltp...  30.1 us
    ppermute x6, waiting for transfers between devices, apply_ham(): return ((part, *(lax.ppermute(part, 'op', perm) for perm in ALONG_X)), held)  10.9 us
    ppermute x7, starting transfers between devices, swap(): return lax.ppermute(x, 'op', CORE_SWAP)  9.7 us
    ppermute x7, waiting for transfers between devices, swap(): return lax.ppermute(x, 'op', CORE_SWAP)  7.81 us
    ppermute x6, starting transfers between devices, apply_ham(): return ((part, *(lax.ppermute(part, 'op', perm) for perm in ALONG_X)), held)  5.86 us
  transfers between devices with their start and end apart: 13, of which 10 were waited for; matrix products, arithmetic and copies ran while one was open for 0% of the time, Pallas kernels for 1%

profile of v5, /device:TPU:1, one launch (start us, length us, event | category | flops | bytes accessed | tf_op | source)
XLA Modules:
  0.0 159.3 jit_solution(17718892215050153456)
XLA Ops:
  0.6 1.0 square_kernel.1
  1.6 14.9 %all_to_all.25.got_ref = f32[16,8,128]{2,1,0:T(8,128)S(1)} all-to-all(f32[16,8,128]{2,1,0:T(8,128)S(1)} %get-tuple-element.23), channel_id=1, replica_groups=mesh['op'=8,'sec'=16] {'sec'}, dimensions={0} | all-to-all | bytes 131072 | tf_op jit(solution)/shard_map/all_to_all | solution.py:298
  16.8 18.5 %all_to_all.26.own_ref = bf16[16,128,256]{2,1,0:T(8,128)(2,1)S(1)} all-to-all(bf16[16,128,256]{2,1,0:T(8,128)(2,1)S(1)} %get-tuple-element.25), channel_id=1, replica_groups=mesh['op'=8,'sec'=16] {'sec'}, dimensions={0} | all-to-all | bytes 2097152 | tf_op jit(solution)/shard_map/all_to_all | solution.py:298
  35.3 3.0 %collective-permute-start = (bf16[16,128,256]{2,1,0:T(8,128)(2,1)S(1)}, bf16[16,128,256]{2,1,0:T(8,128)(2,1)S(1)}, u32[]{:S(2)}, u32[]{:S(2)}) collective-permute-start(bf16[16,128,256]{2,1,0:T(8,128)(2,1)S(1)} %all_to_all.26.own_ref), channel_id=1, source_target_pairs={{0,16},{16,0},{32,48},{48,32},{64,80},{80,64},{96,112},{112,96},{1... | collective-permute-start | bytes 3145736 | tf_op jit(solution)/shard_map/ppermute | solution.py:294
  39.0 2.2 %head_kernel.1 = (bf16[16,256,256]{2,1,0:T(8,128)(2,1)S(1)}, bf16[16,256,256]{2,1,0:T(8,128)(2,1)S(1)}) custom-call(bf16[64,256,256]{2,1,0:T(8,128)(2,1)} %left_ref.3, bf16[64,256,256]{2,1,0:T(8,128)(2,1)} %right_ref.3), custom_call_target="tpu_custom_call" | custom-call | tf_op jit(solution)/shard_map/head_kernel/pallas_call | solution.py:283
  41.3 12.1 %apply_kernel.2 = (f32[16,128,256]{2,1,0:T(8,128)S(1)}, bf16[16,128,256]{2,1,0:T(8,128)(2,1)S(1)}, f32[3,8,128]{2,1,0:T(8,128)S(1)}, bf16[48,256,256]{2,1,0:T(8,128)(2,1)S(1)}, bf16[48,256,256]{2,1,0:T(8,128)(2,1)S(1)}) custom-call(s32[1]{0:T(128)S(6)} %copy.9.count_ref, s32[64]{0:T(128)S(1)} %copy-done.1, s32[64]{0:T(128)S(1)} %copy-done.2, s32[1]{0:T(128)} %bitcast.at_ref, ...), custom_call_target="tpu_custom_call" | custom-call | tf_op jit(solution)/shard_map/apply_kernel/pallas_call | solution.py:283
  53.5 0.5 collective-permute-start.2
  54.0 2.2 %collective-permute-done.2.got_sums_ref = f32[3,8,128]{2,1,0:T(8,128)S(1)} collective-permute-done((f32[3,8,128]{2,1,0:T(8,128)S(1)}, f32[3,8,128]{2,1,0:T(8,128)S(1)}, u32[]{:S(2)}, u32[]{:S(2)}) %collective-permute-start.2) | collective-permute-done | bytes 12320 | tf_op jit(solution)/shard_map/ppermute | solution.py:294
  56.5 20.4 %all_to_all.27.got_ref = bf16[16,272,128]{2,1,0:T(8,128)(2,1)S(1)} all-to-all(bf16[16,272,128]{2,1,0:T(8,128)(2,1)S(1)} %join_kernel.2), channel_id=1, replica_groups=mesh['op'=8,'sec'=16] {'sec'}, dimensions={0} | all-to-all | bytes 2228224 | tf_op jit(solution)/shard_map/all_to_all | solution.py:298
  77.1 1.4 collective-permute-start.5
  78.5 1.1 collective-permute-start.4
  79.6 0.7 collective-permute-start.3
  80.3 0.7 collective-permute-done.5.far_ref
  81.0 2.9 %collective-permute-done.4.across_ref = f32[264,128]{1,0:T(8,128)S(1)} collective-permute-done((f32[264,128]{1,0:T(8,128)S(1)}, f32[264,128]{1,0:T(8,128)S(1)}, u32[]{:S(2)}, u32[]{:S(2)}) %collective-permute-start.4) | collective-permute-done | bytes 135200 | tf_op jit(solution)/shard_map/ppermute | solution.py:330
  83.9 2.0 %collective-permute-done.3.near_ref = f32[264,128]{1,0:T(8,128)S(1)} collective-permute-done((f32[264,128]{1,0:T(8,128)S(1)}, f32[264,128]{1,0:T(8,128)S(1)}, u32[]{:S(2)}, u32[]{:S(2)}) %collective-permute-start.3) | collective-permute-done | bytes 135200 | tf_op jit(solution)/shard_map/ppermute | solution.py:330
  85.9 0.5 correct_kernel.1
  86.4 19.9 %all_to_all.28.own_ref = bf16[16,128,256]{2,1,0:T(8,128)(2,1)S(1)} all-to-all(bf16[16,128,256]{2,1,0:T(8,128)(2,1)S(1)} %get-tuple-element.34), channel_id=1, replica_groups=mesh['op'=8,'sec'=16] {'sec'}, dimensions={0} | all-to-all | bytes 2097152 | tf_op jit(solution)/shard_map/all_to_all | solution.py:298
  106.3 2.9 %collective-permute-start.6 = (bf16[16,128,256]{2,1,0:T(8,128)(2,1)S(1)}, bf16[16,128,256]{2,1,0:T(8,128)(2,1)S(1)}, u32[]{:S(2)}, u32[]{:S(2)}) collective-permute-start(bf16[16,128,256]{2,1,0:T(8,128)(2,1)S(1)} %all_to_all.28.own_ref), channel_id=1, source_target_pairs={{0,16},{16,0},{32,48},{48,32},{64,80},{80,64},{96,112},{112,96},{1... | collective-permute-start | bytes 3145736 | tf_op jit(solution)/shard_map/ppermute | solution.py:294
  109.1 2.3 %collective-permute-done.6.other_ref = bf16[16,128,256]{2,1,0:T(8,128)(2,1)S(1)} collective-permute-done((bf16[16,128,256]{2,1,0:T(8,128)(2,1)S(1)}, bf16[16,128,256]{2,1,0:T(8,128)(2,1)S(1)}, u32[]{:S(2)}, u32[]{:S(2)}) %collective-permute-start.6) | collective-permute-done | bytes 1048608 | tf_op jit(solution)/shard_map/ppermute | solution.py:294
  111.4 11.9 %apply_kernel.3 = (f32[16,128,256]{2,1,0:T(8,128)S(1)}, bf16[16,128,256]{2,1,0:T(8,128)(2,1)S(1)}, f32[6,8,128]{2,1,0:T(8,128)S(1)}) custom-call(s32[1]{0:T(128)S(6)} %copy.9.count_ref, s32[64]{0:T(128)S(1)} %copy-done.1, s32[64]{0:T(128)S(1)} %copy-done.2, s32[1]{0:T(128)} %bitcast.at_ref, bf16[16,128,256]{2,1,0:T(8,128)(2,1)S(1)} %all_to_all.28.own_ref, ...), custom_call_target="tpu_custom_call" | custom-call | tf_op jit(solution)/shard_map/apply_kernel/pallas_call | solution.py:283
  123.4 0.5 collective-permute-start.7
  123.9 2.2 %collective-permute-done.8.got_sums_ref = f32[6,8,128]{2,1,0:T(8,128)S(1)} collective-permute-done((f32[6,8,128]{2,1,0:T(8,128)S(1)}, f32[6,8,128]{2,1,0:T(8,128)S(1)}, u32[]{:S(2)}, u32[]{:S(2)}) %collective-permute-start.8) | collective-permute-done | bytes 24608 | tf_op jit(solution)/shard_map/ppermute | solution.py:294
  126.1 0.4 join_kernel.3
  126.5 19.7 %all_to_all.29.got_ref = bf16[16,272,128]{2,1,0:T(8,128)(2,1)S(1)} all-to-all(bf16[16,272,128]{2,1,0:T(8,128)(2,1)S(1)} %join_kernel.3), channel_id=1, replica_groups=mesh['op'=8,'sec'=16] {'sec'}, dimensions={0} | all-to-all | bytes 2228224 | tf_op jit(solution)/shard_map/all_to_all | solution.py:298
  146.4 1.7 %collective-permute-start.10 = (f32[264,128]{1,0:T(8,128)S(1)}, f32[264,128]{1,0:T(8,128)S(1)}, u32[]{:S(2)}, u32[]{:S(2)}) collective-permute-start(f32[264,128]{1,0:T(8,128)S(1)} %sum_kernel.3.own_ref), channel_id=1, source_target_pairs={{0,64},{16,80},{32,96},{48,112},{64,0},{80,16},{96,32},{112,48},{1... | collective-permute-start | bytes 405512 | tf_op jit(solution)/shard_map/ppermute | solution.py:330
  148.2 0.8 collective-permute-start.9
  148.9 1.3 collective-permute-done.11.far_ref
  150.3 1.6 %collective-permute-done.10.across_ref = f32[264,128]{1,0:T(8,128)S(1)} collective-permute-done((f32[264,128]{1,0:T(8,128)S(1)}, f32[264,128]{1,0:T(8,128)S(1)}, u32[]{:S(2)}, u32[]{:S(2)}) %collective-permute-start.10) | collective-permute-done | bytes 135200 | tf_op jit(solution)/shard_map/ppermute | solution.py:330
  151.9 2.4 %collective-permute-done.9.near_ref = f32[264,128]{1,0:T(8,128)S(1)} collective-permute-done((f32[264,128]{1,0:T(8,128)S(1)}, f32[264,128]{1,0:T(8,128)S(1)}, u32[]{:S(2)}, u32[]{:S(2)}) %collective-permute-start.9) | collective-permute-done | bytes 135200 | tf_op jit(solution)/shard_map/ppermute | solution.py:330
  154.6 2.7 %collective-permute-start.12 = (f32[2,128,256]{2,1,0:T(8,128)S(1)}, f32[2,128,256]{2,1,0:T(8,128)S(1)}, u32[]{:S(2)}, u32[]{:S(2)}) collective-permute-start(f32[2,128,256]{2,1,0:T(8,128)S(1)} %ritz_kernel.1.own_ref), channel_id=1, source_target_pairs={{0,16},{16,0},{32,48},{48,32},{64,80},{80,64},{96,112},{112,96},{1... | collective-permute-start | bytes 786440 | tf_op jit(solution)/shard_map/ppermute | solution.py:294
  157.3 1.2 collective-permute-done.12.other_ref
  158.5 0.8 place_kernel.1
  (17 shorter events, 1.5 us)
Async XLA Ops:
  35.3 5.9 %collective-permute-start = (bf16[16,128,256]{2,1,0:T(8,128)(2,1)S(1)}, bf16[16,128,256]{2,1,0:T(8,128)(2,1)S(1)}, u32[]{:S(2)}, u32[]{:S(2)}) collective-permute-start(bf16[16,128,256]{2,1,0:T(8,128)(2,1)S(1)} %all_to_all.26.own_ref), channel_id=1, source_target_pairs={{0,16},{16,0},{32,48},{48,32},{64,80},{80,64},{96,112},{112,96},{1... | collective-permute-start | bytes 3145736 | tf_op jit(solution)/shard_map/ppermute | solution.py:294
  39.0 2.3 %copy-start.1 = (s32[64]{0:T(128)S(1)}, s32[64]{0:T(128)}, u32[]{:S(2)}) copy-start(s32[64]{0:T(128)} %from_ref.3) | copy-start | bytes 772
  39.0 2.3 %copy-start.2 = (s32[64]{0:T(128)S(1)}, s32[64]{0:T(128)}, u32[]{:S(2)}) copy-start(s32[64]{0:T(128)} %to_ref.3) | copy-start | bytes 772
  53.4 2.8 %collective-permute-start.1 = (bf16[16,128,256]{2,1,0:T(8,128)(2,1)S(1)}, bf16[16,128,256]{2,1,0:T(8,128)(2,1)S(1)}, u32[]{:S(2)}, u32[]{:S(2)}) collective-permute-start(bf16[16,128,256]{2,1,0:T(8,128)(2,1)S(1)} %get-tuple-element.30), channel_id=1, source_target_pairs={{0,16},{16,0},{32,48},{48,32},{64,80},{80,64},{96,112},{112,96},{1... | collective-permute-start | bytes 3145736 | tf_op jit(solution)/shard_map/ppermute | solution.py:294
  53.5 2.7 %collective-permute-start.2 = (f32[3,8,128]{2,1,0:T(8,128)S(1)}, f32[3,8,128]{2,1,0:T(8,128)S(1)}, u32[]{:S(2)}, u32[]{:S(2)}) collective-permute-start(f32[3,8,128]{2,1,0:T(8,128)S(1)} %get-tuple-element.31.sums_ref), channel_id=1, source_target_pairs={{0,16},{16,0},{32,48},{48,32},{64,80},{80,64},{96,112},{112,96},{1... | collective-permute-start | bytes 36872 | tf_op jit(solution)/shard_map/ppermute | solution.py:294
  56.5 29.4 %copy-start = (f32[1,256,256]{2,1,0:T(8,128)S(1)}, f32[1,256,256]{2,1,0:T(8,128)}, u32[]{:S(2)}) copy-start(f32[1,256,256]{2,1,0:T(8,128)} %diag_ref.1) | copy-start | bytes 786436
  77.1 3.9 %collective-permute-start.5 = (f32[264,128]{1,0:T(8,128)S(1)}, f32[264,128]{1,0:T(8,128)S(1)}, u32[]{:S(2)}, u32[]{:S(2)}) collective-permute-start(f32[264,128]{1,0:T(8,128)S(1)} %sum_kernel.2.own_ref), channel_id=1, source_target_pairs={{0,96},{16,112},{32,0},{48,16},{64,32},{80,48},{96,64},{112,80},{1... | collective-permute-start | bytes 405512 | tf_op jit(solution)/shard_map/ppermute | solution.py:330
  78.5 5.4 %collective-permute-start.4 = (f32[264,128]{1,0:T(8,128)S(1)}, f32[264,128]{1,0:T(8,128)S(1)}, u32[]{:S(2)}, u32[]{:S(2)}) collective-permute-start(f32[264,128]{1,0:T(8,128)S(1)} %sum_kernel.2.own_ref), channel_id=1, source_target_pairs={{0,64},{16,80},{32,96},{48,112},{64,0},{80,16},{96,32},{112,48},{1... | collective-permute-start | bytes 405512 | tf_op jit(solution)/shard_map/ppermute | solution.py:330
  79.6 6.3 %collective-permute-start.3 = (f32[264,128]{1,0:T(8,128)S(1)}, f32[264,128]{1,0:T(8,128)S(1)}, u32[]{:S(2)}, u32[]{:S(2)}) collective-permute-start(f32[264,128]{1,0:T(8,128)S(1)} %sum_kernel.2.own_ref), channel_id=1, source_target_pairs={{0,32},{16,48},{32,64},{48,80},{64,96},{80,112},{96,0},{112,16},{1... | collective-permute-start | bytes 405512 | tf_op jit(solution)/shard_map/ppermute | solution.py:330
  106.3 5.2 %collective-permute-start.6 = (bf16[16,128,256]{2,1,0:T(8,128)(2,1)S(1)}, bf16[16,128,256]{2,1,0:T(8,128)(2,1)S(1)}, u32[]{:S(2)}, u32[]{:S(2)}) collective-permute-start(bf16[16,128,256]{2,1,0:T(8,128)(2,1)S(1)} %all_to_all.28.own_ref), channel_id=1, source_target_pairs={{0,16},{16,0},{32,48},{48,32},{64,80},{80,64},{96,112},{112,96},{1... | collective-permute-start | bytes 3145736 | tf_op jit(solution)/shard_map/ppermute | solution.py:294
  123.4 2.8 %collective-permute-start.7 = (bf16[16,128,256]{2,1,0:T(8,128)(2,1)S(1)}, bf16[16,128,256]{2,1,0:T(8,128)(2,1)S(1)}, u32[]{:S(2)}, u32[]{:S(2)}) collective-permute-start(bf16[16,128,256]{2,1,0:T(8,128)(2,1)S(1)} %get-tuple-element.39), channel_id=1, source_target_pairs={{0,16},{16,0},{32,48},{48,32},{64,80},{80,64},{96,112},{112,96},{1... | collective-permute-start | bytes 3145736 | tf_op jit(solution)/shard_map/ppermute | solution.py:294
  123.8 2.3 %collective-permute-start.8 = (f32[6,8,128]{2,1,0:T(8,128)S(1)}, f32[6,8,128]{2,1,0:T(8,128)S(1)}, u32[]{:S(2)}, u32[]{:S(2)}) collective-permute-start(f32[6,8,128]{2,1,0:T(8,128)S(1)} %get-tuple-element.40.sums_ref), channel_id=1, source_target_pairs={{0,16},{16,0},{32,48},{48,32},{64,80},{80,64},{96,112},{112,96},{1... | collective-permute-start | bytes 73736 | tf_op jit(solution)/shard_map/ppermute | solution.py:294
  146.3 3.9 %collective-permute-start.11 = (f32[264,128]{1,0:T(8,128)S(1)}, f32[264,128]{1,0:T(8,128)S(1)}, u32[]{:S(2)}, u32[]{:S(2)}) collective-permute-start(f32[264,128]{1,0:T(8,128)S(1)} %sum_kernel.3.own_ref), channel_id=1, source_target_pairs={{0,96},{16,112},{32,0},{48,16},{64,32},{80,48},{96,64},{112,80},{1... | collective-permute-start | bytes 405512 | tf_op jit(solution)/shard_map/ppermute | solution.py:330
  146.4 5.5 %collective-permute-start.10 = (f32[264,128]{1,0:T(8,128)S(1)}, f32[264,128]{1,0:T(8,128)S(1)}, u32[]{:S(2)}, u32[]{:S(2)}) collective-permute-start(f32[264,128]{1,0:T(8,128)S(1)} %sum_kernel.3.own_ref), channel_id=1, source_target_pairs={{0,64},{16,80},{32,96},{48,112},{64,0},{80,16},{96,32},{112,48},{1... | collective-permute-start | bytes 405512 | tf_op jit(solution)/shard_map/ppermute | solution.py:330
  148.2 6.1 %collective-permute-start.9 = (f32[264,128]{1,0:T(8,128)S(1)}, f32[264,128]{1,0:T(8,128)S(1)}, u32[]{:S(2)}, u32[]{:S(2)}) collective-permute-start(f32[264,128]{1,0:T(8,128)S(1)} %sum_kernel.3.own_ref), channel_id=1, source_target_pairs={{0,32},{16,48},{32,64},{48,80},{64,96},{80,112},{96,0},{112,16},{1... | collective-permute-start | bytes 405512 | tf_op jit(solution)/shard_map/ppermute | solution.py:330
  154.6 3.8 %collective-permute-start.12 = (f32[2,128,256]{2,1,0:T(8,128)S(1)}, f32[2,128,256]{2,1,0:T(8,128)S(1)}, u32[]{:S(2)}, u32[]{:S(2)}) collective-permute-start(f32[2,128,256]{2,1,0:T(8,128)S(1)} %ritz_kernel.1.own_ref), channel_id=1, source_target_pairs={{0,16},{16,0},{32,48},{48,32},{64,80},{80,64},{96,112},{112,96},{1... | collective-permute-start | bytes 786440 | tf_op jit(solution)/shard_map/ppermute | solution.py:294

commit v6 on v5

--- a/solution.py
+++ b/solution.py
@@ -14,7 +14,6 @@
 ENTRIES = SEC * B * B
 CORE_SWAP = [(i, i ^ 1) for i in range(N_OP)]
 ALONG_X = [[(i, (i + 2 * hops) % N_OP) for i in range(N_OP)] for hops in range(1, CHIPS_X)]
-SCALARS = 16
 
 
 def dot(a, b, contract):
@@ -43,33 +42,73 @@
     return jnp.sum(ref, keepdims=True)
 
 
-def square_kernel(at_ref, start_ref, out_ref, half_ref, start, sem):
+def ratio(whole, part):
+    return jnp.where(part > 0.0, whole / jnp.where(part > 0.0, part, 1.0), 1.0)
+
+
+def over_rows(places):
+    return jnp.broadcast_to(places, (B // 8, 8, LANES)).reshape(B, LANES)
+
+
+def as_codes(values):
+    return values.astype(jnp.int32).astype(jnp.int16)
+
+
+def exponent_of(values):
+    return jnp.ceil(jnp.log2(jnp.maximum(jnp.abs(values), 1e-30)) + 0.001)
+
+
+def encode(half):
+    exponent = exponent_of(jnp.max(jnp.abs(half).reshape(B // 8, 8, LANES), axis=0)) - 15.0
+    codes = jnp.round(half * over_rows(jnp.exp2(-exponent)))
+    return as_codes(jnp.clip(codes, -32767.0, 32767.0)), exponent
+
+
+def encode_kernel(at_ref, start_ref, codes_ref, half_ref, start, sem):
     copy = pltpu.make_async_copy(start_ref, start, sem)
     copy.start()
     copy.wait()
-    squares = fold(start[0] * start[0])
+    half = fold_columns(start[0, half_rows(at_ref[0]), :])
+    half_ref[...] = half
+    codes, exponent = encode(half)
+    tail = as_codes(jnp.concatenate([exponent, jnp.zeros((8, LANES), F32)], axis=0))
     for s in range(SEC):
-        out_ref[s] = squares
-    half_ref[...] = start[0, half_rows(at_ref[0]), :]
-
-
-def scale_kernel(got_ref, start_ref, copies_ref, sums_ref, start_half_ref, norm_ref):
-    squares = got_ref[0]
-    for s in range(1, SEC):
-        squares = squares + got_ref[s]
-    mean_sq = total_of(squares) / ENTRIES
+        codes_ref[s, :B, :] = codes
+        codes_ref[s, B:, :] = tail
+
+
+def decode(ref, s):
+    exponent = ref[s, B:, :].astype(jnp.int32).astype(F32)[:8, :]
+    return ref[s, :B, :].astype(jnp.int32).astype(F32) * over_rows(jnp.exp2(exponent))
+
+
+def decode_start(core, own_ref, other_ref, x_ref, norm_ref):
+    zero = jnp.zeros((8, LANES), F32)
+
+    def squares(s, total):
+        for ref in (own_ref, other_ref):
+            block = decode(ref, s)
+            total = total + fold(block * block)
+        return total
+
+    mean_sq = total_of(lax.fori_loop(0, SEC, squares, zero)) / ENTRIES
     scale = 1.0 / jnp.sqrt(mean_sq + 1e-06)
     norm_ref[0] = jnp.broadcast_to(scale, (8, LANES))
     norm_ref[1] = jnp.broadcast_to(mean_sq, (8, LANES))
-    start = start_ref[...]
-    start_half_ref[...] = fold_columns(start)
-    vec = start * scale
-    rounded = vec.astype(BF16)
-    for s in range(SEC):
-        copies_ref[s] = rounded
-    wide = rounded.astype(F32)
-    sums_ref[0] = fold(vec * wide) / CHIPS_X
-    sums_ref[1] = fold(wide * wide) / CHIPS_X
+
+    def place(s, totals):
+        vec_round, round_sq = totals
+        for ref, at in ((own_ref, core), (other_ref, 1 - core)):
+            vec = decode(ref, s) * scale
+            rounded = vec.astype(BF16)
+            x_ref[s, half_rows(at), :LANES] = rounded[:HALF, :]
+            x_ref[s, half_rows(at), LANES:] = rounded[HALF:, :]
+            wide = rounded.astype(F32)
+            vec_round, round_sq = vec_round + fold(vec * wide), round_sq + fold(wide * wide)
+        return vec_round, round_sq
+
+    vec_round, round_sq = lax.fori_loop(0, SEC, place, (zero, zero))
+    return ratio(total_of(vec_round), total_of(round_sq))
 
 
 def head_kernel(left_ref, right_ref, left_out, right_out, sems):
@@ -83,19 +122,48 @@
         copy.wait()
 
 
-def apply_kernel(count_ref, from_ref, to_ref, at_ref, own_ref, other_ref, more_ref, left_head, right_head,
-                 left_ref, right_ref, keep_ref, send_ref, sums_ref, *rest):
+def first_kernel(count_ref, from_ref, to_ref, at_ref, own_ref, other_ref, left_head, right_head, left_ref, right_ref,
+                 keep_ref, send_ref, sums_ref, norm_ref, left, right, x_ref, acc_ref, halves_ref, sems, term_sems):
+    def prepare(core):
+        return decode_start(core, own_ref, other_ref, x_ref, norm_ref)
+
+    apply_terms(
+        prepare, (count_ref, from_ref, to_ref, at_ref), (left_head, right_head), (left_ref, right_ref), (left, right),
+        keep_ref, send_ref, sums_ref, x_ref, acc_ref, halves_ref, sems, term_sems,
+    )
+
+
+def second_kernel(count_ref, from_ref, to_ref, at_ref, own_ref, other_ref, more_ref, left_head, right_head,
+                  left, right, keep_ref, send_ref, sums_ref, x_ref, acc_ref, halves_ref, sems):
+    def prepare(core):
+        copies = [
+            pltpu.make_async_copy(own_ref, x_ref.at[:, half_rows(core), :], sems.at[0]),
+            pltpu.make_async_copy(other_ref, x_ref.at[:, half_rows(1 - core), :], sems.at[1]),
+        ]
+        for copy in copies:
+            copy.start()
+        sums_ref[1:] = more_ref[...]
+        for copy in copies:
+            copy.wait()
+        return 1.0
+
+    apply_terms(
+        prepare, (count_ref, from_ref, to_ref, at_ref), (left_head, right_head), None, (left, right),
+        keep_ref, send_ref, sums_ref, x_ref, acc_ref, halves_ref, sems, None,
+    )
+
+
+def apply_terms(prepare, terms, heads, far, held, keep_ref, send_ref, sums_ref, x_ref, acc_ref, halves_ref, sems,
+                term_sems):
+    count_ref, from_ref, to_ref, at_ref = terms
     core = at_ref[0]
-    fetched = len(rest) > 4
-    left, right = rest[:2] if fetched else (left_ref, right_ref)
-    x_ref, acc_ref, halves_ref, sems = rest[2:6] if fetched else rest
 
     def term_copies(i):
         out = pl.ds(i * GROUP, GROUP)
         at = pl.ds(STEP + i * GROUP, GROUP)
         return [
-            pltpu.make_async_copy(ref.at[at], held.at[out], rest[6].at[k, i])
-            for k, (ref, held) in enumerate(((left_ref, left), (right_ref, right)))
+            pltpu.make_async_copy(ref.at[at], to.at[out], term_sems.at[k, i])
+            for k, (ref, to) in enumerate(zip(far, held))
         ]
 
     def fetch(i):
@@ -104,13 +172,7 @@
             for copy in term_copies(i):
                 copy.start()
 
-    gathers = [
-        pltpu.make_async_copy(own_ref, x_ref.at[:, half_rows(core), :], sems.at[0]),
-        pltpu.make_async_copy(other_ref, x_ref.at[:, half_rows(1 - core), :], sems.at[1]),
-    ]
-    for copy in gathers:
-        copy.start()
-    if fetched:
+    if far:
         for i in range(AHEAD):
             fetch(i)
 
@@ -118,8 +180,7 @@
     def _(s):
         acc_ref[s] = jnp.zeros((B, B), F32)
 
-    for copy in gathers:
-        copy.wait()
+    weight = prepare(core)
 
     def step(i, lefts, rights, base):
         live = count_ref[0] - i * STEP
@@ -150,11 +211,11 @@
                 first_half(j)
                 second_half(j)
 
-    step(0, left_head, right_head, 0)
+    step(0, *heads, 0)
 
     @pl.loop(0, TERMS // STEP - 1)
     def _(i):
-        for k in range(STEP // GROUP if fetched else 0):
+        for k in range(STEP // GROUP if far else 0):
             @pl.when(count_ref[0] > (i + 1) * STEP + k * GROUP)
             def _():
                 for copy in term_copies(i * (STEP // GROUP) + k):
@@ -162,7 +223,7 @@
 
             fetch(i * (STEP // GROUP) + k + AHEAD)
 
-        step(i + 1, left, right, i * STEP)
+        step(i + 1, *held, i * STEP)
 
     keep_copy = pltpu.make_async_copy(acc_ref.at[:, half_rows(core), :], keep_ref, sems.at[0])
     keep_copy.start()
@@ -174,41 +235,40 @@
         total = total + fold(x_ref[s, theirs, :].astype(F32) * part)
         return total + fold(x_ref[s, mine, :].astype(F32) * acc_ref[s, mine, :])
 
-    sums_ref[0] = lax.fori_loop(0, SEC, inner, jnp.zeros((8, LANES), F32))
-    sums_ref[1:] = more_ref[...]
+    sums_ref[0] = lax.fori_loop(0, SEC, inner, jnp.zeros((8, LANES), F32)) * weight
     keep_copy.wait()
 
 
 def join_kernel(keep_ref, got_ref, sums_ref, got_sums_ref, out_ref):
-    row = lax.broadcasted_iota(jnp.int32, (SCALARS, LANES), 0)
-    lane = lax.broadcasted_iota(jnp.int32, (SCALARS, LANES), 1)
-    tile = jnp.zeros((SCALARS, LANES), F32)
+    lane = lax.broadcasted_iota(jnp.int32, (8, LANES), 1)
+    scalars = jnp.zeros((8, LANES), F32)
     for k in range(sums_ref.shape[0]):
-        rest = total_of(sums_ref[k] + got_sums_ref[k])
-        for part in range(3):
-            top = rest.astype(BF16).astype(F32)
-            tile = jnp.where((row == part) & (lane == k), top, tile)
-            rest = rest - top
-    tile = tile.astype(BF16)
-
-    @pl.loop(0, SEC)
+        scalars = jnp.where(lane == k, total_of(sums_ref[k] + got_sums_ref[k]), scalars)
+    power = exponent_of(scalars)
+    scaled = scalars * jnp.exp2(14.0 - power)
+    high = jnp.round(scaled)
+    low = jnp.round((scaled - high) * 32768.0)
+    row = lax.broadcasted_iota(jnp.int32, (8, LANES), 0)
+    lower = jnp.where(row == 0, high, jnp.where(row == 1, low, jnp.where(row == 2, power, 0.0)))
+
+    @pl.loop(0, SEC, unroll=4)
     def _(s):
-        block = (keep_ref[s] + got_ref[s].astype(F32)).astype(BF16)
-        out_ref[s, :HALF, :] = block[:, :LANES]
-        out_ref[s, HALF:B, :] = block[:, LANES:]
-        out_ref[s, B:, :] = tile
+        codes, exponent = encode(fold_columns(keep_ref[s] + got_ref[s].astype(F32)))
+        out_ref[s, :B, :] = codes
+        out_ref[s, B:, :] = as_codes(jnp.concatenate([exponent, lower], axis=0))
 
 
 def sum_kernel(got_ref, out_ref):
-    for k in range(0, B, HALF):
-        total = got_ref[0, k:k + HALF, :].astype(F32)
-        for s in range(1, SEC):
-            total = total + got_ref[s, k:k + HALF, :].astype(F32)
-        out_ref[k:k + HALF, :] = total
-    tile = got_ref[0, B:, :].astype(F32)
-    for s in range(1, SEC):
-        tile = tile + got_ref[s, B:, :].astype(F32)
-    out_ref[B:, :] = tile[:8, :] + tile[8:, :]
+    def add(s, totals):
+        tail = got_ref[s, B:, :].astype(jnp.int32).astype(F32)
+        scalars = (tail[8:9, :] + tail[9:10, :] * (1.0 / 32768.0)) * jnp.exp2(tail[10:11, :] - 14.0)
+        return totals[0] + decode(got_ref, s), totals[1] + scalars
+
+    zeros = jnp.zeros((B, LANES), F32), jnp.zeros((1, LANES), F32)
+    total, scalars = lax.fori_loop(0, SEC, add, zeros, unroll=4)
+    out_ref[:B, :] = total
+    row = lax.broadcasted_iota(jnp.int32, (8, LANES), 0)
+    out_ref[B:, :] = jnp.where(row == 0, jnp.broadcast_to(scalars, (8, LANES)), 0.0)
 
 
 def sum_of_chips(part_refs, scalars):
@@ -220,13 +280,8 @@
     return total[:B, :], means
 
 
-def ratio(whole, part):
-    return jnp.where(part > 0.0, whole / jnp.where(part > 0.0, part, 1.0), 1.0)
-
-
 def correct_kernel(at_ref, own_ref, near_ref, across_ref, far_ref, start_ref, diag_ref, norm_ref, copies_ref, sums_ref, corr_ref, sigma_ref, theta_ref):
-    sigma, (theta, vec_round, round_sq) = sum_of_chips((own_ref, near_ref, across_ref, far_ref), 3)
-    theta = theta * ratio(vec_round, round_sq)
+    sigma, (theta,) = sum_of_chips((own_ref, near_ref, across_ref, far_ref), 1)
     vec = start_ref[...] * norm_ref[0, :1, :1]
     diag = fold_columns(diag_ref[0, half_rows(at_ref[0]), :])
     corr = (sigma - theta * vec) / jnp.maximum(jnp.abs(diag - theta), 1.0)
@@ -277,6 +332,7 @@
 ANY = pl.BlockSpec(memory_space=pl.ANY)
 GATHER = shape(SEC, HALF, B, dtype=BF16)
 COLUMNS = shape(B, LANES)
+PIECES = shape(SEC, B + 16, LANES, dtype=jnp.int16)
 
 
 def call(kernel, mib, ins, outs, *args, **kwargs):
@@ -306,54 +362,60 @@
     return [shape(count, B, B, dtype=BF16)] * 2
 
 
-def apply_ham(terms, copies, more, head, left, right, fetch):
-    own = over_sectors(copies)
-    keep, send, sums, *held = call(
-        apply_kernel,
-        28,
-        [SMEM] * 4 + [ANY] * 2 + [WHOLE] * 3 + [ANY if fetch else WHOLE] * 2,
-        [shape(SEC, HALF, B), GATHER, shape(more.shape[0] + 1, 8, LANES)] + terms_shape(TERMS - STEP) * fetch,
-        *terms, own, swap(own), more, *head, left, right,
-        out_specs=[ANY] + [WHOLE] * (4 if fetch else 2),
-        scratch_shapes=[
-            pltpu.VMEM((SEC, B, B), BF16),
-            pltpu.VMEM((SEC, B, B), F32),
-            pltpu.VMEM((2 * STEP, B, B), BF16),
-            pltpu.SemaphoreType.DMA((2,)),
-        ] + [pltpu.SemaphoreType.DMA((2, GROUPS))] * fetch,
-    )
+APPLY_SCRATCH = [
+    pltpu.VMEM((SEC, B, B), BF16),
+    pltpu.VMEM((SEC, B, B), F32),
+    pltpu.VMEM((2 * STEP, B, B), BF16),
+    pltpu.SemaphoreType.DMA((2,)),
+]
+SPLIT = [shape(SEC, HALF, B), GATHER]
+
+
+def reduce_partial(keep, send, sums):
     payload = call(
-        join_kernel, 16, [WHOLE] * 4, shape(SEC, B + SCALARS, LANES, dtype=BF16),
+        join_kernel, 16, [WHOLE] * 4, PIECES,
         keep, swap(send), sums, swap(sums),
     )
     part = call(sum_kernel, 16, [WHOLE], shape(B + 8, LANES), over_sectors(payload))
-    return (part, *(lax.ppermute(part, "op", perm) for perm in ALONG_X)), held
+    return part, *(lax.ppermute(part, "op", perm) for perm in ALONG_X)
 
 
 def per_device(start_vector, diag_guess, left_env, right_env, sector_from, sector_to, term_count):
     at = (lax.axis_index("op") % 2).astype(jnp.int32).reshape(1)
     terms = (term_count, sector_from, sector_to, at)
-    squares, half = call(
-        square_kernel, 16, [SMEM, ANY], [shape(SEC, 8, LANES), shape(HALF, B)], at, *in_hbm(start_vector),
+    codes, start = call(
+        encode_kernel, 16, [SMEM, ANY], [PIECES, COLUMNS],
+        at, *in_hbm(start_vector),
         scratch_shapes=[pltpu.VMEM((1, B, B), F32), pltpu.SemaphoreType.DMA],
-    )
-    copies, more, start, norm = call(
-        scale_kernel, 16, [WHOLE] * 2,
-        [GATHER, shape(2, 8, LANES), COLUMNS, shape(2, 8, LANES)],
-        over_sectors(squares), half,
     )
     far = in_hbm(left_env, right_env)
     head = call(
         head_kernel, 16, [ANY] * 2, terms_shape(STEP), *far,
         out_specs=[WHOLE] * 2, scratch_shapes=[pltpu.SemaphoreType.DMA((2,))],
     )
-    got, held = apply_ham(terms, copies, more, head, *far, True)
+    own = over_sectors(codes)
+    keep, send, sums, norm, *held = call(
+        first_kernel, 28, [SMEM] * 4 + [WHOLE] * 4 + [ANY] * 2,
+        SPLIT + [shape(1, 8, LANES), shape(2, 8, LANES)] + terms_shape(TERMS - STEP),
+        *terms, own, swap(own), *head, *far,
+        out_specs=[ANY] + [WHOLE] * 5,
+        scratch_shapes=APPLY_SCRATCH + [pltpu.SemaphoreType.DMA((2, GROUPS))],
+    )
+    got = reduce_partial(keep, send, sums)
     copies, more, corr, sigma, theta = call(
         correct_kernel, 16, [SMEM] + [WHOLE] * 7,
         [GATHER, shape(5, 8, LANES), COLUMNS, COLUMNS, shape(8, LANES)],
         at, *got, start, diag_guess, norm,
     )
-    got, _ = apply_ham(terms, copies, more, head, *held, False)
+    own = over_sectors(copies)
+    keep, send, sums = call(
+        second_kernel, 28, [SMEM] * 4 + [ANY] * 2 + [WHOLE] * 5,
+        SPLIT + [shape(6, 8, LANES)],
+        *terms, own, swap(own), more, *head, *held,
+        out_specs=[ANY] + [WHOLE] * 2,
+        scratch_shapes=APPLY_SCRATCH,
+    )
+    got = reduce_partial(keep, send, sums)
     halves = call(ritz_kernel, 16, [WHOLE] * 9, shape(2, HALF, B), *got, start, norm, corr, sigma, theta)
     return call(
         place_kernel, 16, [SMEM] + [WHOLE] * 2, [shape(1, B, B), shape(1, B, B)], at, halves, swap(halves)

time: 160 us -> 156 us (0.975)
  Pallas kernels: 30.1 us -> 19.2 us
  blocking collectives: 93.4 us -> 99.9 us
  waiting for transfers between devices: 18.7 us -> 22.7 us
  starting transfers between devices: 15.6 us -> 12.7 us
    pallas_call x12 -> x11, Pallas kernels: 30.1 us -> 19.2 us  [call(): pl.pallas_call(kernel, out_shape=outs, in_specs=ins, compiler_params=pltp...]
    all_to_all x5 -> x4, blocking collectives: 93.4 us -> 99.9 us  [over_sectors(): return lax.all_to_all(x, 'sec', 0, 0, tiled=True)]
    ppermute x6, waiting for transfers between devices: 10.9 us -> 14.9 us  [reduce_partial(): return (part, *(lax.ppermute(part, 'op', perm) for perm in ALONG_X))]
    ppermute x7, starting transfers between devices: 9.7 us -> 7.53 us  [swap(): return lax.ppermute(x, 'op', CORE_SWAP)]
where the time goes in v6:
time: 156 us
  blocking collectives  99.9 us (64%)
  waiting for transfers between devices  22.7 us (15%)
  Pallas kernels  19.2 us (12%)
  starting transfers between devices  12.7 us (8%)
    all_to_all x4, blocking collectives, over_sectors(): return lax.all_to_all(x, 'sec', 0, 0, tiled=True)  99.9 us
    pallas_call x11, Pallas kernels, call(): pl.pallas_call(kernel, out_shape=outs, in_specs=ins, compiler_params=pltp...  19.2 us
    ppermute x6, waiting for transfers between devices, reduce_partial(): return (part, *(lax.ppermute(part, 'op', perm) for perm in ALONG_X))  14.9 us
    ppermute x7, waiting for transfers between devices, swap(): return lax.ppermute(x, 'op', CORE_SWAP)  7.8 us
    ppermute x7, starting transfers between devices, swap(): return lax.ppermute(x, 'op', CORE_SWAP)  7.53 us
    ppermute x6, starting transfers between devices, reduce_partial(): return (part, *(lax.ppermute(part, 'op', perm) for perm in ALONG_X))  5.15 us
  transfers between devices with their start and end apart: 13, of which 10 were waited for; matrix products, arithmetic and copies ran while one was open for 0% of the time, Pallas kernels for 1%

profile of v6, /device:TPU:1, one launch (start us, length us, event | category | flops | bytes accessed | tf_op | source)
XLA Modules:
  0.0 155.9 jit_solution(10792092682723769985)
XLA Ops:
  0.6 1.1 encode_kernel.1
  1.8 25.3 %all_to_all.20.own_ref = s16[16,272,128]{2,1,0:T(8,128)(2,1)S(1)} all-to-all(s16[16,272,128]{2,1,0:T(8,128)(2,1)S(1)} %get-tuple-element.20), channel_id=1, replica_groups=mesh['op'=8,'sec'=16] {'sec'}, dimensions={0} | all-to-all | bytes 2228224 | tf_op jit(solution)/shard_map/all_to_all | solution.py:354
  27.1 2.0 %collective-permute-start = (s16[16,272,128]{2,1,0:T(8,128)(2,1)S(1)}, s16[16,272,128]{2,1,0:T(8,128)(2,1)S(1)}, u32[]{:S(2)}, u32[]{:S(2)}) collective-permute-start(s16[16,272,128]{2,1,0:T(8,128)(2,1)S(1)} %all_to_all.20.own_ref), channel_id=1, source_target_pairs={{0,16},{16,0},{32,48},{48,32},{64,80},{80,64},{96,112},{112,96},{1... | collective-permute-start | bytes 3342344 | tf_op jit(solution)/shard_map/ppermute | solution.py:350
  29.7 2.2 %head_kernel.1 = (bf16[16,256,256]{2,1,0:T(8,128)(2,1)S(1)}, bf16[16,256,256]{2,1,0:T(8,128)(2,1)S(1)}) custom-call(bf16[64,256,256]{2,1,0:T(8,128)(2,1)} %left_ref.3, bf16[64,256,256]{2,1,0:T(8,128)(2,1)} %right_ref.3), custom_call_target="tpu_custom_call" | custom-call | tf_op jit(solution)/shard_map/head_kernel/pallas_call | solution.py:339
  32.0 7.4 %first_kernel.1 = (f32[16,128,256]{2,1,0:T(8,128)S(1)}, bf16[16,128,256]{2,1,0:T(8,128)(2,1)S(1)}, f32[1,8,128]{2,1,0:T(8,128)S(1)}, f32[2,8,128]{2,1,0:T(8,128)...) custom-call(s32[1]{0:T(128)S(6)} %copy.9.count_ref, s32[64]{0:T(128)S(1)} %copy-done.1, ...), custom_call_target="tpu_custom_call" | custom-call | tf_op jit(solution)/shard_map/first_kernel/pallas_call | solution.py:339
  39.5 0.5 collective-permute-start.2
  40.0 2.2 %collective-permute-done.2.got_sums_ref = f32[1,8,128]{2,1,0:T(8,128)S(1)} collective-permute-done((f32[1,8,128]{2,1,0:T(8,128)S(1)}, f32[1,8,128]{2,1,0:T(8,128)S(1)}, u32[]{:S(2)}, u32[]{:S(2)}) %collective-permute-start.2) | collective-permute-done | bytes 4128 | tf_op jit(solution)/shard_map/ppermute | solution.py:350
  42.2 0.8 join_kernel.2
  42.9 28.0 %all_to_all.21.got_ref = s16[16,272,128]{2,1,0:T(8,128)(2,1)S(1)} all-to-all(s16[16,272,128]{2,1,0:T(8,128)(2,1)S(1)} %join_kernel.2), channel_id=1, replica_groups=mesh['op'=8,'sec'=16] {'sec'}, dimensions={0} | all-to-all | bytes 2228224 | tf_op jit(solution)/shard_map/all_to_all | solution.py:354
  70.9 0.4 sum_kernel.2.own_ref
  71.3 2.5 %collective-permute-start.5 = (f32[264,128]{1,0:T(8,128)S(1)}, f32[264,128]{1,0:T(8,128)S(1)}, u32[]{:S(2)}, u32[]{:S(2)}) collective-permute-start(f32[264,128]{1,0:T(8,128)S(1)} %sum_kernel.2.own_ref), channel_id=1, source_target_pairs={{0,96},{16,112},{32,0},{48,16},{64,32},{80,48},{96,64},{112,80},{1... | collective-permute-start | bytes 405512 | tf_op jit(solution)/shard_map/ppermute | solution.py:380
  74.2 0.8 collective-permute-start.3
  74.9 1.4 collective-permute-done.5.far_ref
  76.3 3.0 %collective-permute-done.4.across_ref = f32[264,128]{1,0:T(8,128)S(1)} collective-permute-done((f32[264,128]{1,0:T(8,128)S(1)}, f32[264,128]{1,0:T(8,128)S(1)}, u32[]{:S(2)}, u32[]{:S(2)}) %collective-permute-start.4) | collective-permute-done | bytes 135200 | tf_op jit(solution)/shard_map/ppermute | solution.py:380
  79.3 3.5 %collective-permute-done.3.near_ref = f32[264,128]{1,0:T(8,128)S(1)} collective-permute-done((f32[264,128]{1,0:T(8,128)S(1)}, f32[264,128]{1,0:T(8,128)S(1)}, u32[]{:S(2)}, u32[]{:S(2)}) %collective-permute-start.3) | collective-permute-done | bytes 135200 | tf_op jit(solution)/shard_map/ppermute | solution.py:380
  82.8 0.5 correct_kernel.1
  83.3 19.1 %all_to_all.22.own_ref = bf16[16,128,256]{2,1,0:T(8,128)(2,1)S(1)} all-to-all(bf16[16,128,256]{2,1,0:T(8,128)(2,1)S(1)} %get-tuple-element.28), channel_id=1, replica_groups=mesh['op'=8,'sec'=16] {'sec'}, dimensions={0} | all-to-all | bytes 2097152 | tf_op jit(solution)/shard_map/all_to_all | solution.py:354
  102.4 2.3 %collective-permute-start.6 = (bf16[16,128,256]{2,1,0:T(8,128)(2,1)S(1)}, bf16[16,128,256]{2,1,0:T(8,128)(2,1)S(1)}, u32[]{:S(2)}, u32[]{:S(2)}) collective-permute-start(bf16[16,128,256]{2,1,0:T(8,128)(2,1)S(1)} %all_to_all.22.own_ref), channel_id=1, source_target_pairs={{0,16},{16,0},{32,48},{48,32},{64,80},{80,64},{96,112},{112,96},{1... | collective-permute-start | bytes 3145736 | tf_op jit(solution)/shard_map/ppermute | solution.py:350
  104.7 2.3 %collective-permute-done.6.other_ref = bf16[16,128,256]{2,1,0:T(8,128)(2,1)S(1)} collective-permute-done((bf16[16,128,256]{2,1,0:T(8,128)(2,1)S(1)}, bf16[16,128,256]{2,1,0:T(8,128)(2,1)S(1)}, u32[]{:S(2)}, u32[]{:S(2)}) %collective-permute-start.6) | collective-permute-done | bytes 1048608 | tf_op jit(solution)/shard_map/ppermute | solution.py:350
  107.0 4.5 %second_kernel.1 = (f32[16,128,256]{2,1,0:T(8,128)S(1)}, bf16[16,128,256]{2,1,0:T(8,128)(2,1)S(1)}, f32[6,8,128]{2,1,0:T(8,128)S(1)}) custom-call(s32[1]{0:T(128)S(6)} %copy.9.count_ref, s32[64]{0:T(128)S(1)} %copy-done.1, s32[64]{0:T(128)S(1)} %copy-done.2, s32[1]{0:T(128)} %bitcast.at_ref, bf16[16,128,256]{2,1,0:T(8,128)(2,1)S(1)} %all_to_all.22.own_ref, ...), custom_call_target="tpu_custom_call" | custom-call | tf_op jit(solution)/shard_map/second_kernel/pallas_call | solution.py:339
  111.5 0.5 collective-permute-start.7
  112.1 2.2 %collective-permute-done.8.got_sums_ref = f32[6,8,128]{2,1,0:T(8,128)S(1)} collective-permute-done((f32[6,8,128]{2,1,0:T(8,128)S(1)}, f32[6,8,128]{2,1,0:T(8,128)S(1)}, u32[]{:S(2)}, u32[]{:S(2)}) %collective-permute-start.8) | collective-permute-done | bytes 24608 | tf_op jit(solution)/shard_map/ppermute | solution.py:350
  114.3 0.7 join_kernel.3
  115.1 27.5 %all_to_all.23.got_ref = s16[16,272,128]{2,1,0:T(8,128)(2,1)S(1)} all-to-all(s16[16,272,128]{2,1,0:T(8,128)(2,1)S(1)} %join_kernel.3), channel_id=1, replica_groups=mesh['op'=8,'sec'=16] {'sec'}, dimensions={0} | all-to-all | bytes 2228224 | tf_op jit(solution)/shard_map/all_to_all | solution.py:354
  142.6 0.4 sum_kernel.3.own_ref
  143.2 1.4 collective-permute-start.9
  144.5 2.4 %collective-permute-done.11.far_ref = f32[264,128]{1,0:T(8,128)S(1)} collective-permute-done((f32[264,128]{1,0:T(8,128)S(1)}, f32[264,128]{1,0:T(8,128)S(1)}, u32[]{:S(2)}, u32[]{:S(2)}) %collective-permute-start.11) | collective-permute-done | bytes 135200 | tf_op jit(solution)/shard_map/ppermute | solution.py:380
  146.9 1.7 %collective-permute-done.10.across_ref = f32[264,128]{1,0:T(8,128)S(1)} collective-permute-done((f32[264,128]{1,0:T(8,128)S(1)}, f32[264,128]{1,0:T(8,128)S(1)}, u32[]{:S(2)}, u32[]{:S(2)}) %collective-permute-start.10) | collective-permute-done | bytes 135200 | tf_op jit(solution)/shard_map/ppermute | solution.py:380
  148.6 3.0 %collective-permute-done.9.near_ref = f32[264,128]{1,0:T(8,128)S(1)} collective-permute-done((f32[264,128]{1,0:T(8,128)S(1)}, f32[264,128]{1,0:T(8,128)S(1)}, u32[]{:S(2)}, u32[]{:S(2)}) %collective-permute-start.9) | collective-permute-done | bytes 135200 | tf_op jit(solution)/shard_map/ppermute | solution.py:380
  151.9 2.1 %collective-permute-start.12 = (f32[2,128,256]{2,1,0:T(8,128)S(1)}, f32[2,128,256]{2,1,0:T(8,128)S(1)}, u32[]{:S(2)}, u32[]{:S(2)}) collective-permute-start(f32[2,128,256]{2,1,0:T(8,128)S(1)} %ritz_kernel.1.own_ref), channel_id=1, source_target_pairs={{0,16},{16,0},{32,48},{48,32},{64,80},{80,64},{96,112},{112,96},{1... | collective-permute-start | bytes 786440 | tf_op jit(solution)/shard_map/ppermute | solution.py:350
  153.9 1.2 collective-permute-done.12.other_ref
  155.1 0.8 place_kernel.1
  (15 shorter events, 1.0 us)
Async XLA Ops:
  27.1 4.9 %collective-permute-start = (s16[16,272,128]{2,1,0:T(8,128)(2,1)S(1)}, s16[16,272,128]{2,1,0:T(8,128)(2,1)S(1)}, u32[]{:S(2)}, u32[]{:S(2)}) collective-permute-start(s16[16,272,128]{2,1,0:T(8,128)(2,1)S(1)} %all_to_all.20.own_ref), channel_id=1, source_target_pairs={{0,16},{16,0},{32,48},{48,32},{64,80},{80,64},{96,112},{112,96},{1... | collective-permute-start | bytes 3342344 | tf_op jit(solution)/shard_map/ppermute | solution.py:350
  29.7 2.3 %copy-start.1 = (s32[64]{0:T(128)S(1)}, s32[64]{0:T(128)}, u32[]{:S(2)}) copy-start(s32[64]{0:T(128)} %from_ref.3) | copy-start | bytes 772
  29.7 2.3 %copy-start.2 = (s32[64]{0:T(128)S(1)}, s32[64]{0:T(128)}, u32[]{:S(2)}) copy-start(s32[64]{0:T(128)} %to_ref.3) | copy-start | bytes 772
  39.4 2.7 %collective-permute-start.1 = (bf16[16,128,256]{2,1,0:T(8,128)(2,1)S(1)}, bf16[16,128,256]{2,1,0:T(8,128)(2,1)S(1)}, u32[]{:S(2)}, u32[]{:S(2)}) collective-permute-start(bf16[16,128,256]{2,1,0:T(8,128)(2,1)S(1)} %get-tuple-element.24), channel_id=1, source_target_pairs={{0,16},{16,0},{32,48},{48,32},{64,80},{80,64},{96,112},{112,96},{1... | collective-permute-start | bytes 3145736 | tf_op jit(solution)/shard_map/ppermute | solution.py:350
  39.5 2.7 %collective-permute-start.2 = (f32[1,8,128]{2,1,0:T(8,128)S(1)}, f32[1,8,128]{2,1,0:T(8,128)S(1)}, u32[]{:S(2)}, u32[]{:S(2)}) collective-permute-start(f32[1,8,128]{2,1,0:T(8,128)S(1)} %get-tuple-element.25.sums_ref), channel_id=1, source_target_pairs={{0,16},{16,0},{32,48},{48,32},{64,80},{80,64},{96,112},{112,96},{1... | collective-permute-start | bytes 12296 | tf_op jit(solution)/shard_map/ppermute | solution.py:350
  42.9 39.9 %copy-start = (f32[1,256,256]{2,1,0:T(8,128)S(1)}, f32[1,256,256]{2,1,0:T(8,128)}, u32[]{:S(2)}) copy-start(f32[1,256,256]{2,1,0:T(8,128)} %diag_ref.1) | copy-start | bytes 786436
  71.3 5.0 %collective-permute-start.5 = (f32[264,128]{1,0:T(8,128)S(1)}, f32[264,128]{1,0:T(8,128)S(1)}, u32[]{:S(2)}, u32[]{:S(2)}) collective-permute-start(f32[264,128]{1,0:T(8,128)S(1)} %sum_kernel.2.own_ref), channel_id=1, source_target_pairs={{0,96},{16,112},{32,0},{48,16},{64,32},{80,48},{96,64},{112,80},{1... | collective-permute-start | bytes 405512 | tf_op jit(solution)/shard_map/ppermute | solution.py:380
  73.8 5.5 %collective-permute-start.4 = (f32[264,128]{1,0:T(8,128)S(1)}, f32[264,128]{1,0:T(8,128)S(1)}, u32[]{:S(2)}, u32[]{:S(2)}) collective-permute-start(f32[264,128]{1,0:T(8,128)S(1)} %sum_kernel.2.own_ref), channel_id=1, source_target_pairs={{0,64},{16,80},{32,96},{48,112},{64,0},{80,16},{96,32},{112,48},{1... | collective-permute-start | bytes 405512 | tf_op jit(solution)/shard_map/ppermute | solution.py:380
  74.2 8.7 %collective-permute-start.3 = (f32[264,128]{1,0:T(8,128)S(1)}, f32[264,128]{1,0:T(8,128)S(1)}, u32[]{:S(2)}, u32[]{:S(2)}) collective-permute-start(f32[264,128]{1,0:T(8,128)S(1)} %sum_kernel.2.own_ref), channel_id=1, source_target_pairs={{0,32},{16,48},{32,64},{48,80},{64,96},{80,112},{96,0},{112,16},{1... | collective-permute-start | bytes 405512 | tf_op jit(solution)/shard_map/ppermute | solution.py:380
  102.4 4.6 %collective-permute-start.6 = (bf16[16,128,256]{2,1,0:T(8,128)(2,1)S(1)}, bf16[16,128,256]{2,1,0:T(8,128)(2,1)S(1)}, u32[]{:S(2)}, u32[]{:S(2)}) collective-permute-start(bf16[16,128,256]{2,1,0:T(8,128)(2,1)S(1)} %all_to_all.22.own_ref), channel_id=1, source_target_pairs={{0,16},{16,0},{32,48},{48,32},{64,80},{80,64},{96,112},{112,96},{1... | collective-permute-start | bytes 3145736 | tf_op jit(solution)/shard_map/ppermute | solution.py:350
  111.5 2.8 %collective-permute-start.7 = (bf16[16,128,256]{2,1,0:T(8,128)(2,1)S(1)}, bf16[16,128,256]{2,1,0:T(8,128)(2,1)S(1)}, u32[]{:S(2)}, u32[]{:S(2)}) collective-permute-start(bf16[16,128,256]{2,1,0:T(8,128)(2,1)S(1)} %get-tuple-element.33), channel_id=1, source_target_pairs={{0,16},{16,0},{32,48},{48,32},{64,80},{80,64},{96,112},{112,96},{1... | collective-permute-start | bytes 3145736 | tf_op jit(solution)/shard_map/ppermute | solution.py:350
  112.0 2.3 %collective-permute-start.8 = (f32[6,8,128]{2,1,0:T(8,128)S(1)}, f32[6,8,128]{2,1,0:T(8,128)S(1)}, u32[]{:S(2)}, u32[]{:S(2)}) collective-permute-start(f32[6,8,128]{2,1,0:T(8,128)S(1)} %get-tuple-element.34.sums_ref), channel_id=1, source_target_pairs={{0,16},{16,0},{32,48},{48,32},{64,80},{80,64},{96,112},{112,96},{1... | collective-permute-start | bytes 73736 | tf_op jit(solution)/shard_map/ppermute | solution.py:350
  143.0 3.9 %collective-permute-start.11 = (f32[264,128]{1,0:T(8,128)S(1)}, f32[264,128]{1,0:T(8,128)S(1)}, u32[]{:S(2)}, u32[]{:S(2)}) collective-permute-start(f32[264,128]{1,0:T(8,128)S(1)} %sum_kernel.3.own_ref), channel_id=1, source_target_pairs={{0,96},{16,112},{32,0},{48,16},{64,32},{80,48},{96,64},{112,80},{1... | collective-permute-start | bytes 405512 | tf_op jit(solution)/shard_map/ppermute | solution.py:380
  143.1 5.5 %collective-permute-start.10 = (f32[264,128]{1,0:T(8,128)S(1)}, f32[264,128]{1,0:T(8,128)S(1)}, u32[]{:S(2)}, u32[]{:S(2)}) collective-permute-start(f32[264,128]{1,0:T(8,128)S(1)} %sum_kernel.3.own_ref), channel_id=1, source_target_pairs={{0,64},{16,80},{32,96},{48,112},{64,0},{80,16},{96,32},{112,48},{1... | collective-permute-start | bytes 405512 | tf_op jit(solution)/shard_map/ppermute | solution.py:380
  143.2 8.4 %collective-permute-start.9 = (f32[264,128]{1,0:T(8,128)S(1)}, f32[264,128]{1,0:T(8,128)S(1)}, u32[]{:S(2)}, u32[]{:S(2)}) collective-permute-start(f32[264,128]{1,0:T(8,128)S(1)} %sum_kernel.3.own_ref), channel_id=1, source_target_pairs={{0,32},{16,48},{32,64},{48,80},{64,96},{80,112},{96,0},{112,16},{1... | collective-permute-start | bytes 405512 | tf_op jit(solution)/shard_map/ppermute | solution.py:380
  151.9 3.2 %collective-permute-start.12 = (f32[2,128,256]{2,1,0:T(8,128)S(1)}, f32[2,128,256]{2,1,0:T(8,128)S(1)}, u32[]{:S(2)}, u32[]{:S(2)}) collective-permute-start(f32[2,128,256]{2,1,0:T(8,128)S(1)} %ritz_kernel.1.own_ref), channel_id=1, source_target_pairs={{0,16},{16,0},{32,48},{48,32},{64,80},{80,64},{96,112},{112,96},{1... | collective-permute-start | bytes 786440 | tf_op jit(solution)/shard_map/ppermute | solution.py:350

commit v7 on v6

--- a/solution.py
+++ b/solution.py
@@ -77,9 +77,9 @@
         codes_ref[s, B:, :] = tail
 
 
-def decode(ref, s):
-    exponent = ref[s, B:, :].astype(jnp.int32).astype(F32)[:8, :]
-    return ref[s, :B, :].astype(jnp.int32).astype(F32) * over_rows(jnp.exp2(exponent))
+def decode(piece):
+    exponent = piece[B:, :].astype(jnp.int32).astype(F32)[:8, :]
+    return piece[:B, :].astype(jnp.int32).astype(F32) * over_rows(jnp.exp2(exponent))
 
 
 def decode_start(core, own_ref, other_ref, x_ref, norm_ref):
@@ -87,11 +87,11 @@
 
     def squares(s, total):
         for ref in (own_ref, other_ref):
-            block = decode(ref, s)
+            block = decode(ref.at[s])
             total = total + fold(block * block)
         return total
 
-    mean_sq = total_of(lax.fori_loop(0, SEC, squares, zero)) / ENTRIES
+    mean_sq = total_of(lax.fori_loop(0, SEC, squares, zero, unroll=4)) / ENTRIES
     scale = 1.0 / jnp.sqrt(mean_sq + 1e-06)
     norm_ref[0] = jnp.broadcast_to(scale, (8, LANES))
     norm_ref[1] = jnp.broadcast_to(mean_sq, (8, LANES))
@@ -99,7 +99,7 @@
     def place(s, totals):
         vec_round, round_sq = totals
         for ref, at in ((own_ref, core), (other_ref, 1 - core)):
-            vec = decode(ref, s) * scale
+            vec = decode(ref.at[s]) * scale
             rounded = vec.astype(BF16)
             x_ref[s, half_rows(at), :LANES] = rounded[:HALF, :]
             x_ref[s, half_rows(at), LANES:] = rounded[HALF:, :]
@@ -107,7 +107,7 @@
             vec_round, round_sq = vec_round + fold(vec * wide), round_sq + fold(wide * wide)
         return vec_round, round_sq
 
-    vec_round, round_sq = lax.fori_loop(0, SEC, place, (zero, zero))
+    vec_round, round_sq = lax.fori_loop(0, SEC, place, (zero, zero), unroll=2)
     return ratio(total_of(vec_round), total_of(round_sq))
 
 
@@ -239,45 +239,54 @@
     keep_copy.wait()
 
 
+def scalar_rows(scalars):
+    power = exponent_of(scalars)
+    scaled = scalars * jnp.exp2(14.0 - power)
+    high = jnp.round(scaled)
+    low = jnp.round((scaled - high) * 32768.0)
+    row = lax.broadcasted_iota(jnp.int32, (8, LANES), 0)
+    return jnp.where(row == 0, high, jnp.where(row == 1, low, jnp.where(row == 2, power, 0.0)))
+
+
+def store_piece(ref, half, rows):
+    codes, exponent = encode(half)
+    ref[:B, :] = codes
+    ref[B:, :] = as_codes(jnp.concatenate([exponent, rows], axis=0))
+
+
+def load_piece(ref):
+    tail = ref[B:, :].astype(jnp.int32).astype(F32)
+    scalars = (tail[8:9, :] + tail[9:10, :] * (1.0 / 32768.0)) * jnp.exp2(tail[10:11, :] - 14.0)
+    return decode(ref), scalars
+
+
 def join_kernel(keep_ref, got_ref, sums_ref, got_sums_ref, out_ref):
     lane = lax.broadcasted_iota(jnp.int32, (8, LANES), 1)
     scalars = jnp.zeros((8, LANES), F32)
     for k in range(sums_ref.shape[0]):
         scalars = jnp.where(lane == k, total_of(sums_ref[k] + got_sums_ref[k]), scalars)
-    power = exponent_of(scalars)
-    scaled = scalars * jnp.exp2(14.0 - power)
-    high = jnp.round(scaled)
-    low = jnp.round((scaled - high) * 32768.0)
-    row = lax.broadcasted_iota(jnp.int32, (8, LANES), 0)
-    lower = jnp.where(row == 0, high, jnp.where(row == 1, low, jnp.where(row == 2, power, 0.0)))
+    rows = scalar_rows(scalars)
 
     @pl.loop(0, SEC, unroll=4)
     def _(s):
-        codes, exponent = encode(fold_columns(keep_ref[s] + got_ref[s].astype(F32)))
-        out_ref[s, :B, :] = codes
-        out_ref[s, B:, :] = as_codes(jnp.concatenate([exponent, lower], axis=0))
+        store_piece(out_ref.at[s], fold_columns(keep_ref[s] + got_ref[s].astype(F32)), rows)
 
 
 def sum_kernel(got_ref, out_ref):
     def add(s, totals):
-        tail = got_ref[s, B:, :].astype(jnp.int32).astype(F32)
-        scalars = (tail[8:9, :] + tail[9:10, :] * (1.0 / 32768.0)) * jnp.exp2(tail[10:11, :] - 14.0)
-        return totals[0] + decode(got_ref, s), totals[1] + scalars
+        half, scalars = load_piece(got_ref.at[s])
+        return totals[0] + half, totals[1] + scalars
 
     zeros = jnp.zeros((B, LANES), F32), jnp.zeros((1, LANES), F32)
-    total, scalars = lax.fori_loop(0, SEC, add, zeros, unroll=4)
-    out_ref[:B, :] = total
-    row = lax.broadcasted_iota(jnp.int32, (8, LANES), 0)
-    out_ref[B:, :] = jnp.where(row == 0, jnp.broadcast_to(scalars, (8, LANES)), 0.0)
-
-
-def sum_of_chips(part_refs, scalars):
-    own, near, across, far = (ref[...] for ref in part_refs)
-    total = (own + across) + (near + far)
-    tile = total[B:, :]
-    lane = lax.broadcasted_iota(jnp.int32, tile.shape, 1)
-    means = [total_of(jnp.where(lane == k, tile, 0.0)) / ENTRIES for k in range(scalars)]
-    return total[:B, :], means
+    half, scalars = lax.fori_loop(0, SEC, add, zeros, unroll=4)
+    store_piece(out_ref, half, scalar_rows(jnp.broadcast_to(scalars, (8, LANES))))
+
+
+def sum_of_chips(part_refs, count):
+    own, near, across, far = (load_piece(ref) for ref in part_refs)
+    half, scalars = ((own[k] + across[k]) + (near[k] + far[k]) for k in range(2))
+    lane = lax.broadcasted_iota(jnp.int32, scalars.shape, 1)
+    return half, [total_of(jnp.where(lane == k, scalars, 0.0)) / ENTRIES for k in range(count)]
 
 
 def correct_kernel(at_ref, own_ref, near_ref, across_ref, far_ref, start_ref, diag_ref, norm_ref, copies_ref, sums_ref, corr_ref, sigma_ref, theta_ref):
@@ -376,7 +385,7 @@
         join_kernel, 16, [WHOLE] * 4, PIECES,
         keep, swap(send), sums, swap(sums),
     )
-    part = call(sum_kernel, 16, [WHOLE], shape(B + 8, LANES), over_sectors(payload))
+    part = call(sum_kernel, 16, [WHOLE], shape(B + 16, LANES, dtype=jnp.int16), over_sectors(payload))
     return part, *(lax.ppermute(part, "op", perm) for perm in ALONG_X)
 
 

time: 156 us -> 151 us (0.968)
  waiting for transfers between devices: 22.7 us -> 16.5 us
  starting transfers between devices: 12.7 us -> 16 us
  blocking collectives: 99.9 us -> 97.4 us
    ppermute x6, waiting for transfers between devices: 14.9 us -> 8.72 us  [reduce_partial(): return (part, *(lax.ppermute(part, 'op', perm) for perm in ALONG_X))]
    ppermute x7, starting transfers between devices: 7.53 us -> 10.6 us  [swap(): return lax.ppermute(x, 'op', CORE_SWAP)]
    all_to_all x4, blocking collectives: 99.9 us -> 97.4 us  [over_sectors(): return lax.all_to_all(x, 'sec', 0, 0, tiled=True)]
where the time goes in v7:
time: 151 us; the launch traced here: 150 us
  blocking collectives  97.4 us (65%)
  Pallas kernels  19 us (13%)
  waiting for transfers between devices  16.5 us (11%)
  starting transfers between devices  16 us (11%)
    all_to_all x4, blocking collectives, over_sectors(): return lax.all_to_all(x, 'sec', 0, 0, tiled=True)  97.4 us
    pallas_call x11, Pallas kernels, call(): pl.pallas_call(kernel, out_shape=outs, in_specs=ins, compiler_params=pltp...  19 us
    ppermute x7, starting transfers between devices, swap(): return lax.ppermute(x, 'op', CORE_SWAP)  10.6 us
    ppermute x6, waiting for transfers between devices, reduce_partial(): return (part, *(lax.ppermute(part, 'op', perm) for perm in ALONG_X))  8.72 us
    ppermute x7, waiting for transfers between devices, swap(): return lax.ppermute(x, 'op', CORE_SWAP)  7.8 us
    ppermute x6, starting transfers between devices, reduce_partial(): return (part, *(lax.ppermute(part, 'op', perm) for perm in ALONG_X))  5.38 us
  transfers between devices with their start and end apart: 13, of which 10 were waited for; matrix products, arithmetic and copies ran while one was open for 0% of the time, Pallas kernels for 1%

profile of v7, /device:TPU:1, one launch (start us, length us, event | category | flops | bytes accessed | tf_op | source)
XLA Modules:
  0.0 150.4 jit_solution(9429445929131969489)
XLA Ops:
  0.6 1.1 encode_kernel.1
  1.8 25.3 %all_to_all.20.own_ref = s16[16,272,128]{2,1,0:T(8,128)(2,1)S(1)} all-to-all(s16[16,272,128]{2,1,0:T(8,128)(2,1)S(1)} %get-tuple-element.20), channel_id=1, replica_groups=mesh['op'=8,'sec'=16] {'sec'}, dimensions={0} | all-to-all | bytes 2228224 | tf_op jit(solution)/shard_map/all_to_all | solution.py:363
  27.1 2.0 %collective-permute-start = (s16[16,272,128]{2,1,0:T(8,128)(2,1)S(1)}, s16[16,272,128]{2,1,0:T(8,128)(2,1)S(1)}, u32[]{:S(2)}, u32[]{:S(2)}) collective-permute-start(s16[16,272,128]{2,1,0:T(8,128)(2,1)S(1)} %all_to_all.20.own_ref), channel_id=1, source_target_pairs={{0,16},{16,0},{32,48},{48,32},{64,80},{80,64},{96,112},{112,96},{1... | collective-permute-start | bytes 3342344 | tf_op jit(solution)/shard_map/ppermute | solution.py:359
  29.7 2.2 %head_kernel.1 = (bf16[16,256,256]{2,1,0:T(8,128)(2,1)S(1)}, bf16[16,256,256]{2,1,0:T(8,128)(2,1)S(1)}) custom-call(bf16[64,256,256]{2,1,0:T(8,128)(2,1)} %left_ref.3, bf16[64,256,256]{2,1,0:T(8,128)(2,1)} %right_ref.3), custom_call_target="tpu_custom_call" | custom-call | tf_op jit(solution)/shard_map/head_kernel/pallas_call | solution.py:348
  32.0 7.1 %first_kernel.1 = (f32[16,128,256]{2,1,0:T(8,128)S(1)}, bf16[16,128,256]{2,1,0:T(8,128)(2,1)S(1)}, f32[1,8,128]{2,1,0:T(8,128)S(1)}, f32[2,8,128]{2,1,0:T(8,128)...) custom-call(s32[1]{0:T(128)S(6)} %copy.9.count_ref, s32[64]{0:T(128)S(1)} %copy-done.1, ...), custom_call_target="tpu_custom_call" | custom-call | tf_op jit(solution)/shard_map/first_kernel/pallas_call | solution.py:348
  39.2 0.5 collective-permute-start.2
  39.7 2.2 %collective-permute-done.2.got_sums_ref = f32[1,8,128]{2,1,0:T(8,128)S(1)} collective-permute-done((f32[1,8,128]{2,1,0:T(8,128)S(1)}, f32[1,8,128]{2,1,0:T(8,128)S(1)}, u32[]{:S(2)}, u32[]{:S(2)}) %collective-permute-start.2) | collective-permute-done | bytes 4128 | tf_op jit(solution)/shard_map/ppermute | solution.py:359
  41.9 0.8 join_kernel.2
  42.7 27.9 %all_to_all.21.got_ref = s16[16,272,128]{2,1,0:T(8,128)(2,1)S(1)} all-to-all(s16[16,272,128]{2,1,0:T(8,128)(2,1)S(1)} %join_kernel.2), channel_id=1, replica_groups=mesh['op'=8,'sec'=16] {'sec'}, dimensions={0} | all-to-all | bytes 2228224 | tf_op jit(solution)/shard_map/all_to_all | solution.py:363
  70.5 0.4 sum_kernel.2.own_ref
  71.0 2.6 %collective-permute-start.5 = (s16[272,128]{1,0:T(8,128)(2,1)S(1)}, s16[272,128]{1,0:T(8,128)(2,1)S(1)}, u32[]{:S(2)}, u32[]{:S(2)}) collective-permute-start(s16[272,128]{1,0:T(8,128)(2,1)S(1)} %sum_kernel.2.own_ref), channel_id=1, source_target_pairs={{0,96},{16,112},{32,0},{48,16},{64,32},{80,48},{96,64},{112,80},{1... | collective-permute-start | bytes 208904 | tf_op jit(solution)/shard_map/ppermute | solution.py:389
  73.9 0.8 collective-permute-start.3
  74.9 3.4 %collective-permute-done.4.across_ref = s16[272,128]{1,0:T(8,128)(2,1)S(1)} collective-permute-done((s16[272,128]{1,0:T(8,128)(2,1)S(1)}, s16[272,128]{1,0:T(8,128)(2,1)S(1)}, u32[]{:S(2)}, u32[]{:S(2)}) %collective-permute-start.4) | collective-permute-done | bytes 69664 | tf_op jit(solution)/shard_map/ppermute | solution.py:389
  78.3 0.7 collective-permute-done.3.near_ref
  79.0 0.5 correct_kernel.1
  79.5 17.0 %all_to_all.22.own_ref = bf16[16,128,256]{2,1,0:T(8,128)(2,1)S(1)} all-to-all(bf16[16,128,256]{2,1,0:T(8,128)(2,1)S(1)} %get-tuple-element.28), channel_id=1, replica_groups=mesh['op'=8,'sec'=16] {'sec'}, dimensions={0} | all-to-all | bytes 2097152 | tf_op jit(solution)/shard_map/all_to_all | solution.py:363
  96.5 4.2 %collective-permute-start.6 = (bf16[16,128,256]{2,1,0:T(8,128)(2,1)S(1)}, bf16[16,128,256]{2,1,0:T(8,128)(2,1)S(1)}, u32[]{:S(2)}, u32[]{:S(2)}) collective-permute-start(bf16[16,128,256]{2,1,0:T(8,128)(2,1)S(1)} %all_to_all.22.own_ref), channel_id=1, source_target_pairs={{0,16},{16,0},{32,48},{48,32},{64,80},{80,64},{96,112},{112,96},{1... | collective-permute-start | bytes 3145736 | tf_op jit(solution)/shard_map/ppermute | solution.py:359
  100.8 2.3 %collective-permute-done.6.other_ref = bf16[16,128,256]{2,1,0:T(8,128)(2,1)S(1)} collective-permute-done((bf16[16,128,256]{2,1,0:T(8,128)(2,1)S(1)}, bf16[16,128,256]{2,1,0:T(8,128)(2,1)S(1)}, u32[]{:S(2)}, u32[]{:S(2)}) %collective-permute-start.6) | collective-permute-done | bytes 1048608 | tf_op jit(solution)/shard_map/ppermute | solution.py:359
  103.1 4.5 %second_kernel.1 = (f32[16,128,256]{2,1,0:T(8,128)S(1)}, bf16[16,128,256]{2,1,0:T(8,128)(2,1)S(1)}, f32[6,8,128]{2,1,0:T(8,128)S(1)}) custom-call(s32[1]{0:T(128)S(6)} %copy.9.count_ref, s32[64]{0:T(128)S(1)} %copy-done.1, s32[64]{0:T(128)S(1)} %copy-done.2, s32[1]{0:T(128)} %bitcast.at_ref, bf16[16,128,256]{2,1,0:T(8,128)(2,1)S(1)} %all_to_all.22.own_ref, ...), custom_call_target="tpu_custom_call" | custom-call | tf_op jit(solution)/shard_map/second_kernel/pallas_call | solution.py:348
  107.6 0.5 collective-permute-start.7
  108.2 2.2 %collective-permute-done.8.got_sums_ref = f32[6,8,128]{2,1,0:T(8,128)S(1)} collective-permute-done((f32[6,8,128]{2,1,0:T(8,128)S(1)}, f32[6,8,128]{2,1,0:T(8,128)S(1)}, u32[]{:S(2)}, u32[]{:S(2)}) %collective-permute-start.8) | collective-permute-done | bytes 24608 | tf_op jit(solution)/shard_map/ppermute | solution.py:359
  110.4 0.7 join_kernel.3
  111.1 27.2 %all_to_all.23.got_ref = s16[16,272,128]{2,1,0:T(8,128)(2,1)S(1)} all-to-all(s16[16,272,128]{2,1,0:T(8,128)(2,1)S(1)} %join_kernel.3), channel_id=1, replica_groups=mesh['op'=8,'sec'=16] {'sec'}, dimensions={0} | all-to-all | bytes 2228224 | tf_op jit(solution)/shard_map/all_to_all | solution.py:363
  138.3 0.4 sum_kernel.3.own_ref
  138.7 0.7 collective-permute-start.11
  139.6 0.8 collective-permute-start.9
  140.4 1.6 %collective-permute-done.11.far_ref = s16[272,128]{1,0:T(8,128)(2,1)S(1)} collective-permute-done((s16[272,128]{1,0:T(8,128)(2,1)S(1)}, s16[272,128]{1,0:T(8,128)(2,1)S(1)}, u32[]{:S(2)}, u32[]{:S(2)}) %collective-permute-start.11) | collective-permute-done | bytes 69664 | tf_op jit(solution)/shard_map/ppermute | solution.py:389
  142.0 2.2 %collective-permute-done.10.across_ref = s16[272,128]{1,0:T(8,128)(2,1)S(1)} collective-permute-done((s16[272,128]{1,0:T(8,128)(2,1)S(1)}, s16[272,128]{1,0:T(8,128)(2,1)S(1)}, u32[]{:S(2)}, u32[]{:S(2)}) %collective-permute-start.10) | collective-permute-done | bytes 69664 | tf_op jit(solution)/shard_map/ppermute | solution.py:389
  144.1 0.7 collective-permute-done.9.near_ref
  145.1 3.3 %collective-permute-start.12 = (f32[2,128,256]{2,1,0:T(8,128)S(1)}, f32[2,128,256]{2,1,0:T(8,128)S(1)}, u32[]{:S(2)}, u32[]{:S(2)}) collective-permute-start(f32[2,128,256]{2,1,0:T(8,128)S(1)} %ritz_kernel.1.own_ref), channel_id=1, source_target_pairs={{0,16},{16,0},{32,48},{48,32},{64,80},{80,64},{96,112},{112,96},{1... | collective-permute-start | bytes 786440 | tf_op jit(solution)/shard_map/ppermute | solution.py:359
  148.4 1.2 collective-permute-done.12.other_ref
  149.6 0.8 place_kernel.1
  (15 shorter events, 1.4 us)
Async XLA Ops:
  27.1 4.9 %collective-permute-start = (s16[16,272,128]{2,1,0:T(8,128)(2,1)S(1)}, s16[16,272,128]{2,1,0:T(8,128)(2,1)S(1)}, u32[]{:S(2)}, u32[]{:S(2)}) collective-permute-start(s16[16,272,128]{2,1,0:T(8,128)(2,1)S(1)} %all_to_all.20.own_ref), channel_id=1, source_target_pairs={{0,16},{16,0},{32,48},{48,32},{64,80},{80,64},{96,112},{112,96},{1... | collective-permute-start | bytes 3342344 | tf_op jit(solution)/shard_map/ppermute | solution.py:359
  29.7 2.3 %copy-start.1 = (s32[64]{0:T(128)S(1)}, s32[64]{0:T(128)}, u32[]{:S(2)}) copy-start(s32[64]{0:T(128)} %from_ref.3) | copy-start | bytes 772
  29.7 2.3 %copy-start.2 = (s32[64]{0:T(128)S(1)}, s32[64]{0:T(128)}, u32[]{:S(2)}) copy-start(s32[64]{0:T(128)} %to_ref.3) | copy-start | bytes 772
  39.1 2.7 %collective-permute-start.1 = (bf16[16,128,256]{2,1,0:T(8,128)(2,1)S(1)}, bf16[16,128,256]{2,1,0:T(8,128)(2,1)S(1)}, u32[]{:S(2)}, u32[]{:S(2)}) collective-permute-start(bf16[16,128,256]{2,1,0:T(8,128)(2,1)S(1)} %get-tuple-element.24), channel_id=1, source_target_pairs={{0,16},{16,0},{32,48},{48,32},{64,80},{80,64},{96,112},{112,96},{1... | collective-permute-start | bytes 3145736 | tf_op jit(solution)/shard_map/ppermute | solution.py:359
  39.2 2.7 %collective-permute-start.2 = (f32[1,8,128]{2,1,0:T(8,128)S(1)}, f32[1,8,128]{2,1,0:T(8,128)S(1)}, u32[]{:S(2)}, u32[]{:S(2)}) collective-permute-start(f32[1,8,128]{2,1,0:T(8,128)S(1)} %get-tuple-element.25.sums_ref), channel_id=1, source_target_pairs={{0,16},{16,0},{32,48},{48,32},{64,80},{80,64},{96,112},{112,96},{1... | collective-permute-start | bytes 12296 | tf_op jit(solution)/shard_map/ppermute | solution.py:359
  42.6 36.3 %copy-start = (f32[1,256,256]{2,1,0:T(8,128)S(1)}, f32[1,256,256]{2,1,0:T(8,128)}, u32[]{:S(2)}) copy-start(f32[1,256,256]{2,1,0:T(8,128)} %diag_ref.1) | copy-start | bytes 786436
  71.0 4.0 %collective-permute-start.5 = (s16[272,128]{1,0:T(8,128)(2,1)S(1)}, s16[272,128]{1,0:T(8,128)(2,1)S(1)}, u32[]{:S(2)}, u32[]{:S(2)}) collective-permute-start(s16[272,128]{1,0:T(8,128)(2,1)S(1)} %sum_kernel.2.own_ref), channel_id=1, source_target_pairs={{0,96},{16,112},{32,0},{48,16},{64,32},{80,48},{96,64},{112,80},{1... | collective-permute-start | bytes 208904 | tf_op jit(solution)/shard_map/ppermute | solution.py:389
  73.6 4.7 %collective-permute-start.4 = (s16[272,128]{1,0:T(8,128)(2,1)S(1)}, s16[272,128]{1,0:T(8,128)(2,1)S(1)}, u32[]{:S(2)}, u32[]{:S(2)}) collective-permute-start(s16[272,128]{1,0:T(8,128)(2,1)S(1)} %sum_kernel.2.own_ref), channel_id=1, source_target_pairs={{0,64},{16,80},{32,96},{48,112},{64,0},{80,16},{96,32},{112,48},{1... | collective-permute-start | bytes 208904 | tf_op jit(solution)/shard_map/ppermute | solution.py:389
  73.9 5.1 %collective-permute-start.3 = (s16[272,128]{1,0:T(8,128)(2,1)S(1)}, s16[272,128]{1,0:T(8,128)(2,1)S(1)}, u32[]{:S(2)}, u32[]{:S(2)}) collective-permute-start(s16[272,128]{1,0:T(8,128)(2,1)S(1)} %sum_kernel.2.own_ref), channel_id=1, source_target_pairs={{0,32},{16,48},{32,64},{48,80},{64,96},{80,112},{96,0},{112,16},{1... | collective-permute-start | bytes 208904 | tf_op jit(solution)/shard_map/ppermute | solution.py:389
  96.5 6.5 %collective-permute-start.6 = (bf16[16,128,256]{2,1,0:T(8,128)(2,1)S(1)}, bf16[16,128,256]{2,1,0:T(8,128)(2,1)S(1)}, u32[]{:S(2)}, u32[]{:S(2)}) collective-permute-start(bf16[16,128,256]{2,1,0:T(8,128)(2,1)S(1)} %all_to_all.22.own_ref), channel_id=1, source_target_pairs={{0,16},{16,0},{32,48},{48,32},{64,80},{80,64},{96,112},{112,96},{1... | collective-permute-start | bytes 3145736 | tf_op jit(solution)/shard_map/ppermute | solution.py:359
  107.6 2.8 %collective-permute-start.7 = (bf16[16,128,256]{2,1,0:T(8,128)(2,1)S(1)}, bf16[16,128,256]{2,1,0:T(8,128)(2,1)S(1)}, u32[]{:S(2)}, u32[]{:S(2)}) collective-permute-start(bf16[16,128,256]{2,1,0:T(8,128)(2,1)S(1)} %get-tuple-element.33), channel_id=1, source_target_pairs={{0,16},{16,0},{32,48},{48,32},{64,80},{80,64},{96,112},{112,96},{1... | collective-permute-start | bytes 3145736 | tf_op jit(solution)/shard_map/ppermute | solution.py:359
  108.0 2.3 %collective-permute-start.8 = (f32[6,8,128]{2,1,0:T(8,128)S(1)}, f32[6,8,128]{2,1,0:T(8,128)S(1)}, u32[]{:S(2)}, u32[]{:S(2)}) collective-permute-start(f32[6,8,128]{2,1,0:T(8,128)S(1)} %get-tuple-element.34.sums_ref), channel_id=1, source_target_pairs={{0,16},{16,0},{32,48},{48,32},{64,80},{80,64},{96,112},{112,96},{1... | collective-permute-start | bytes 73736 | tf_op jit(solution)/shard_map/ppermute | solution.py:359
  138.7 3.2 %collective-permute-start.11 = (s16[272,128]{1,0:T(8,128)(2,1)S(1)}, s16[272,128]{1,0:T(8,128)(2,1)S(1)}, u32[]{:S(2)}, u32[]{:S(2)}) collective-permute-start(s16[272,128]{1,0:T(8,128)(2,1)S(1)} %sum_kernel.3.own_ref), channel_id=1, source_target_pairs={{0,96},{16,112},{32,0},{48,16},{64,32},{80,48},{96,64},{112,80},{1... | collective-permute-start | bytes 208904 | tf_op jit(solution)/shard_map/ppermute | solution.py:389
  139.4 4.7 %collective-permute-start.10 = (s16[272,128]{1,0:T(8,128)(2,1)S(1)}, s16[272,128]{1,0:T(8,128)(2,1)S(1)}, u32[]{:S(2)}, u32[]{:S(2)}) collective-permute-start(s16[272,128]{1,0:T(8,128)(2,1)S(1)} %sum_kernel.3.own_ref), channel_id=1, source_target_pairs={{0,64},{16,80},{32,96},{48,112},{64,0},{80,16},{96,32},{112,48},{1... | collective-permute-start | bytes 208904 | tf_op jit(solution)/shard_map/ppermute | solution.py:389
  139.6 5.2 %collective-permute-start.9 = (s16[272,128]{1,0:T(8,128)(2,1)S(1)}, s16[272,128]{1,0:T(8,128)(2,1)S(1)}, u32[]{:S(2)}, u32[]{:S(2)}) collective-permute-start(s16[272,128]{1,0:T(8,128)(2,1)S(1)} %sum_kernel.3.own_ref), channel_id=1, source_target_pairs={{0,32},{16,48},{32,64},{48,80},{64,96},{80,112},{96,0},{112,16},{1... | collective-permute-start | bytes 208904 | tf_op jit(solution)/shard_map/ppermute | solution.py:389
  145.1 4.4 %collective-permute-start.12 = (f32[2,128,256]{2,1,0:T(8,128)S(1)}, f32[2,128,256]{2,1,0:T(8,128)S(1)}, u32[]{:S(2)}, u32[]{:S(2)}) collective-permute-start(f32[2,128,256]{2,1,0:T(8,128)S(1)} %ritz_kernel.1.own_ref), channel_id=1, source_target_pairs={{0,16},{16,0},{32,48},{48,32},{64,80},{80,64},{96,112},{112,96},{1... | collective-permute-start | bytes 786440 | tf_op jit(solution)/shard_map/ppermute | solution.py:359

commit v8 on v7

--- a/solution.py
+++ b/solution.py
@@ -64,51 +64,65 @@
     return as_codes(jnp.clip(codes, -32767.0, 32767.0)), exponent
 
 
+def decode(piece):
+    exponent = piece[B:, :].astype(jnp.int32).astype(F32)[:8, :]
+    return piece[:B, :].astype(jnp.int32).astype(F32) * over_rows(jnp.exp2(exponent))
+
+
+def scalar_rows(scalars):
+    power = exponent_of(scalars)
+    scaled = scalars * jnp.exp2(14.0 - power)
+    high = jnp.round(scaled)
+    low = jnp.round((scaled - high) * 32768.0)
+    row = lax.broadcasted_iota(jnp.int32, (8, LANES), 0)
+    return jnp.where(row == 0, high, jnp.where(row == 1, low, jnp.where(row == 2, power, 0.0)))
+
+
+def store_piece(ref, half, rows):
+    codes, exponent = encode(half)
+    ref[:B, :] = codes
+    ref[B:, :] = as_codes(jnp.concatenate([exponent, rows], axis=0))
+
+
+def load_scalars(ref):
+    tail = ref[B:, :].astype(jnp.int32).astype(F32)
+    return (tail[8:9, :] + tail[9:10, :] * (1.0 / 32768.0)) * jnp.exp2(tail[10:11, :] - 14.0)
+
+
+def load_piece(ref):
+    return decode(ref), load_scalars(ref)
+
+
 def encode_kernel(at_ref, start_ref, codes_ref, half_ref, start, sem):
     copy = pltpu.make_async_copy(start_ref, start, sem)
     copy.start()
     copy.wait()
     half = fold_columns(start[0, half_rows(at_ref[0]), :])
     half_ref[...] = half
-    codes, exponent = encode(half)
-    tail = as_codes(jnp.concatenate([exponent, jnp.zeros((8, LANES), F32)], axis=0))
+    rows = scalar_rows(jnp.broadcast_to(total_of(half * half), (8, LANES)))
     for s in range(SEC):
-        codes_ref[s, :B, :] = codes
-        codes_ref[s, B:, :] = tail
-
-
-def decode(piece):
-    exponent = piece[B:, :].astype(jnp.int32).astype(F32)[:8, :]
-    return piece[:B, :].astype(jnp.int32).astype(F32) * over_rows(jnp.exp2(exponent))
-
-
-def decode_start(core, own_ref, other_ref, x_ref, norm_ref):
-    zero = jnp.zeros((8, LANES), F32)
-
-    def squares(s, total):
-        for ref in (own_ref, other_ref):
-            block = decode(ref.at[s])
-            total = total + fold(block * block)
-        return total
-
-    mean_sq = total_of(lax.fori_loop(0, SEC, squares, zero, unroll=4)) / ENTRIES
+        store_piece(codes_ref.at[s], half, rows)
+
+
+def decode_start(core, own_ref, other_ref, start_ref, x_ref, norm_ref, sums_ref):
+    squares = load_scalars(own_ref.at[0]) + load_scalars(other_ref.at[0])
+    for s in range(1, SEC):
+        squares = squares + (load_scalars(own_ref.at[s]) + load_scalars(other_ref.at[s]))
+    mean_sq = squares[:, :1] / ENTRIES
     scale = 1.0 / jnp.sqrt(mean_sq + 1e-06)
     norm_ref[0] = jnp.broadcast_to(scale, (8, LANES))
     norm_ref[1] = jnp.broadcast_to(mean_sq, (8, LANES))
-
-    def place(s, totals):
-        vec_round, round_sq = totals
+    vec = start_ref[...] * scale
+    wide = vec.astype(BF16).astype(F32)
+    sums_ref[1] = fold(vec * wide) / CHIPS_X
+    sums_ref[2] = fold(wide * wide) / CHIPS_X
+
+    @pl.loop(0, SEC, unroll=2)
+    def _(s):
         for ref, at in ((own_ref, core), (other_ref, 1 - core)):
-            vec = decode(ref.at[s]) * scale
-            rounded = vec.astype(BF16)
+            rounded = (decode(ref.at[s]) * scale).astype(BF16)
             x_ref[s, half_rows(at), :LANES] = rounded[:HALF, :]
             x_ref[s, half_rows(at), LANES:] = rounded[HALF:, :]
-            wide = rounded.astype(F32)
-            vec_round, round_sq = vec_round + fold(vec * wide), round_sq + fold(wide * wide)
-        return vec_round, round_sq
-
-    vec_round, round_sq = lax.fori_loop(0, SEC, place, (zero, zero), unroll=2)
-    return ratio(total_of(vec_round), total_of(round_sq))
 
 
 def head_kernel(left_ref, right_ref, left_out, right_out, sems):
@@ -122,10 +136,10 @@
         copy.wait()
 
 
-def first_kernel(count_ref, from_ref, to_ref, at_ref, own_ref, other_ref, left_head, right_head, left_ref, right_ref,
+def first_kernel(count_ref, from_ref, to_ref, at_ref, own_ref, other_ref, start_ref, left_head, right_head, left_ref, right_ref,
                  keep_ref, send_ref, sums_ref, norm_ref, left, right, x_ref, acc_ref, halves_ref, sems, term_sems):
     def prepare(core):
-        return decode_start(core, own_ref, other_ref, x_ref, norm_ref)
+        decode_start(core, own_ref, other_ref, start_ref, x_ref, norm_ref, sums_ref)
 
     apply_terms(
         prepare, (count_ref, from_ref, to_ref, at_ref), (left_head, right_head), (left_ref, right_ref), (left, right),
@@ -145,7 +159,6 @@
         sums_ref[1:] = more_ref[...]
         for copy in copies:
             copy.wait()
-        return 1.0
 
     apply_terms(
         prepare, (count_ref, from_ref, to_ref, at_ref), (left_head, right_head), None, (left, right),
@@ -180,7 +193,7 @@
     def _(s):
         acc_ref[s] = jnp.zeros((B, B), F32)
 
-    weight = prepare(core)
+    prepare(core)
 
     def step(i, lefts, rights, base):
         live = count_ref[0] - i * STEP
@@ -235,29 +248,8 @@
         total = total + fold(x_ref[s, theirs, :].astype(F32) * part)
         return total + fold(x_ref[s, mine, :].astype(F32) * acc_ref[s, mine, :])
 
-    sums_ref[0] = lax.fori_loop(0, SEC, inner, jnp.zeros((8, LANES), F32)) * weight
+    sums_ref[0] = lax.fori_loop(0, SEC, inner, jnp.zeros((8, LANES), F32))
     keep_copy.wait()
-
-
-def scalar_rows(scalars):
-    power = exponent_of(scalars)
-    scaled = scalars * jnp.exp2(14.0 - power)
-    high = jnp.round(scaled)
-    low = jnp.round((scaled - high) * 32768.0)
-    row = lax.broadcasted_iota(jnp.int32, (8, LANES), 0)
-    return jnp.where(row == 0, high, jnp.where(row == 1, low, jnp.where(row == 2, power, 0.0)))
-
-
-def store_piece(ref, half, rows):
-    codes, exponent = encode(half)
-    ref[:B, :] = codes
-    ref[B:, :] = as_codes(jnp.concatenate([exponent, rows], axis=0))
-
-
-def load_piece(ref):
-    tail = ref[B:, :].astype(jnp.int32).astype(F32)
-    scalars = (tail[8:9, :] + tail[9:10, :] * (1.0 / 32768.0)) * jnp.exp2(tail[10:11, :] - 14.0)
-    return decode(ref), scalars
 
 
 def join_kernel(keep_ref, got_ref, sums_ref, got_sums_ref, out_ref):
@@ -290,7 +282,8 @@
 
 
 def correct_kernel(at_ref, own_ref, near_ref, across_ref, far_ref, start_ref, diag_ref, norm_ref, copies_ref, sums_ref, corr_ref, sigma_ref, theta_ref):
-    sigma, (theta,) = sum_of_chips((own_ref, near_ref, across_ref, far_ref), 1)
+    sigma, (theta, vec_round, round_sq) = sum_of_chips((own_ref, near_ref, across_ref, far_ref), 3)
+    theta = theta * ratio(vec_round, round_sq)
     vec = start_ref[...] * norm_ref[0, :1, :1]
     diag = fold_columns(diag_ref[0, half_rows(at_ref[0]), :])
     corr = (sigma - theta * vec) / jnp.maximum(jnp.abs(diag - theta), 1.0)
@@ -404,9 +397,9 @@
     )
     own = over_sectors(codes)
     keep, send, sums, norm, *held = call(
-        first_kernel, 28, [SMEM] * 4 + [WHOLE] * 4 + [ANY] * 2,
-        SPLIT + [shape(1, 8, LANES), shape(2, 8, LANES)] + terms_shape(TERMS - STEP),
-        *terms, own, swap(own), *head, *far,
+        first_kernel, 28, [SMEM] * 4 + [WHOLE] * 5 + [ANY] * 2,
+        SPLIT + [shape(3, 8, LANES), shape(2, 8, LANES)] + terms_shape(TERMS - STEP),
+        *terms, own, swap(own), start, *head, *far,
         out_specs=[ANY] + [WHOLE] * 5,
         scratch_shapes=APPLY_SCRATCH + [pltpu.SemaphoreType.DMA((2, GROUPS))],
     )

time: 151 us -> 148 us (0.980)
  blocking collectives: 97.4 us -> 83.2 us
  starting transfers between devices: 16 us -> 24.8 us
  Pallas kernels: 19 us -> 21.9 us
    all_to_all x4, blocking collectives: 97.4 us -> 83.2 us  [over_sectors(): return lax.all_to_all(x, 'sec', 0, 0, tiled=True)]
    ppermute x7, starting transfers between devices: 10.6 us -> 20 us  [swap(): return lax.ppermute(x, 'op', CORE_SWAP)]
    pallas_call x11, Pallas kernels: 19 us -> 21.9 us  [call(): pl.pallas_call(kernel, out_shape=outs, in_specs=ins, compiler_params=pltp...]
  transfers between devices with their start and end apart: 13 -> 13, of which waited for: 10 -> 10; matrix products, arithmetic and copies ran while one was open for 0% -> 0% of each run, Pallas kernels for 1% -> 2%
where the time goes in v8:
time: 148 us
  blocking collectives  83.2 us (56%)
  starting transfers between devices  24.8 us (17%)
  Pallas kernels  21.9 us (15%)
  waiting for transfers between devices  16.6 us (11%)
    all_to_all x4, blocking collectives, over_sectors(): return lax.all_to_all(x, 'sec', 0, 0, tiled=True)  83.2 us
    pallas_call x11, Pallas kernels, call(): pl.pallas_call(kernel, out_shape=outs, in_specs=ins, compiler_params=pltp...  21.9 us
    ppermute x7, starting transfers between devices, swap(): return lax.ppermute(x, 'op', CORE_SWAP)  20 us
    ppermute x6, waiting for transfers between devices, reduce_partial(): return (part, *(lax.ppermute(part, 'op', perm) for perm in ALONG_X))  8.72 us
    ppermute x7, waiting for transfers between devices, swap(): return lax.ppermute(x, 'op', CORE_SWAP)  7.9 us
    ppermute x6, starting transfers between devices, reduce_partial(): return (part, *(lax.ppermute(part, 'op', perm) for perm in ALONG_X))  4.85 us
  transfers between devices with their start and end apart: 13, of which 10 were waited for; matrix products, arithmetic and copies ran while one was open for 0% of the time, Pallas kernels for 2%

profile of v8, /device:TPU:1, one launch (start us, length us, event | category | flops | bytes accessed | tf_op | source)
XLA Modules:
  0.0 147.9 jit_solution(16654835909442753604)
XLA Ops:
  0.6 1.2 encode_kernel.1
  1.8 25.3 %all_to_all.20.own_ref = s16[16,272,128]{2,1,0:T(8,128)(2,1)S(1)} all-to-all(s16[16,272,128]{2,1,0:T(8,128)(2,1)S(1)} %get-tuple-element.20), channel_id=1, replica_groups=mesh['op'=8,'sec'=16] {'sec'}, dimensions={0} | all-to-all | bytes 2228224 | tf_op jit(solution)/shard_map/all_to_all | solution.py:356
  27.1 2.0 %collective-permute-start = (s16[16,272,128]{2,1,0:T(8,128)(2,1)S(1)}, s16[16,272,128]{2,1,0:T(8,128)(2,1)S(1)}, u32[]{:S(2)}, u32[]{:S(2)}) collective-permute-start(s16[16,272,128]{2,1,0:T(8,128)(2,1)S(1)} %all_to_all.20.own_ref), channel_id=1, source_target_pairs={{0,16},{16,0},{32,48},{48,32},{64,80},{80,64},{96,112},{112,96},{1... | collective-permute-start | bytes 3342344 | tf_op jit(solution)/shard_map/ppermute | solution.py:352
  29.8 2.2 %head_kernel.1 = (bf16[16,256,256]{2,1,0:T(8,128)(2,1)S(1)}, bf16[16,256,256]{2,1,0:T(8,128)(2,1)S(1)}) custom-call(bf16[64,256,256]{2,1,0:T(8,128)(2,1)} %left_ref.3, bf16[64,256,256]{2,1,0:T(8,128)(2,1)} %right_ref.3), custom_call_target="tpu_custom_call" | custom-call | tf_op jit(solution)/shard_map/head_kernel/pallas_call | solution.py:341
  32.0 7.6 %first_kernel.1 = (f32[16,128,256]{2,1,0:T(8,128)S(1)}, bf16[16,128,256]{2,1,0:T(8,128)(2,1)S(1)}, f32[3,8,128]{2,1,0:T(8,128)S(1)}, f32[2,8,128]{2,1,0:T(8,128)...) custom-call(s32[1]{0:T(128)S(6)} %copy.9.count_ref, s32[64]{0:T(128)S(1)} %copy-done.1, ...), custom_call_target="tpu_custom_call" | custom-call | tf_op jit(solution)/shard_map/first_kernel/pallas_call | solution.py:341
  39.6 5.0 %collective-permute-start.1 = (bf16[16,128,256]{2,1,0:T(8,128)(2,1)S(1)}, bf16[16,128,256]{2,1,0:T(8,128)(2,1)S(1)}, u32[]{:S(2)}, u32[]{:S(2)}) collective-permute-start(bf16[16,128,256]{2,1,0:T(8,128)(2,1)S(1)} %get-tuple-element.25), channel_id=1, source_target_pairs={{0,16},{16,0},{32,48},{48,32},{64,80},{80,64},{96,112},{112,96},{1... | collective-permute-start | bytes 3145736 | tf_op jit(solution)/shard_map/ppermute | solution.py:352
  44.7 2.2 %collective-permute-done.2.got_sums_ref = f32[3,8,128]{2,1,0:T(8,128)S(1)} collective-permute-done((f32[3,8,128]{2,1,0:T(8,128)S(1)}, f32[3,8,128]{2,1,0:T(8,128)S(1)}, u32[]{:S(2)}, u32[]{:S(2)}) %collective-permute-start.2) | collective-permute-done | bytes 12320 | tf_op jit(solution)/shard_map/ppermute | solution.py:352
  47.0 0.8 join_kernel.2
  47.7 20.6 %all_to_all.21.got_ref = s16[16,272,128]{2,1,0:T(8,128)(2,1)S(1)} all-to-all(s16[16,272,128]{2,1,0:T(8,128)(2,1)S(1)} %join_kernel.2), channel_id=1, replica_groups=mesh['op'=8,'sec'=16] {'sec'}, dimensions={0} | all-to-all | bytes 2228224 | tf_op jit(solution)/shard_map/all_to_all | solution.py:356
  68.3 0.4 sum_kernel.2.own_ref
  68.8 2.5 %collective-permute-start.5 = (s16[272,128]{1,0:T(8,128)(2,1)S(1)}, s16[272,128]{1,0:T(8,128)(2,1)S(1)}, u32[]{:S(2)}, u32[]{:S(2)}) collective-permute-start(s16[272,128]{1,0:T(8,128)(2,1)S(1)} %sum_kernel.2.own_ref), channel_id=1, source_target_pairs={{0,96},{16,112},{32,0},{48,16},{64,32},{80,48},{96,64},{112,80},{1... | collective-permute-start | bytes 208904 | tf_op jit(solution)/shard_map/ppermute | solution.py:382
  71.3 0.4 collective-permute-start.4
  72.1 0.6 collective-permute-done.5.far_ref
  72.7 3.4 %collective-permute-done.4.across_ref = s16[272,128]{1,0:T(8,128)(2,1)S(1)} collective-permute-done((s16[272,128]{1,0:T(8,128)(2,1)S(1)}, s16[272,128]{1,0:T(8,128)(2,1)S(1)}, u32[]{:S(2)}, u32[]{:S(2)}) %collective-permute-start.4) | collective-permute-done | bytes 69664 | tf_op jit(solution)/shard_map/ppermute | solution.py:382
  76.0 0.7 collective-permute-done.3.near_ref
  76.7 0.5 correct_kernel.1
  77.2 17.0 %all_to_all.22.own_ref = bf16[16,128,256]{2,1,0:T(8,128)(2,1)S(1)} all-to-all(bf16[16,128,256]{2,1,0:T(8,128)(2,1)S(1)} %get-tuple-element.28), channel_id=1, replica_groups=mesh['op'=8,'sec'=16] {'sec'}, dimensions={0} | all-to-all | bytes 2097152 | tf_op jit(solution)/shard_map/all_to_all | solution.py:356
  94.2 4.2 %collective-permute-start.6 = (bf16[16,128,256]{2,1,0:T(8,128)(2,1)S(1)}, bf16[16,128,256]{2,1,0:T(8,128)(2,1)S(1)}, u32[]{:S(2)}, u32[]{:S(2)}) collective-permute-start(bf16[16,128,256]{2,1,0:T(8,128)(2,1)S(1)} %all_to_all.22.own_ref), channel_id=1, source_target_pairs={{0,16},{16,0},{32,48},{48,32},{64,80},{80,64},{96,112},{112,96},{1... | collective-permute-start | bytes 3145736 | tf_op jit(solution)/shard_map/ppermute | solution.py:352
  98.5 2.3 %collective-permute-done.6.other_ref = bf16[16,128,256]{2,1,0:T(8,128)(2,1)S(1)} collective-permute-done((bf16[16,128,256]{2,1,0:T(8,128)(2,1)S(1)}, bf16[16,128,256]{2,1,0:T(8,128)(2,1)S(1)}, u32[]{:S(2)}, u32[]{:S(2)}) %collective-permute-start.6) | collective-permute-done | bytes 1048608 | tf_op jit(solution)/shard_map/ppermute | solution.py:352
  100.8 6.9 %second_kernel.1 = (f32[16,128,256]{2,1,0:T(8,128)S(1)}, bf16[16,128,256]{2,1,0:T(8,128)(2,1)S(1)}, f32[6,8,128]{2,1,0:T(8,128)S(1)}) custom-call(s32[1]{0:T(128)S(6)} %copy.9.count_ref, s32[64]{0:T(128)S(1)} %copy-done.1, s32[64]{0:T(128)S(1)} %copy-done.2, s32[1]{0:T(128)} %bitcast.at_ref, bf16[16,128,256]{2,1,0:T(8,128)(2,1)S(1)} %all_to_all.22.own_ref, ...), custom_call_target="tpu_custom_call" | custom-call | tf_op jit(solution)/shard_map/second_kernel/pallas_call | solution.py:341
  107.6 5.3 %collective-permute-start.7 = (bf16[16,128,256]{2,1,0:T(8,128)(2,1)S(1)}, bf16[16,128,256]{2,1,0:T(8,128)(2,1)S(1)}, u32[]{:S(2)}, u32[]{:S(2)}) collective-permute-start(bf16[16,128,256]{2,1,0:T(8,128)(2,1)S(1)} %get-tuple-element.33), channel_id=1, source_target_pairs={{0,16},{16,0},{32,48},{48,32},{64,80},{80,64},{96,112},{112,96},{1... | collective-permute-start | bytes 3145736 | tf_op jit(solution)/shard_map/ppermute | solution.py:352
  113.1 2.2 %collective-permute-done.8.got_sums_ref = f32[6,8,128]{2,1,0:T(8,128)S(1)} collective-permute-done((f32[6,8,128]{2,1,0:T(8,128)S(1)}, f32[6,8,128]{2,1,0:T(8,128)S(1)}, u32[]{:S(2)}, u32[]{:S(2)}) %collective-permute-start.8) | collective-permute-done | bytes 24608 | tf_op jit(solution)/shard_map/ppermute | solution.py:352
  115.3 0.7 join_kernel.3
  116.0 20.2 %all_to_all.23.got_ref = s16[16,272,128]{2,1,0:T(8,128)(2,1)S(1)} all-to-all(s16[16,272,128]{2,1,0:T(8,128)(2,1)S(1)} %join_kernel.3), channel_id=1, replica_groups=mesh['op'=8,'sec'=16] {'sec'}, dimensions={0} | all-to-all | bytes 2228224 | tf_op jit(solution)/shard_map/all_to_all | solution.py:356
  136.3 0.4 sum_kernel.3.own_ref
  137.0 1.3 collective-permute-start.9
  138.2 1.7 %collective-permute-done.11.far_ref = s16[272,128]{1,0:T(8,128)(2,1)S(1)} collective-permute-done((s16[272,128]{1,0:T(8,128)(2,1)S(1)}, s16[272,128]{1,0:T(8,128)(2,1)S(1)}, u32[]{:S(2)}, u32[]{:S(2)}) %collective-permute-start.11) | collective-permute-done | bytes 69664 | tf_op jit(solution)/shard_map/ppermute | solution.py:382
  139.9 1.6 %collective-permute-done.10.across_ref = s16[272,128]{1,0:T(8,128)(2,1)S(1)} collective-permute-done((s16[272,128]{1,0:T(8,128)(2,1)S(1)}, s16[272,128]{1,0:T(8,128)(2,1)S(1)}, u32[]{:S(2)}, u32[]{:S(2)}) %collective-permute-start.10) | collective-permute-done | bytes 69664 | tf_op jit(solution)/shard_map/ppermute | solution.py:382
  141.5 0.8 collective-permute-done.9.near_ref
  142.7 3.2 %collective-permute-start.12 = (f32[2,128,256]{2,1,0:T(8,128)S(1)}, f32[2,128,256]{2,1,0:T(8,128)S(1)}, u32[]{:S(2)}, u32[]{:S(2)}) collective-permute-start(f32[2,128,256]{2,1,0:T(8,128)S(1)} %ritz_kernel.1.own_ref), channel_id=1, source_target_pairs={{0,16},{16,0},{32,48},{48,32},{64,80},{80,64},{96,112},{112,96},{1... | collective-permute-start | bytes 786440 | tf_op jit(solution)/shard_map/ppermute | solution.py:352
  145.9 1.2 collective-permute-done.12.other_ref
  147.1 0.8 place_kernel.1
  (15 shorter events, 1.2 us)
Async XLA Ops:
  27.1 4.9 %collective-permute-start = (s16[16,272,128]{2,1,0:T(8,128)(2,1)S(1)}, s16[16,272,128]{2,1,0:T(8,128)(2,1)S(1)}, u32[]{:S(2)}, u32[]{:S(2)}) collective-permute-start(s16[16,272,128]{2,1,0:T(8,128)(2,1)S(1)} %all_to_all.20.own_ref), channel_id=1, source_target_pairs={{0,16},{16,0},{32,48},{48,32},{64,80},{80,64},{96,112},{112,96},{1... | collective-permute-start | bytes 3342344 | tf_op jit(solution)/shard_map/ppermute | solution.py:352
  29.7 2.3 %copy-start.1 = (s32[64]{0:T(128)S(1)}, s32[64]{0:T(128)}, u32[]{:S(2)}) copy-start(s32[64]{0:T(128)} %from_ref.3) | copy-start | bytes 772
  29.7 2.3 %copy-start.2 = (s32[64]{0:T(128)S(1)}, s32[64]{0:T(128)}, u32[]{:S(2)}) copy-start(s32[64]{0:T(128)} %to_ref.3) | copy-start | bytes 772
  39.6 7.3 %collective-permute-start.1 = (bf16[16,128,256]{2,1,0:T(8,128)(2,1)S(1)}, bf16[16,128,256]{2,1,0:T(8,128)(2,1)S(1)}, u32[]{:S(2)}, u32[]{:S(2)}) collective-permute-start(bf16[16,128,256]{2,1,0:T(8,128)(2,1)S(1)} %get-tuple-element.25), channel_id=1, source_target_pairs={{0,16},{16,0},{32,48},{48,32},{64,80},{80,64},{96,112},{112,96},{1... | collective-permute-start | bytes 3145736 | tf_op jit(solution)/shard_map/ppermute | solution.py:352
  44.7 2.3 %collective-permute-start.2 = (f32[3,8,128]{2,1,0:T(8,128)S(1)}, f32[3,8,128]{2,1,0:T(8,128)S(1)}, u32[]{:S(2)}, u32[]{:S(2)}) collective-permute-start(f32[3,8,128]{2,1,0:T(8,128)S(1)} %get-tuple-element.26.sums_ref), channel_id=1, source_target_pairs={{0,16},{16,0},{32,48},{48,32},{64,80},{80,64},{96,112},{112,96},{1... | collective-permute-start | bytes 36872 | tf_op jit(solution)/shard_map/ppermute | solution.py:352
  47.7 29.0 %copy-start = (f32[1,256,256]{2,1,0:T(8,128)S(1)}, f32[1,256,256]{2,1,0:T(8,128)}, u32[]{:S(2)}) copy-start(f32[1,256,256]{2,1,0:T(8,128)} %diag_ref.1) | copy-start | bytes 786436
  68.8 3.9 %collective-permute-start.5 = (s16[272,128]{1,0:T(8,128)(2,1)S(1)}, s16[272,128]{1,0:T(8,128)(2,1)S(1)}, u32[]{:S(2)}, u32[]{:S(2)}) collective-permute-start(s16[272,128]{1,0:T(8,128)(2,1)S(1)} %sum_kernel.2.own_ref), channel_id=1, source_target_pairs={{0,96},{16,112},{32,0},{48,16},{64,32},{80,48},{96,64},{112,80},{1... | collective-permute-start | bytes 208904 | tf_op jit(solution)/shard_map/ppermute | solution.py:382
  71.3 4.7 %collective-permute-start.4 = (s16[272,128]{1,0:T(8,128)(2,1)S(1)}, s16[272,128]{1,0:T(8,128)(2,1)S(1)}, u32[]{:S(2)}, u32[]{:S(2)}) collective-permute-start(s16[272,128]{1,0:T(8,128)(2,1)S(1)} %sum_kernel.2.own_ref), channel_id=1, source_target_pairs={{0,64},{16,80},{32,96},{48,112},{64,0},{80,16},{96,32},{112,48},{1... | collective-permute-start | bytes 208904 | tf_op jit(solution)/shard_map/ppermute | solution.py:382
  71.7 5.0 %collective-permute-start.3 = (s16[272,128]{1,0:T(8,128)(2,1)S(1)}, s16[272,128]{1,0:T(8,128)(2,1)S(1)}, u32[]{:S(2)}, u32[]{:S(2)}) collective-permute-start(s16[272,128]{1,0:T(8,128)(2,1)S(1)} %sum_kernel.2.own_ref), channel_id=1, source_target_pairs={{0,32},{16,48},{32,64},{48,80},{64,96},{80,112},{96,0},{112,16},{1... | collective-permute-start | bytes 208904 | tf_op jit(solution)/shard_map/ppermute | solution.py:382
  94.2 6.5 %collective-permute-start.6 = (bf16[16,128,256]{2,1,0:T(8,128)(2,1)S(1)}, bf16[16,128,256]{2,1,0:T(8,128)(2,1)S(1)}, u32[]{:S(2)}, u32[]{:S(2)}) collective-permute-start(bf16[16,128,256]{2,1,0:T(8,128)(2,1)S(1)} %all_to_all.22.own_ref), channel_id=1, source_target_pairs={{0,16},{16,0},{32,48},{48,32},{64,80},{80,64},{96,112},{112,96},{1... | collective-permute-start | bytes 3145736 | tf_op jit(solution)/shard_map/ppermute | solution.py:352
  107.6 7.7 %collective-permute-start.7 = (bf16[16,128,256]{2,1,0:T(8,128)(2,1)S(1)}, bf16[16,128,256]{2,1,0:T(8,128)(2,1)S(1)}, u32[]{:S(2)}, u32[]{:S(2)}) collective-permute-start(bf16[16,128,256]{2,1,0:T(8,128)(2,1)S(1)} %get-tuple-element.33), channel_id=1, source_target_pairs={{0,16},{16,0},{32,48},{48,32},{64,80},{80,64},{96,112},{112,96},{1... | collective-permute-start | bytes 3145736 | tf_op jit(solution)/shard_map/ppermute | solution.py:352
  113.0 2.3 %collective-permute-start.8 = (f32[6,8,128]{2,1,0:T(8,128)S(1)}, f32[6,8,128]{2,1,0:T(8,128)S(1)}, u32[]{:S(2)}, u32[]{:S(2)}) collective-permute-start(f32[6,8,128]{2,1,0:T(8,128)S(1)} %get-tuple-element.34.sums_ref), channel_id=1, source_target_pairs={{0,16},{16,0},{32,48},{48,32},{64,80},{80,64},{96,112},{112,96},{1... | collective-permute-start | bytes 73736 | tf_op jit(solution)/shard_map/ppermute | solution.py:352
  136.7 3.2 %collective-permute-start.11 = (s16[272,128]{1,0:T(8,128)(2,1)S(1)}, s16[272,128]{1,0:T(8,128)(2,1)S(1)}, u32[]{:S(2)}, u32[]{:S(2)}) collective-permute-start(s16[272,128]{1,0:T(8,128)(2,1)S(1)} %sum_kernel.3.own_ref), channel_id=1, source_target_pairs={{0,96},{16,112},{32,0},{48,16},{64,32},{80,48},{96,64},{112,80},{1... | collective-permute-start | bytes 208904 | tf_op jit(solution)/shard_map/ppermute | solution.py:382
  136.8 4.7 %collective-permute-start.10 = (s16[272,128]{1,0:T(8,128)(2,1)S(1)}, s16[272,128]{1,0:T(8,128)(2,1)S(1)}, u32[]{:S(2)}, u32[]{:S(2)}) collective-permute-start(s16[272,128]{1,0:T(8,128)(2,1)S(1)} %sum_kernel.3.own_ref), channel_id=1, source_target_pairs={{0,64},{16,80},{32,96},{48,112},{64,0},{80,16},{96,32},{112,48},{1... | collective-permute-start | bytes 208904 | tf_op jit(solution)/shard_map/ppermute | solution.py:382
  137.0 5.4 %collective-permute-start.9 = (s16[272,128]{1,0:T(8,128)(2,1)S(1)}, s16[272,128]{1,0:T(8,128)(2,1)S(1)}, u32[]{:S(2)}, u32[]{:S(2)}) collective-permute-start(s16[272,128]{1,0:T(8,128)(2,1)S(1)} %sum_kernel.3.own_ref), channel_id=1, source_target_pairs={{0,32},{16,48},{32,64},{48,80},{64,96},{80,112},{96,0},{112,16},{1... | collective-permute-start | bytes 208904 | tf_op jit(solution)/shard_map/ppermute | solution.py:382
  142.7 4.4 %collective-permute-start.12 = (f32[2,128,256]{2,1,0:T(8,128)S(1)}, f32[2,128,256]{2,1,0:T(8,128)S(1)}, u32[]{:S(2)}, u32[]{:S(2)}) collective-permute-start(f32[2,128,256]{2,1,0:T(8,128)S(1)} %ritz_kernel.1.own_ref), channel_id=1, source_target_pairs={{0,16},{16,0},{32,48},{48,32},{64,80},{80,64},{96,112},{112,96},{1... | collective-permute-start | bytes 786440 | tf_op jit(solution)/shard_map/ppermute | solution.py:352
